TPU v7x, 32 devices: a whole 2x2x4 slice. The times are simulated.
32 devices in a mesh: section: 2 (over x), dp: 4 (over z), tensor: 4 (over y, core).
Axes of the slice: x: 2, y: 2, z: 4, core: 2. Of those that a mesh axis runs over, the one named last changes fastest.
Arguments:
- tokens: bfloat16 [2, 4, 1024, 1024], P(None, 'dp'), may hold values from -6 to 6
- cotangent: bfloat16 [2, 4, 1024, 1024], P(None, 'dp'), may hold values from -6 to 6
- lengths: int32 [2, 4], P(None, 'dp'), may hold values from 128 to 1024, as said below
- attn_gain: float32 [2, 1024], P('section'), may hold values from 0.25 to 1.75
- attn_bias: float32 [2, 1024], P('section'), may hold values from -1.75 to 1.75
- ffn_gain: float32 [2, 1024], P('section'), may hold values from 0.25 to 1.75
- ffn_bias: float32 [2, 1024], P('section'), may hold values from -1.75 to 1.75
- w_query: bfloat16 [2, 1024, 1024], P('section', None, 'tensor'), may hold values from -0.1875 to 0.1875
- w_key: bfloat16 [2, 1024, 1024], P('section', None, 'tensor'), may hold values from -0.1875 to 0.1875
- w_value: bfloat16 [2, 1024, 1024], P('section', None, 'tensor'), may hold values from -0.1875 to 0.1875
- w_out: bfloat16 [2, 1024, 1024], P('section', 'tensor'), may hold values from -1.5 to 1.5
- feat_scale: float32 [2, 16, 64], P('section', 'tensor'), may hold values from 0.25 to 4
- w_up: bfloat16 [2, 1024, 4096], P('section', None, 'tensor'), may hold values from -0.1875 to 0.1875
- w_down: bfloat16 [2, 4096, 1024], P('section', 'tensor'), may hold values from -0.09375 to 0.09375
- down_bias: float32 [2, 1024], P('section'), may hold values from -1.75 to 1.75
Outputs:
- ends: float32 [2, 2, 4, 1024, 1024], P('section', None, 'dp', 'tensor')
- grad_attn_gain: float32 [2, 1024], P('section', 'dp')
- grad_attn_bias: float32 [2, 1024], P('section', 'dp')
- grad_ffn_gain: float32 [2, 1024], P('section', 'dp')
- grad_ffn_bias: float32 [2, 1024], P('section', 'dp')
- grad_w_query: float32 [2, 1024, 1024], P('section', 'dp', 'tensor')
- grad_w_key: float32 [2, 1024, 1024], P('section', 'dp', 'tensor')
- grad_w_value: float32 [2, 1024, 1024], P('section', 'dp', 'tensor')
- grad_w_out: float32 [2, 1024, 1024], P('section', 'tensor', 'dp')
- grad_feat_scale: float32 [2, 16, 64], P('section', 'tensor', 'dp')
- grad_w_up: float32 [2, 1024, 4096], P('section', 'dp', 'tensor')
- grad_w_down: float32 [2, 4096, 1024], P('section', 'tensor', 'dp')
- grad_down_bias: float32 [2, 1024], P('section', 'dp')
Inputs may be any that keep to these rules, and one draw needn't show every extreme that they name: `lengths`: in every draw some sequence fills all 1024 slots.
All inputs are finite; a program needn't handle non-finite values.
Results may differ from a plain program's by a relative error of at most 0.015.
Values may be sent and summed in bfloat16 or wider, within the bound.
No kernel may reach another device: no remote copies, remote signals or barrier semaphores. Data moves between devices by JAX's collectives and lax.ppermute only.
A program may use at most 320 MiB of HBM per device.

v0:
```python
import math

import jax
import jax.numpy as jnp
from jax import lax
from jax.sharding import PartitionSpec as P

ROT = 16
SPAN = 64


EPSILON = 1e-05
HIGHEST = lax.Precision.HIGHEST


def from_behind(x, axis, by):
    size = lax.axis_size(axis)
    pairs = [(i, i + by) for i in range(size) if 0 <= i + by < size]
    return lax.ppermute(x, axis, pairs)


def layer_norm(hidden, gain, shift):
    center = hidden - jnp.mean(hidden, axis=-1, keepdims=True)
    spread = jnp.mean(center * center, axis=-1, keepdims=True)
    return center * lax.rsqrt(spread + EPSILON) * gain + shift


def flat_tables(slot_rows, rotary_dims, head_count, head_size):
    width = head_count * head_size
    halfway = rotary_dims // 2
    position = jnp.arange(slot_rows).astype(jnp.float32)
    column = jnp.arange(width) % head_size
    pair = jnp.where(column < halfway, column, column - halfway)
    inverse = jnp.exp(pair.astype(jnp.float32) * (-2.0 * math.log(10000.0) / rotary_dims))
    angles = position[:, None] * inverse[None, :]
    turned = column < 2 * halfway
    cos_full = jnp.where(turned[None, :], jnp.cos(angles), 1.0)
    sin_full = jnp.where(turned[None, :], jnp.sin(angles), 0.0)
    source = jnp.arange(width)[:, None]
    target = jnp.arange(width)[None, :]
    target_col = target % head_size
    minus_part = (target_col < halfway) & (source == target + halfway)
    plus_part = (target_col >= halfway) & (target_col < 2 * halfway) & (source == target - halfway)
    partner = jnp.where(minus_part, -1.0, 0.0) + jnp.where(plus_part, 1.0, 0.0)
    index = jnp.arange(head_size).astype(jnp.float32)
    table = jnp.cos(math.pi * (index[None, :] + 0.5) * index[:, None] / head_size) * math.sqrt(
        2.0 / head_size
    )
    table = jnp.where(index[:, None] == 0.0, table * math.sqrt(0.5), table)
    same_head = (source // head_size == target // head_size).astype(jnp.float32)
    dct_big = same_head * table[target % head_size, source % head_size]
    head_mask = (jnp.arange(width)[None, :] // head_size == jnp.arange(head_count)[:, None]).astype(
        jnp.float32
    )
    return (cos_full, sin_full, partner, dct_big, head_mask, same_head)


def feat_map(queries, key_rows, scales, keep, tables):
    cos_full, sin_full, partner, dct_big, head_mask, same_head = tables

    def lift(values):
        swapped = jnp.einsum("srd,de->sre", values, partner, precision=HIGHEST)
        turned = values * cos_full + swapped * sin_full
        coeffs = jnp.einsum("srd,de->sre", turned, dct_big, precision=HIGHEST)
        return scales * jnp.exp(coeffs)

    return (lift(queries), lift(key_rows) * keep[:, :, None])


def linear_attend(query_feats, key_feats, value_rows, block, tables):
    cos_full, sin_full, partner, dct_big, head_mask, same_head = tables
    seq_count, slot_rows, width = query_feats.shape
    blocks = slot_rows // block
    query_blocks = query_feats.reshape(seq_count, blocks, block, width)
    key_blocks = key_feats.reshape(seq_count, blocks, block, width)
    value_blocks = value_rows.reshape(seq_count, blocks, block, width)
    causal = (jnp.arange(block)[:, None] >= jnp.arange(block)[None, :]).astype(jnp.float32)
    query_heads = query_blocks[:, :, None, :, :] * head_mask[None, None, :, None, :]
    scores = jnp.einsum("snhid,snjd->snhij", query_heads, key_blocks, precision=HIGHEST) * causal
    inner = jnp.einsum("snhij,snjd->snhid", scores, value_blocks, precision=HIGHEST)
    inner = jnp.sum(inner * head_mask[None, None, :, None, :], axis=2)
    inner_total = jnp.einsum("snhij,hd->snid", scores, head_mask, precision=HIGHEST)
    states = jnp.einsum("snjd,snje->snde", key_blocks, value_blocks, precision=HIGHEST) * same_head
    state_totals = jnp.sum(key_blocks, axis=2)
    earlier = jnp.cumsum(states, axis=1) - states
    earlier_totals = jnp.cumsum(state_totals, axis=1) - state_totals
    outer = jnp.einsum("snid,snde->snie", query_blocks, earlier, precision=HIGHEST)
    outer_total = jnp.einsum(
        "snid,de->snie", query_blocks * earlier_totals[:, :, None, :], same_head, precision=HIGHEST
    )
    result = (inner + outer) / (inner_total + outer_total)
    return result.reshape(seq_count, slot_rows, width)


def body(
    tokens,
    cotangent,
    lengths,
    attn_gain,
    attn_bias,
    ffn_gain,
    ffn_bias,
    w_query,
    w_key,
    w_value,
    w_out,
    feat_scale,
    w_up,
    w_down,
    down_bias,
):
    section_pos = lax.axis_index("section")
    is_first = section_pos == 0
    tensor_pos = lax.axis_index("tensor")
    tensor_count = lax.axis_size("tensor")
    micro_count, seq_count, slot_rows, model_width = tokens.shape
    part_rows = slot_rows // tensor_count
    gain_one = attn_gain[0]
    shift_one = attn_bias[0]
    gain_two = ffn_gain[0]
    shift_two = ffn_bias[0]
    mat_query = w_query[0]
    mat_key = w_key[0]
    mat_value = w_value[0]
    mat_out = w_out[0]
    head_count, head_size = (feat_scale.shape[1], feat_scale.shape[2])
    scales = feat_scale[0].reshape(-1)
    mat_up = w_up[0]
    mat_down = w_down[0]
    bias_back = down_bias[0]
    inner_width = head_count * head_size
    shape_flat = (seq_count, slot_rows, inner_width)
    tables = flat_tables(slot_rows, ROT, head_count, head_size)
    keep_all = (jnp.arange(slot_rows)[None, None, :] < lengths[:, :, None]).astype(jnp.float32)
    slot_count = micro_count + 1

    def own_rows(full_rows):
        return lax.dynamic_slice_in_dim(full_rows, tensor_pos * part_rows, part_rows, 1)

    def attend(query_feats, key_feats, value_rows):
        return linear_attend(query_feats, key_feats, value_rows, SPAN, tables)

    def backward(grad_out, saved, keep):
        (
            stored,
            norm_one,
            norm_two,
            queries,
            key_rows,
            query_low,
            key_low,
            value_rows,
            mixed_low,
            up_rows,
        ) = saved
        grad_low = lax.all_gather(grad_out.astype(jnp.bfloat16), "tensor", axis=1, tiled=True)
        grad_flat = grad_low.reshape(-1, model_width)
        grad_act = jnp.einsum("rd,fd->rf", grad_flat, mat_down, preferred_element_type=jnp.float32)
        act_full, gelu_back = jax.vjp(
            lambda inputs: jax.nn.gelu(inputs, approximate=False), up_rows
        )
        grad_up = gelu_back(grad_act)[0].astype(jnp.bfloat16)
        grad_mixed = jnp.einsum(
            "rd,ed->re", grad_flat, mat_out, preferred_element_type=jnp.float32
        ).astype(jnp.bfloat16)
        attend_out, attend_back = jax.vjp(
            attend,
            query_low.astype(jnp.float32),
            key_low.astype(jnp.float32),
            value_rows.reshape(shape_flat).astype(jnp.float32),
        )
        grad_qfeat, grad_kfeat, grad_values = attend_back(
            grad_mixed.reshape(shape_flat).astype(jnp.float32)
        )

        def features(query_in, key_in, scale_in):
            return feat_map(query_in, key_in, scale_in, keep, tables)

        feat_out, feat_back = jax.vjp(
            features, queries.reshape(shape_flat), key_rows.reshape(shape_flat), scales
        )
        grad_queries, grad_keys, grad_scales = feat_back((grad_qfeat, grad_kfeat))
        grad_scales = grad_scales.reshape(head_count, head_size)
        query_grads = grad_queries.reshape(-1, inner_width).astype(jnp.bfloat16)
        key_grads = grad_keys.reshape(-1, inner_width).astype(jnp.bfloat16)
        value_grads = grad_values.reshape(-1, inner_width).astype(jnp.bfloat16)
        grad_norm_one = jnp.einsum(
            "rf,df->rd", query_grads, mat_query, preferred_element_type=jnp.float32
        )
        grad_norm_one = grad_norm_one + jnp.einsum(
            "rf,df->rd", key_grads, mat_key, preferred_element_type=jnp.float32
        )
        grad_norm_one = grad_norm_one + jnp.einsum(
            "rf,df->rd", value_grads, mat_value, preferred_element_type=jnp.float32
        )
        grad_norm_two = jnp.einsum("rf,df->rd", grad_up, mat_up, preferred_element_type=jnp.float32)
        grad_norm_one = grad_norm_one.reshape(seq_count, slot_rows, model_width)
        grad_norm_two = grad_norm_two.reshape(seq_count, slot_rows, model_width)
        grad_norm_one, grad_norm_two = (
            lax.psum_scatter(
                grad_norm_one.astype(jnp.bfloat16), "tensor", scatter_dimension=1, tiled=True
            ).astype(jnp.float32),
            lax.psum_scatter(
                grad_norm_two.astype(jnp.bfloat16), "tensor", scatter_dimension=1, tiled=True
            ).astype(jnp.float32),
        )
        hidden_f = stored.astype(jnp.float32)
        norm_out, norm_back_one = jax.vjp(layer_norm, hidden_f, gain_one, shift_one)
        grad_hid_one, grad_gain_one, grad_shift_one = norm_back_one(grad_norm_one)
        norm_out, norm_back_two = jax.vjp(layer_norm, hidden_f, gain_two, shift_two)
        grad_hid_two, grad_gain_two, grad_shift_two = norm_back_two(grad_norm_two)
        grad_hid = grad_hid_one + grad_hid_two
        grad_hidden = grad_out + grad_hid
        small_grads = (
            grad_gain_one,
            grad_shift_one,
            grad_gain_two,
            grad_shift_two,
            jnp.sum(grad_out, axis=(0, 1)),
            grad_scales,
        )
        weight_data = (
            norm_one,
            norm_two,
            mixed_low,
            act_full.astype(jnp.bfloat16),
            grad_low,
            grad_up,
            query_grads,
            key_grads,
            value_grads,
        )
        return (grad_hidden, small_grads, weight_data)

    received = jnp.zeros((seq_count, part_rows, model_width), jnp.bfloat16)
    saved_list = []
    output_list = []
    for tick in range(slot_count):
        fresh = own_rows(tokens[min(tick, micro_count - 1)])
        hidden = jnp.where(is_first, fresh, received)
        which = jnp.clip(tick - section_pos, 0, micro_count - 1)
        keep = lax.dynamic_index_in_dim(keep_all, which, 0, keepdims=False)
        forward_hidden_f = hidden.astype(jnp.float32)
        forward_norm_one = layer_norm(forward_hidden_f, gain_one, shift_one).astype(jnp.bfloat16)
        forward_norm_two = layer_norm(forward_hidden_f, gain_two, shift_two).astype(jnp.bfloat16)
        forward_norm_one, forward_norm_two = (
            lax.all_gather(forward_norm_one, "tensor", axis=1, tiled=True),
            lax.all_gather(forward_norm_two, "tensor", axis=1, tiled=True),
        )
        forward_flat_one = forward_norm_one.reshape(-1, model_width)
        forward_flat_two = forward_norm_two.reshape(-1, model_width)
        forward_queries = jnp.dot(forward_flat_one, mat_query, preferred_element_type=jnp.float32)
        forward_key_rows = jnp.dot(forward_flat_one, mat_key, preferred_element_type=jnp.float32)
        forward_value_rows = jnp.dot(
            forward_flat_one, mat_value, preferred_element_type=jnp.float32
        ).astype(jnp.bfloat16)
        forward_query_feats, forward_key_feats = feat_map(
            forward_queries.reshape(shape_flat),
            forward_key_rows.reshape(shape_flat),
            scales,
            keep,
            tables,
        )
        forward_query_low = forward_query_feats.astype(jnp.bfloat16)
        forward_key_low = forward_key_feats.astype(jnp.bfloat16)
        mixed = attend(
            forward_query_low.astype(jnp.float32),
            forward_key_low.astype(jnp.float32),
            forward_value_rows.reshape(shape_flat).astype(jnp.float32),
        )
        forward_mixed_low = mixed.reshape(-1, inner_width).astype(jnp.bfloat16)
        forward_up_rows = jnp.dot(forward_flat_two, mat_up, preferred_element_type=jnp.float32)
        forward_act_rows = jax.nn.gelu(forward_up_rows, approximate=False).astype(jnp.bfloat16)
        branch = jnp.dot(forward_mixed_low, mat_out, preferred_element_type=jnp.float32) + jnp.dot(
            forward_act_rows, mat_down, preferred_element_type=jnp.float32
        )
        summed = lax.psum_scatter(
            branch.reshape(seq_count, slot_rows, model_width),
            "tensor",
            scatter_dimension=1,
            tiled=True,
        )
        result = forward_hidden_f + summed + bias_back
        result, saved = (
            result,
            (
                hidden,
                forward_norm_one,
                forward_norm_two,
                forward_queries,
                forward_key_rows,
                forward_query_low,
                forward_key_low,
                forward_value_rows,
                forward_mixed_low,
                forward_up_rows,
            ),
        )
        saved_list.append(saved)
        output_list.append(result)
        if tick < micro_count:
            received = from_behind(result.astype(jnp.bfloat16), "section", 1)
    saved_all = jax.tree.map(lambda *items: jnp.stack(items), *saved_list)
    back_received = jnp.zeros((seq_count, part_rows, model_width), jnp.bfloat16)
    small_total = None
    weight_list = []
    input_grads = []
    for tick in range(slot_count):
        which = tick - 1 + section_pos
        forward_tick = jnp.clip(tick - 1 + 2 * section_pos, 0, micro_count)
        saved = jax.tree.map(
            lambda stacked: lax.dynamic_index_in_dim(stacked, forward_tick, 0, keepdims=False),
            saved_all,
        )
        micro_pos = jnp.clip(which, 0, micro_count - 1)
        keep = lax.dynamic_index_in_dim(keep_all, micro_pos, 0, keepdims=False)
        given = own_rows(lax.dynamic_index_in_dim(cotangent, micro_pos, 0, keepdims=False)).astype(
            jnp.float32
        )
        grad_out = jnp.where(is_first, back_received.astype(jnp.float32), given)
        grad_hidden, small_grads, weight_data = backward(grad_out, saved, keep)
        valid = ((which >= 0) & (which < micro_count)).astype(jnp.float32)
        small_grads = tuple((valid * item for item in small_grads))
        small_total = (
            small_grads
            if small_total is None
            else tuple((left + right for left, right in zip(small_total, small_grads)))
        )
        weight_list.append(weight_data)
        input_grads.append(grad_hidden)
        if tick < micro_count:
            back_received = from_behind(grad_hidden.astype(jnp.bfloat16), "section", -1)
    ends = jnp.where(is_first, jnp.stack(input_grads[1:]), jnp.stack(output_list[1:]))[None]
    grad_gain_one, grad_shift_one, grad_gain_two, grad_shift_two, grad_bias_back = lax.psum(
        (small_total[0], small_total[1], small_total[2], small_total[3], small_total[4]), "tensor"
    )
    grad_scales = small_total[5]
    weight_all = jax.tree.map(lambda *items: jnp.stack(items), *weight_list)
    weight_sel = jax.tree.map(
        lambda stacked: lax.dynamic_slice_in_dim(stacked, 1 - section_pos, micro_count, 0),
        weight_all,
    )

    def weight_terms(
        norm_one,
        norm_two,
        mixed_low,
        act_rows,
        grad_low,
        grad_up,
        query_grads,
        key_grads,
        value_grads,
    ):
        flat_one = norm_one.reshape(-1, model_width)
        flat_two = norm_two.reshape(-1, model_width)
        flat_grad = grad_low.reshape(-1, model_width)
        flat_mixed = mixed_low.reshape(-1, inner_width)
        flat_act = act_rows.reshape(-1, act_rows.shape[-1])
        flat_up = grad_up.reshape(-1, grad_up.shape[-1])
        grad_wq = jnp.einsum(
            "rd,rf->df",
            flat_one,
            query_grads.reshape(-1, inner_width),
            preferred_element_type=jnp.float32,
        )
        grad_wk = jnp.einsum(
            "rd,rf->df",
            flat_one,
            key_grads.reshape(-1, inner_width),
            preferred_element_type=jnp.float32,
        )
        grad_wv = jnp.einsum(
            "rd,rf->df",
            flat_one,
            value_grads.reshape(-1, inner_width),
            preferred_element_type=jnp.float32,
        )
        grad_wo = jnp.einsum("rf,rd->fd", flat_mixed, flat_grad, preferred_element_type=jnp.float32)
        grad_wup = jnp.einsum("rd,rf->df", flat_two, flat_up, preferred_element_type=jnp.float32)
        grad_wdown = jnp.einsum(
            "rf,rd->fd", flat_act, flat_grad, preferred_element_type=jnp.float32
        )
        return (grad_wq, grad_wk, grad_wv, grad_wo, grad_wup, grad_wdown)

    grad_wq, grad_wk, grad_wv, grad_wo, grad_wup, grad_wdown = weight_terms(*weight_sel)
    shared = (
        lax.psum_scatter(
            grad_gain_one.astype(jnp.bfloat16), "dp", scatter_dimension=0, tiled=True
        ).astype(jnp.float32),
        lax.psum_scatter(
            grad_shift_one.astype(jnp.bfloat16), "dp", scatter_dimension=0, tiled=True
        ).astype(jnp.float32),
        lax.psum_scatter(
            grad_gain_two.astype(jnp.bfloat16), "dp", scatter_dimension=0, tiled=True
        ).astype(jnp.float32),
        lax.psum_scatter(
            grad_shift_two.astype(jnp.bfloat16), "dp", scatter_dimension=0, tiled=True
        ).astype(jnp.float32),
        lax.psum_scatter(
            grad_wq.astype(jnp.bfloat16), "dp", scatter_dimension=0, tiled=True
        ).astype(jnp.float32),
        lax.psum_scatter(
            grad_wk.astype(jnp.bfloat16), "dp", scatter_dimension=0, tiled=True
        ).astype(jnp.float32),
        lax.psum_scatter(
            grad_wv.astype(jnp.bfloat16), "dp", scatter_dimension=0, tiled=True
        ).astype(jnp.float32),
        lax.psum_scatter(
            grad_wo.astype(jnp.bfloat16), "dp", scatter_dimension=1, tiled=True
        ).astype(jnp.float32),
        lax.psum_scatter(
            grad_scales.astype(jnp.bfloat16), "dp", scatter_dimension=1, tiled=True
        ).astype(jnp.float32),
        lax.psum_scatter(
            grad_wup.astype(jnp.bfloat16), "dp", scatter_dimension=0, tiled=True
        ).astype(jnp.float32),
        lax.psum_scatter(
            grad_wdown.astype(jnp.bfloat16), "dp", scatter_dimension=1, tiled=True
        ).astype(jnp.float32),
        lax.psum_scatter(
            grad_bias_back.astype(jnp.bfloat16), "dp", scatter_dimension=0, tiled=True
        ).astype(jnp.float32),
    )
    return (
        ends,
        shared[0][None],
        shared[1][None],
        shared[2][None],
        shared[3][None],
        shared[4][None],
        shared[5][None],
        shared[6][None],
        shared[7][None],
        shared[8][None],
        shared[9][None],
        shared[10][None],
        shared[11][None],
    )


def solution(mesh):
    return jax.shard_map(
        body,
        mesh=mesh,
        in_specs=(
            P(None, "dp", None, None),
            P(None, "dp", None, None),
            P(None, "dp"),
            P("section", None),
            P("section", None),
            P("section", None),
            P("section", None),
            P("section", None, "tensor"),
            P("section", None, "tensor"),
            P("section", None, "tensor"),
            P("section", "tensor", None),
            P("section", "tensor", None),
            P("section", None, "tensor"),
            P("section", "tensor", None),
            P("section", None),
        ),
        out_specs=(
            P("section", None, "dp", "tensor", None),
            P("section", "dp"),
            P("section", "dp"),
            P("section", "dp"),
            P("section", "dp"),
            P("section", "dp", "tensor"),
            P("section", "dp", "tensor"),
            P("section", "dp", "tensor"),
            P("section", "tensor", "dp"),
            P("section", "tensor", "dp"),
            P("section", "dp", "tensor"),
            P("section", "tensor", "dp"),
            P("section", "dp"),
        ),
        check_vma=False,
    )
```

profile of v0, /device:TPU:0, one launch (start us, length us, event | category | flops | bytes accessed | tf_op | source)
XLA Modules:
  0.0 1849.9 jit_solution(12443843675503489840)
XLA Ops:
  7.3 4.8 fusion.1174
  18.5 700.4 %gather_fusion = f32[65536]{0:T(1024)} fusion(f32[64,64]{1,0:T(8,128)S(1)} %multiply_select_fusion, s32[65536]{0:T(1024)S(1)} %bitcast.1113), kind=kCustom, calls=%fused_computation | custom fusion | bytes 1048576 | tf_op jit(solution)/shard_map/gather | solution.py:51
  723.8 4.8 fusion.488
  733.1 5.4 fusion.489
  752.0 4.5 fusion.244
  756.6 10.9 fusion.234
  771.8 47.3 %reduce-scatter.19.cloned.1.call-done = f32[1,256,1024]{2,1,0:T(8,128)} async-done(((f32[1,1024,1024]{2,1,0:T(8,128)}), f32[1,256,1024]{2,1,0:T(8,128)}) %reduce-scatter.19.cloned.1.call-update) | async-done | bytes 1048592 | tf_op jit(solution)/shard_map/reduce_scatter | solution.py:277
  824.1 11.1 collective-permute-done
  839.2 23.1 %all-gather.16.cloned.1.call-done = bf16[1,1024,1024]{2,1,0:T(8,128)(2,1)} async-done(((bf16[1,256,1024]{2,1,0:T(8,128)(2,1)}), bf16[1,1024,1024]{2,1,0:T(8,128)(2,1)}) %all-gather.16.cloned.1.call-update) | async-done | bytes 2097168 | tf_op jit(solution)/shard_map/all_gather | solution.py:247
  865.7 4.8 fusion.486
  875.0 5.0 fusion.487
  895.4 10.8 fusion.232
  919.7 44.2 %reduce-scatter.21.cloned.1.call-done = f32[1,256,1024]{2,1,0:T(8,128)} async-done(((f32[1,1024,1024]{2,1,0:T(8,128)}), f32[1,256,1024]{2,1,0:T(8,128)}) %reduce-scatter.21.cloned.1.call-update) | async-done | bytes 1048592 | tf_op jit(solution)/shard_map/reduce_scatter | solution.py:277
  969.9 11.1 collective-permute-done.1
  991.7 21.2 %all-gather.20.cloned.1.call-done = bf16[1,1024,1024]{2,1,0:T(8,128)(2,1)} async-done(((bf16[1,256,1024]{2,1,0:T(8,128)(2,1)}), bf16[1,1024,1024]{2,1,0:T(8,128)(2,1)}) %all-gather.20.cloned.1.call-update) | async-done | bytes 2097168 | tf_op jit(solution)/shard_map/all_gather | solution.py:247
  1015.5 4.8 fusion.484
  1026.8 5.1 fusion.485
  1043.2 4.6 fusion.14
  1057.0 5.6 multiply_reduce_fusion.9
  1072.0 4.6 fusion.18
  1078.0 5.4 copy.83
  1083.3 5.3 fusion.1175
  1088.6 5.4 copy.84
  1097.8 5.7 fusion.537
  1108.6 8.5 fusion.513
  1124.4 8.2 fusion.511
  1132.7 8.7 fusion.541
  1144.3 8.9 fusion.540
  1165.4 4.7 fusion.210
  1173.4 11.6 fusion.34
  1197.0 34.1 %reduce-scatter.25.cloned.1.call-done = bf16[1,256,1024]{2,1,0:T(8,128)(2,1)} async-done(((bf16[1,1024,1024]{2,1,0:T(8,128)(2,1)}), bf16[1,256,1024]{2,1,0:T(8,128)(2,1)}) %reduce-scatter.25.cloned.1.call-update) | async-done | bytes 524304 | tf_op jit(solution)/shard_map/reduce_scatter | solution.py:203
  1241.3 14.6 collective-permute-done.2
  1259.4 10.4 fusion.517
  1269.7 10.6 fusion.515
  1301.2 4.8 fusion.10
  1309.9 5.4 copy.91
  1315.3 5.3 fusion.1176
  1320.6 5.4 copy.92
  1326.0 5.7 fusion.531
  1339.2 8.7 fusion.543
  1355.4 8.9 fusion.542
  1371.6 13.6 fusion.39
  1402.2 34.6 %reduce-scatter.29.cloned.1.call-done = bf16[1,256,1024]{2,1,0:T(8,128)(2,1)} async-done(((bf16[1,1024,1024]{2,1,0:T(8,128)(2,1)}), bf16[1,256,1024]{2,1,0:T(8,128)(2,1)}) %reduce-scatter.29.cloned.1.call-update) | async-done | bytes 524304 | tf_op jit(solution)/shard_map/reduce_scatter | solution.py:203
  1449.6 12.1 collective-permute-done.3
  1465.7 12.4 fusion.226
  1487.1 9.4 fusion.521
  1496.6 9.0 fusion.519
  1529.5 5.1 convolution_bitcast_fusion
  1534.6 5.4 copy.98
  1540.0 5.4 fusion.1177
  1545.4 5.6 copy.99
  1553.1 4.8 fusion.2
  1583.5 5.7 fusion.452
  1589.5 6.5 fusion.573
  1601.7 8.5 fusion.545
  1617.0 8.5 fusion.544
  1629.9 13.5 fusion.44
  1653.5 28.7 %fusion.56 = (bf16[1,1024,1024]{2,1,0:T(8,128)(2,1)S(1)}, bf16[1,1024,1024]{2,1,0:T(8,128)(2,1)S(1)}, bf16[1,1024,1024]{2,1,0:T(8,128)(2,1)S(1)}) fusion(f32[3,1024,1024]{2,1,0:T(8,128)} %copy-done.4, s32[]{:T(128)S(6)} %min.45, s32[]{:T(128)S(6)} %min.42, s32[]{:T(128)S(6)} %min.38), kind=kLoop, calls=%fused_computation.84 | loop fusion | flops 204472320 | bytes 18874380 | tf_op jit(solution)/shard_map/convert_element_type | solution.py:226
  1684.5 5.8 convolution_convert_fusion
  1706.6 5.8 convolution_convert_fusion.1
  1720.5 28.3 %reduce-scatter.31.cloned.1.call-done = bf16[1,256,1024]{2,1,0:T(8,128)(2,1)} async-done(((bf16[1,1024,1024]{2,1,0:T(8,128)(2,1)}), bf16[1,256,1024]{2,1,0:T(8,128)(2,1)}) %reduce-scatter.31.cloned.1.call-update) | async-done | bytes 524304 | tf_op jit(solution)/shard_map/reduce_scatter | solution.py:200
  1753.4 10.7 all-reduce.5
  1764.1 20.1 %all-reduce.6 = (bf16[1024]{0:T(1024)(128)(2,1)S(1)}, bf16[1024]{0:T(1024)(128)(2,1)S(1)}, bf16[1024]{0:T(1024)(128)(2,1)S(1)}, bf16[1024]{0:T(1024)(128)(2,1)S(1)}, bf16[1024]{0:T(1024)(128)(2,1)S(1)}) all-reduce(bf16[1024]{0:T(1024)(128)(2,1)S(1)} %get-tuple-element.55, ...), channel_id=11, replica_groups=mesh['section'=2,'dp'=4,'tensor'=4] {'dp'}, use_global_device_ids=true, to_apply=%region_79.80.clone | all-reduce | flops 5120 | bytes 20480
  1797.4 43.6 %reduce-scatter.45.cloned.1.call-done = bf16[256,1024]{1,0:T(8,128)(2,1)} async-done(((bf16[1024,1024]{1,0:T(8,128)(2,1)}), bf16[256,1024]{1,0:T(8,128)(2,1)}) %reduce-scatter.45.cloned.1.call-update) | async-done | bytes 524304 | tf_op jit(solution)/shard_map/reduce_scatter | solution.py:415
  (786 shorter events, 407.6 us)
Async XLA Ops:
  7.2 749.4 %copy-start = (bf16[1,1024,1024]{2,1,0:T(8,128)(2,1)S(1)}, bf16[1,1024,1024]{2,1,0:T(8,128)(2,1)}, u32[]{:S(2)}) copy-start(bf16[1,1024,1024]{2,1,0:T(8,128)(2,1)} %param.28) | copy-start | bytes 6291460
  7.2 713.4 %all-gather.12.cloned.1.call-start = ((), (), s32[]{:S(2)}) async-start(), calls=%async_computation.17 | async-start | bytes 2621440 | tf_op jit(solution)/shard_map/all_gather | solution.py:247
  16.8 735.3 %all-gather.14.cloned.1.call-start = ((), (), s32[]{:S(2)}) async-start(), calls=%async_computation.18 | async-start | bytes 2621440 | tf_op jit(solution)/shard_map/all_gather | solution.py:248
  17.5 801.6 %reduce-scatter.19.cloned.1.call-start = ((), (), s32[]{:S(2)}) async-start(), calls=%async_computation.19 | async-start | bytes 5242880 | tf_op jit(solution)/shard_map/reduce_scatter | solution.py:277
  17.6 1126.8 %copy-start.206 = (s32[256]{0:T(256)}, s32[256]{0:T(256)S(1)}, u32[]{:S(2)}) copy-start(s32[256]{0:T(256)S(1)} %get-tuple-element.167) | copy-start | bytes 3076
  17.6 1252.2 %copy-start.203 = (s32[256]{0:T(256)}, s32[256]{0:T(256)S(1)}, u32[]{:S(2)}) copy-start(s32[256]{0:T(256)S(1)} %get-tuple-element.166) | copy-start | bytes 3076
  17.6 1009.2 %copy-start.219 = (pred[256]{0:T(512)(128)(4,1)}, pred[256]{0:T(512)(128)(4,1)S(1)}, u32[]{:S(2)}) copy-start(pred[256]{0:T(512)(128)(4,1)S(1)} %get-tuple-element.162) | copy-start | bytes 772
  17.6 1009.2 %copy-start.223 = (pred[256]{0:T(512)(128)(4,1)}, pred[256]{0:T(512)(128)(4,1)S(1)}, u32[]{:S(2)}) copy-start(pred[256]{0:T(512)(128)(4,1)S(1)} %get-tuple-element.163) | copy-start | bytes 772
  17.6 1009.1 %copy-start.215 = (f32[256]{0:T(256)}, f32[256]{0:T(256)S(1)}, u32[]{:S(2)}) copy-start(f32[256]{0:T(256)S(1)} %fusion.1011) | copy-start | bytes 3076
  17.7 1009.1 %copy-start.227 = (pred[256]{0:T(512)(128)(4,1)}, pred[256]{0:T(512)(128)(4,1)S(1)}, u32[]{:S(2)}) copy-start(pred[256]{0:T(512)(128)(4,1)S(1)} %broadcast_compare_fusion.1) | copy-start | bytes 772
  18.4 701.4 %copy-start.202 = (f32[1,4,64]{2,1,0:T(4,128)S(1)}, f32[1,4,64]{2,1,0:T(4,128)}, u32[]{:S(2)}) copy-start(f32[1,4,64]{2,1,0:T(4,128)} %param.26) | copy-start | bytes 3076
  18.4 702.1 %copy-start.73 = (bf16[1,1024,256]{2,1,0:T(8,128)(2,1)S(1)}, bf16[1,1024,256]{2,1,0:T(8,128)(2,1)}, u32[]{:S(2)}) copy-start(bf16[1,1024,256]{2,1,0:T(8,128)(2,1)} %param.23) | copy-start | bytes 1572868
  771.7 47.4 %copy-start.180 = (f32[1,1024]{1,0:T(1,128)S(1)}, f32[1,1024]{1,0:T(1,128)}, u32[]{:S(2)}) copy-start(f32[1,1024]{1,0:T(1,128)} %param.29) | copy-start | bytes 12292
  771.8 90.6 %all-gather.16.cloned.1.call-start = ((), (), s32[]{:S(2)}) async-start(), calls=%async_computation.20 | async-start | bytes 2621440 | tf_op jit(solution)/shard_map/all_gather | solution.py:247
  820.6 14.6 collective-permute-start
  838.6 50.3 %all-gather.18.cloned.1.call-start = ((), (), s32[]{:S(2)}) async-start(), calls=%async_computation.21 | async-start | bytes 2621440 | tf_op jit(solution)/shard_map/all_gather | solution.py:248
  839.2 124.7 %reduce-scatter.21.cloned.1.call-start = ((), (), s32[]{:S(2)}) async-start(), calls=%async_computation.22 | async-start | bytes 5242880 | tf_op jit(solution)/shard_map/reduce_scatter | solution.py:277
  918.9 69.2 %all-gather.10.cloned.1.call-start = ((), (), s32[]{:S(2)}) async-start(), calls=%async_computation.16 | async-start | bytes 2621440 | tf_op jit(solution)/shard_map/all_gather | solution.py:156
  919.7 93.2 %all-gather.20.cloned.1.call-start = ((), (), s32[]{:S(2)}) async-start(), calls=%async_computation.23 | async-start | bytes 2621440 | tf_op jit(solution)/shard_map/all_gather | solution.py:247
  966.5 14.5 collective-permute-start.1
  984.5 180.9 %all-gather.22.cloned.1.call-start = ((), (), s32[]{:S(2)}) async-start(), calls=%async_computation.25 | async-start | bytes 2621440 | tf_op jit(solution)/shard_map/all_gather | solution.py:248
  991.4 205.6 %reduce-scatter.23.cloned.1.call-start = ((), (), s32[]{:S(2)}) async-start(), calls=%async_computation.24 | async-start | bytes 2621440 | tf_op jit(solution)/shard_map/reduce_scatter | solution.py:200
  1141.4 14.8 copy-start.131
  1165.3 65.9 %reduce-scatter.25.cloned.1.call-start = ((), (), s32[]{:S(2)}) async-start(), calls=%async_computation.26 | async-start | bytes 2621440 | tf_op jit(solution)/shard_map/reduce_scatter | solution.py:203
  1190.1 98.3 %all-gather.24.cloned.1.call-start = ((), (), s32[]{:S(2)}) async-start(), calls=%async_computation.27 | async-start | bytes 2621440 | tf_op jit(solution)/shard_map/all_gather | solution.py:156
  1193.6 65.7 %copy-start.207 = (s32[256]{0:T(256)S(1)}, s32[256]{0:T(256)}, u32[]{:S(2)}) copy-start(s32[256]{0:T(256)} %copy-done.206) | copy-start | bytes 3076
  1240.0 15.9 collective-permute-start.2
  1258.1 144.2 %reduce-scatter.27.cloned.1.call-start = ((), (), s32[]{:S(2)}) async-start(), calls=%async_computation.28 | async-start | bytes 2621440 | tf_op jit(solution)/shard_map/reduce_scatter | solution.py:200
  1259.3 21.1 %copy-start.20 = (f32[16,4,64,64]{2,3,1,0:T(8,128)S(1)}, f32[16,4,64,64]{2,3,1,0:T(8,128)}, u32[]{:S(2)}) copy-start(f32[16,4,64,64]{2,3,1,0:T(8,128)} %copy-done.19) | copy-start | bytes 3145732
  1259.3 21.1 %copy-start.51 = (bf16[1,1024,256]{2,1,0:T(8,128)(2,1)S(1)}, bf16[1,1024,256]{2,1,0:T(8,128)(2,1)}, u32[]{:S(2)}) copy-start(bf16[1,1024,256]{2,1,0:T(8,128)(2,1)} %get-tuple-element.105) | copy-start | bytes 1572868
  1269.7 15.4 copy-start.34
  1371.5 65.3 %reduce-scatter.29.cloned.1.call-start = ((), (), s32[]{:S(2)}) async-start(), calls=%async_computation.29 | async-start | bytes 2621440 | tf_op jit(solution)/shard_map/reduce_scatter | solution.py:203
  1371.6 15.0 copy-start.212
  1390.3 128.9 %all-gather.26.cloned.1.call-start = ((), (), s32[]{:S(2)}) async-start(), calls=%async_computation.30 | async-start | bytes 2621440 | tf_op jit(solution)/shard_map/all_gather | solution.py:156
  1400.1 47.9 %copy-start.183 = (f32[16,4,64]{2,1,0:T(4,128)S(1)}, f32[16,4,64]{2,1,0:T(4,128)}, u32[]{:S(2)}) copy-start(f32[16,4,64]{2,1,0:T(4,128)} %get-tuple-element.51) | copy-start | bytes 49156
  1446.1 15.6 collective-permute-start.3
  1465.6 234.4 %reduce-scatter.35.cloned.1.call-start = ((), (), s32[]{:S(2)}) async-start(), calls=%async_computation.33 | async-start | bytes 5242880 | tf_op jit(solution)/shard_map/reduce_scatter | solution.py:277
  1480.8 231.8 %reduce-scatter.49.cloned.1.call-start = ((), (), s32[]{:S(2)}) async-start(), calls=%async_computation.40 | async-start | bytes 20480
  1487.1 18.5 copy-start.18
  1487.1 18.5 copy-start.47
  1496.5 13.8 copy-start.142
  1496.5 13.8 copy-start.145
  1496.5 13.8 copy-start.148
  1575.3 138.7 %reduce-scatter.43.cloned.1.call-start = ((), (), s32[]{:S(2)}) async-start(), calls=%async_computation.37 | async-start | bytes 655360 | tf_op jit(solution)/shard_map/reduce_scatter | solution.py:409
  1589.2 126.4 %reduce-scatter.41.cloned.1.call-start = ((), (), s32[]{:S(2)}) async-start(), calls=%async_computation.36 | async-start | bytes 655360 | tf_op jit(solution)/shard_map/reduce_scatter | solution.py:406
  1598.9 118.4 %reduce-scatter.39.cloned.1.call-start = ((), (), s32[]{:S(2)}) async-start(), calls=%async_computation.35 | async-start | bytes 655360 | tf_op jit(solution)/shard_map/reduce_scatter | solution.py:403
  1598.9 13.2 copy-start.107
  1614.2 104.6 %reduce-scatter.37.cloned.1.call-start = ((), (), s32[]{:S(2)}) async-start(), calls=%async_computation.34 | async-start | bytes 655360 | tf_op jit(solution)/shard_map/reduce_scatter | solution.py:400
  1629.4 91.1 %reduce-scatter.33.cloned.1.call-start = ((), (), s32[]{:S(2)}) async-start(), calls=%async_computation.32 | async-start | bytes 2621440 | tf_op jit(solution)/shard_map/reduce_scatter | solution.py:203
  1629.9 14.9 copy-start.213
  1648.5 100.3 %reduce-scatter.31.cloned.1.call-start = ((), (), s32[]{:S(2)}) async-start(), calls=%async_computation.31 | async-start | bytes 2621440 | tf_op jit(solution)/shard_map/reduce_scatter | solution.py:200
  1653.4 141.9 %reduce-scatter.47.cloned.1.call-start = ((), (), s32[]{:S(2)}) async-start(), calls=%async_computation.39 | async-start | bytes 2621440 | tf_op jit(solution)/shard_map/reduce_scatter | solution.py:418
  1690.3 150.7 %reduce-scatter.45.cloned.1.call-start = ((), (), s32[]{:S(2)}) async-start(), calls=%async_computation.38 | async-start | bytes 2621440 | tf_op jit(solution)/shard_map/reduce_scatter | solution.py:415
  1706.6 42.2 %copy-start.173 = (f32[1,1024]{1,0:T(1,128)S(1)}, f32[1,1024]{1,0:T(1,128)}, u32[]{:S(2)}) copy-start(f32[1,1024]{1,0:T(1,128)} %param.18) | copy-start | bytes 12292
  1706.6 42.2 %copy-start.175 = (f32[1,1024]{1,0:T(1,128)S(1)}, f32[1,1024]{1,0:T(1,128)}, u32[]{:S(2)}) copy-start(f32[1,1024]{1,0:T(1,128)} %param.20) | copy-start | bytes 12292
  1712.5 38.4 %copy-start.188 = (f32[1024]{0:T(1024)S(1)}, f32[1024]{0:T(1024)}, u32[]{:S(2)}) copy-start(f32[1024]{0:T(1024)} %get-tuple-element.45) | copy-start | bytes 12292
  1712.5 38.4 %copy-start.192 = (f32[1024]{0:T(1024)S(1)}, f32[1024]{0:T(1024)}, u32[]{:S(2)}) copy-start(f32[1024]{0:T(1024)} %get-tuple-element.46) | copy-start | bytes 12292
  1712.5 40.9 %copy-start.189 = (f32[1024]{0:T(1024)S(1)}, f32[1024]{0:T(1024)}, u32[]{:S(2)}) copy-start(f32[1024]{0:T(1024)} %get-tuple-element.15) | copy-start | bytes 12292
  1712.5 40.9 %copy-start.193 = (f32[1024]{0:T(1024)S(1)}, f32[1024]{0:T(1024)}, u32[]{:S(2)}) copy-start(f32[1024]{0:T(1024)} %get-tuple-element.17) | copy-start | bytes 12292
  1712.5 40.9 %copy-start.187 = (f32[1024]{0:T(1024)S(1)}, f32[1024]{0:T(1024)}, u32[]{:S(2)}) copy-start(f32[1024]{0:T(1024)} %get-tuple-element.50) | copy-start | bytes 12292
  1712.5 40.9 %copy-start.191 = (f32[1024]{0:T(1024)S(1)}, f32[1024]{0:T(1024)}, u32[]{:S(2)}) copy-start(f32[1024]{0:T(1024)} %get-tuple-element.49) | copy-start | bytes 12292
  1712.5 40.9 %copy-start.186 = (f32[1024]{0:T(1024)S(1)}, f32[1024]{0:T(1024)}, u32[]{:S(2)}) copy-start(f32[1024]{0:T(1024)} %get-tuple-element.28) | copy-start | bytes 12292
  1712.5 40.9 %copy-start.190 = (f32[1024]{0:T(1024)S(1)}, f32[1024]{0:T(1024)}, u32[]{:S(2)}) copy-start(f32[1024]{0:T(1024)} %get-tuple-element.30) | copy-start | bytes 12292
  1712.5 74.9 %copy-start.134 = (bf16[1,256,1024]{2,1,0:T(8,128)(2,1)S(1)}, bf16[1,256,1024]{2,1,0:T(8,128)(2,1)}, u32[]{:S(2)}) copy-start(bf16[1,256,1024]{2,1,0:T(8,128)(2,1)} %copy-done.133) | copy-start | bytes 1572868
  (196 other events, 1055.9 us)
Sparse Core Ops, SparseCore 0:
  16.9 25.2 all-gather.11
  43.8 22.5 all-gather.13
  771.9 47.1 reduce-scatter.18
  838.7 23.5 all-gather.15
  864.4 22.5 all-gather.17
  919.0 44.8 reduce-scatter.20
  965.5 22.5 all-gather.9
  990.3 22.5 all-gather.19
  1014.5 22.5 all-gather.21
  1165.5 31.5 reduce-scatter.22
  1199.7 31.3 reduce-scatter.24
  1258.2 21.6 all-gather.23
  1371.7 30.5 reduce-scatter.26
  1405.4 31.3 reduce-scatter.28
  1465.8 21.7 all-gather.25
  1489.9 44.4 reduce-scatter.34
  1575.4 17.9 reduce-scatter.48
  1595.6 19.7 reduce-scatter.42
  1617.7 19.8 reduce-scatter.40
  1639.7 19.8 reduce-scatter.38
  1661.9 19.8 reduce-scatter.36
  1684.4 29.6 reduce-scatter.32
  1717.4 31.4 reduce-scatter.30
  1751.0 44.3 reduce-scatter.46
  1797.8 43.2 reduce-scatter.44
where the time goes:
time: 1850 us
  local copies, waits for them, and re-layouts  776 us (42%)
  matrix products  508 us (27%)
  waiting for transfers between devices  339 us (18%)
  other arithmetic  166 us (9%)
  blocking collectives  30.8 us (2%)
  between operations  18.6 us (1%)
    gather x2, local copies, waits for them, and re-layouts, flat_tables(): dct_big = same_head * table[target % head_size, source % head_size]  701 us
    dot_general x18, matrix products, lift(): swapped = jnp.einsum('srd,de->sre', values, partner, precision=HIGHEST)  138 us
    reduce_scatter x3, waiting for transfers between devices, body(): lax.psum_scatter(branch.reshape(seq_count, slot_rows, model_width), 'tens...  91.5 us
    reduce_scatter x3, waiting for transfers between devices, backward(): lax.psum_scatter(grad_norm_two.astype(jnp.bfloat16), 'tensor', scatter_di...  68.7 us
    ppermute x4, waiting for transfers between devices, from_behind(): return lax.ppermute(x, axis, pairs)  48.9 us
    all_gather x3, waiting for transfers between devices, body(): lax.all_gather(forward_norm_one, 'tensor', axis=1, tiled=True)  44.4 us
    reduce_scatter x1, waiting for transfers between devices, body(): lax.psum_scatter(grad_wup.astype(jnp.bfloat16), 'dp', scatter_dimension=0...  43.6 us
    dot_general x12, matrix products, linear_attend(): jnp.einsum('snhij,snjd->snhid', scores, value_blocks, precision=HIGHEST)  43 us
  transfers between devices with their start and end apart: 29, of which 16 were waited for; matrix products, arithmetic and copies ran while one was open for 68% of the time, Pallas kernels for 0%

commit v1 on v0

--- a/solution.py
+++ b/solution.py
@@ -2,6 +2,7 @@
 
 import jax
 import jax.numpy as jnp
+import numpy as np
 from jax import lax
 from jax.sharding import PartitionSpec as P
 
@@ -42,13 +43,11 @@
     minus_part = (target_col < halfway) & (source == target + halfway)
     plus_part = (target_col >= halfway) & (target_col < 2 * halfway) & (source == target - halfway)
     partner = jnp.where(minus_part, -1.0, 0.0) + jnp.where(plus_part, 1.0, 0.0)
-    index = jnp.arange(head_size).astype(jnp.float32)
-    table = jnp.cos(math.pi * (index[None, :] + 0.5) * index[:, None] / head_size) * math.sqrt(
-        2.0 / head_size
-    )
-    table = jnp.where(index[:, None] == 0.0, table * math.sqrt(0.5), table)
+    order = np.arange(head_size)
+    table = np.cos(np.pi * (order[None, :] + 0.5) * order[:, None] / head_size) * np.sqrt(2.0 / head_size)
+    table = np.where(order[:, None] == 0, table * np.sqrt(0.5), table)
     same_head = (source // head_size == target // head_size).astype(jnp.float32)
-    dct_big = same_head * table[target % head_size, source % head_size]
+    dct_big = jnp.asarray(np.kron(np.eye(head_count), table.T), jnp.float32)
     head_mask = (jnp.arange(width)[None, :] // head_size == jnp.arange(head_count)[:, None]).astype(
         jnp.float32
     )

time: 1850 us -> 1180 us (0.64)
  local copies, waits for them, and re-layouts: 776 us -> 75.4 us
  waiting for transfers between devices: 339 us -> 365 us
    gather x2 -> x0, local copies, waits for them, and re-layouts: 701 us -> none  [flat_tables(): dct_big = same_head * table[target % head_size, source % head_size]]
    all_gather x3, waiting for transfers between devices: 44.4 us -> 68 us  [body(): lax.all_gather(forward_norm_one, 'tensor', axis=1, tiled=True)]
  transfers between devices with their start and end apart: 29 -> 29, of which waited for: 16 -> 17; matrix products, arithmetic and copies ran while one was open for 68% -> 47% of each run, Pallas kernels for 0% -> 0%
where the time goes in v1:
time: 1180 us; the launch traced here: 1170 us
  matrix products  505 us (43%)
  waiting for transfers between devices  365 us (31%)
  other arithmetic  162 us (14%)
  local copies, waits for them, and re-layouts  75.4 us (6%)
  blocking collectives  30.8 us (3%)
  between operations  18.5 us (2%)
    dot_general x18, matrix products, lift(): swapped = jnp.einsum('srd,de->sre', values, partner, precision=HIGHEST)  138 us
    reduce_scatter x3, waiting for transfers between devices, body(): lax.psum_scatter(branch.reshape(seq_count, slot_rows, model_width), 'tens...  89.1 us
    reduce_scatter x3, waiting for transfers between devices, backward(): lax.psum_scatter(grad_norm_two.astype(jnp.bfloat16), 'tensor', scatter_di...  68.7 us
    all_gather x3, waiting for transfers between devices, body(): lax.all_gather(forward_norm_one, 'tensor', axis=1, tiled=True)  68 us
    ppermute x4, waiting for transfers between devices, from_behind(): return lax.ppermute(x, axis, pairs)  48.9 us
    reduce_scatter x1, waiting for transfers between devices, body(): lax.psum_scatter(grad_wup.astype(jnp.bfloat16), 'dp', scatter_dimension=0...  43.6 us
    dot_general x12, matrix products, linear_attend(): jnp.einsum('snhij,snjd->snhid', scores, value_blocks, precision=HIGHEST)  42.9 us
    dot_general x12, matrix products, linear_attend(): jnp.einsum('snhid,snjd->snhij', query_heads, key_blocks, precision=HIGHEST)  40.5 us
  transfers between devices with their start and end apart: 29, of which 17 were waited for; matrix products, arithmetic and copies ran while one was open for 47% of the time, Pallas kernels for 0%

profile of v1, /device:TPU:0, one launch (start us, length us, event | category | flops | bytes accessed | tf_op | source)
XLA Modules:
  0.0 1168.1 jit_solution(4327451604387922884)
XLA Ops:
  7.3 4.8 fusion.1170
  19.1 23.6 %all-gather.12.cloned.1.call-done = bf16[1,1024,1024]{2,1,0:T(8,128)(2,1)} async-done(((bf16[1,256,1024]{2,1,0:T(8,128)(2,1)}), bf16[1,1024,1024]{2,1,0:T(8,128)(2,1)}) %all-gather.12.cloned.1.call-update) | async-done | bytes 2097168 | tf_op jit(solution)/shard_map/all_gather | solution.py:246
  46.0 4.8 fusion.488
  55.1 5.3 fusion.489
  78.5 10.9 fusion.234
  93.7 44.9 %reduce-scatter.19.cloned.1.call-done = f32[1,256,1024]{2,1,0:T(8,128)} async-done(((f32[1,1024,1024]{2,1,0:T(8,128)}), f32[1,256,1024]{2,1,0:T(8,128)}) %reduce-scatter.19.cloned.1.call-update) | async-done | bytes 1048592 | tf_op jit(solution)/shard_map/reduce_scatter | solution.py:276
  143.6 11.1 collective-permute-done
  158.8 23.1 %all-gather.16.cloned.1.call-done = bf16[1,1024,1024]{2,1,0:T(8,128)(2,1)} async-done(((bf16[1,256,1024]{2,1,0:T(8,128)(2,1)}), bf16[1,1024,1024]{2,1,0:T(8,128)(2,1)}) %all-gather.16.cloned.1.call-update) | async-done | bytes 2097168 | tf_op jit(solution)/shard_map/all_gather | solution.py:246
  185.3 4.8 fusion.486
  194.5 5.0 fusion.487
  208.3 4.5 fusion.218
  214.9 10.8 fusion.232
  239.1 44.2 %reduce-scatter.21.cloned.1.call-done = f32[1,256,1024]{2,1,0:T(8,128)} async-done(((f32[1,1024,1024]{2,1,0:T(8,128)}), f32[1,256,1024]{2,1,0:T(8,128)}) %reduce-scatter.21.cloned.1.call-update) | async-done | bytes 1048592 | tf_op jit(solution)/shard_map/reduce_scatter | solution.py:276
  289.2 11.1 collective-permute-done.1
  311.0 21.2 %all-gather.20.cloned.1.call-done = bf16[1,1024,1024]{2,1,0:T(8,128)(2,1)} async-done(((bf16[1,256,1024]{2,1,0:T(8,128)(2,1)}), bf16[1,1024,1024]{2,1,0:T(8,128)(2,1)}) %all-gather.20.cloned.1.call-update) | async-done | bytes 2097168 | tf_op jit(solution)/shard_map/all_gather | solution.py:246
  334.8 4.9 fusion.484
  346.2 5.1 fusion.485
  362.6 4.6 fusion.14
  376.4 5.6 multiply_reduce_fusion.9
  391.4 4.6 fusion.18
  397.3 5.3 copy.59
  402.7 5.3 fusion.1171
  408.0 5.3 copy.60
  417.2 5.7 fusion.537
  427.9 8.5 fusion.513
  443.7 8.2 fusion.511
  451.9 8.7 fusion.541
  463.4 8.9 fusion.540
  484.5 4.7 fusion.210
  492.4 11.6 fusion.34
  516.0 34.1 %reduce-scatter.25.cloned.1.call-done = bf16[1,256,1024]{2,1,0:T(8,128)(2,1)} async-done(((bf16[1,1024,1024]{2,1,0:T(8,128)(2,1)}), bf16[1,256,1024]{2,1,0:T(8,128)(2,1)}) %reduce-scatter.25.cloned.1.call-update) | async-done | bytes 524304 | tf_op jit(solution)/shard_map/reduce_scatter | solution.py:202
  560.2 14.6 %collective-permute-done.2 = bf16[1,256,1024]{2,1,0:T(8,128)(2,1)} collective-permute-done((bf16[1,256,1024]{2,1,0:T(8,128)(2,1)}, bf16[1,256,1024]{2,1,0:T(8,128)(2,1)}, u32[]{:S(2)}, u32[]{:S(2)}) %collective-permute-start.2) | collective-permute-done | bytes 524320 | tf_op jit(solution)/shard_map/ppermute | solution.py:20
  578.3 10.4 fusion.517
  588.7 10.6 fusion.515
  620.1 4.8 fusion.10
  628.8 5.4 copy.67
  634.2 5.3 fusion.1172
  639.5 5.4 copy.68
  644.9 5.7 fusion.531
  658.0 8.7 fusion.543
  674.0 8.9 fusion.542
  690.2 13.6 %fusion.39 = bf16[1024,1024]{1,0:T(8,128)(2,1)S(1)} fusion(f32[3,1024,1024]{2,1,0:T(8,128)} %copy-done.5, s32[]{:T(128)S(6)} %min.42, bf16[1,1024,1024]{2,1,0:T(8,128)(2,1)S(1)} %copy-done, bf16[1,1024,1024]{2,1,0:T(8,128)(2,1)} %all-gather.24.cloned.1.call-done), kind=kOutput, calls=%fused_computation.66 | convolution fusion | flops 2222981120 | bytes 10485764 | tf_op jit(solution)/shard_map/rd,fd->rf/dot_general | solution.py:157
  720.8 34.6 %reduce-scatter.29.cloned.1.call-done = bf16[1,256,1024]{2,1,0:T(8,128)(2,1)} async-done(((bf16[1,1024,1024]{2,1,0:T(8,128)(2,1)}), bf16[1,256,1024]{2,1,0:T(8,128)(2,1)}) %reduce-scatter.29.cloned.1.call-update) | async-done | bytes 524304 | tf_op jit(solution)/shard_map/reduce_scatter | solution.py:202
  768.1 12.0 %collective-permute-done.3 = bf16[1,256,1024]{2,1,0:T(8,128)(2,1)S(1)} collective-permute-done((bf16[1,256,1024]{2,1,0:T(8,128)(2,1)S(1)}, bf16[1,256,1024]{2,1,0:T(8,128)(2,1)S(1)}, u32[]{:S(2)}, u32[]{:S(2)}) %collective-permute-start.3) | collective-permute-done | bytes 524320 | tf_op jit(solution)/shard_map/ppermute | solution.py:20
  784.3 12.4 %fusion.226 = f32[1024,1024]{1,0:T(8,128)S(1)} fusion(bf16[1,1024,1024]{2,1,0:T(8,128)(2,1)S(1)} %copy-done, f32[1024,1024]{1,0:T(8,128)} %copy-done.123), kind=kOutput, calls=%fused_computation.337 | convolution fusion | flops 2215641088 | bytes 10485760 | tf_op jit(solution)/shard_map/dot_general | solution.py:273
  805.5 9.4 fusion.521
  815.0 9.0 fusion.519
  847.9 5.1 convolution_bitcast_fusion
  853.0 5.4 copy.74
  858.4 5.4 fusion.1173
  863.8 5.6 copy.75
  871.6 4.7 fusion.2
  901.6 5.7 fusion.452
  907.6 6.4 fusion.573
  919.6 8.5 fusion.545
  932.3 8.5 fusion.544
  944.2 13.5 %fusion.44 = bf16[1024,1024]{1,0:T(8,128)(2,1)S(1)} fusion(f32[3,1024,1024]{2,1,0:T(8,128)} %copy-done.5, s32[]{:T(128)S(6)} %min.45, bf16[1,1024,1024]{2,1,0:T(8,128)(2,1)S(1)} %copy-done, bf16[1,1024,1024]{2,1,0:T(8,128)(2,1)} %all-gather.26.cloned.1.call-done), kind=kOutput, calls=%fused_computation.71 | convolution fusion | flops 2222981120 | bytes 10485764 | tf_op jit(solution)/shard_map/rd,fd->rf/dot_general | solution.py:157
  967.8 28.7 %fusion.56 = (bf16[1,1024,1024]{2,1,0:T(8,128)(2,1)S(1)}, bf16[1,1024,1024]{2,1,0:T(8,128)(2,1)S(1)}, bf16[1,1024,1024]{2,1,0:T(8,128)(2,1)S(1)}) fusion(f32[3,1024,1024]{2,1,0:T(8,128)} %copy-done.5, s32[]{:T(128)S(6)} %min.45, s32[]{:T(128)S(6)} %min.42, s32[]{:T(128)S(6)} %min.38), kind=kLoop, calls=%fused_computation.83 | loop fusion | flops 204472320 | bytes 18874380 | tf_op jit(solution)/shard_map/convert_element_type | solution.py:225
  998.8 5.8 convolution_convert_fusion
  1021.5 5.8 convolution_convert_fusion.1
  1035.4 31.7 %reduce-scatter.31.cloned.1.call-done = bf16[1,256,1024]{2,1,0:T(8,128)(2,1)} async-done(((bf16[1,1024,1024]{2,1,0:T(8,128)(2,1)}), bf16[1,256,1024]{2,1,0:T(8,128)(2,1)}) %reduce-scatter.31.cloned.1.call-update) | async-done | bytes 524304 | tf_op jit(solution)/shard_map/reduce_scatter | solution.py:199
  1071.7 10.7 all-reduce.5
  1082.4 20.1 %all-reduce.6 = (bf16[1024]{0:T(1024)(128)(2,1)S(1)}, bf16[1024]{0:T(1024)(128)(2,1)S(1)}, bf16[1024]{0:T(1024)(128)(2,1)S(1)}, bf16[1024]{0:T(1024)(128)(2,1)S(1)}, bf16[1024]{0:T(1024)(128)(2,1)S(1)}) all-reduce(bf16[1024]{0:T(1024)(128)(2,1)S(1)} %get-tuple-element.55, ...), channel_id=11, replica_groups=mesh['section'=2,'dp'=4,'tensor'=4] {'dp'}, use_global_device_ids=true, to_apply=%region_79.80.clone | all-reduce | flops 5120 | bytes 20480
  1115.7 43.6 %reduce-scatter.45.cloned.1.call-done = bf16[256,1024]{1,0:T(8,128)(2,1)} async-done(((bf16[1024,1024]{1,0:T(8,128)(2,1)}), bf16[256,1024]{1,0:T(8,128)(2,1)}) %reduce-scatter.45.cloned.1.call-update) | async-done | bytes 524304 | tf_op jit(solution)/shard_map/reduce_scatter | solution.py:414
  (781 shorter events, 401.9 us)
Async XLA Ops:
  7.2 71.3 %copy-start = (bf16[1,1024,1024]{2,1,0:T(8,128)(2,1)S(1)}, bf16[1,1024,1024]{2,1,0:T(8,128)(2,1)}, u32[]{:S(2)}) copy-start(bf16[1,1024,1024]{2,1,0:T(8,128)(2,1)} %param.29) | copy-start | bytes 6291460
  7.2 35.5 %all-gather.12.cloned.1.call-start = ((), (), s32[]{:S(2)}) async-start(), calls=%async_computation.17 | async-start | bytes 2621440 | tf_op jit(solution)/shard_map/all_gather | solution.py:246
  12.1 30.6 %copy-start.77 = (bf16[1,1024,256]{2,1,0:T(8,128)(2,1)S(1)}, bf16[1,1024,256]{2,1,0:T(8,128)(2,1)}, u32[]{:S(2)}) copy-start(bf16[1,1024,256]{2,1,0:T(8,128)(2,1)} %param.24) | copy-start | bytes 1572868
  17.2 56.7 %all-gather.14.cloned.1.call-start = ((), (), s32[]{:S(2)}) async-start(), calls=%async_computation.18 | async-start | bytes 2621440 | tf_op jit(solution)/shard_map/all_gather | solution.py:247
  18.0 120.7 %reduce-scatter.19.cloned.1.call-start = ((), (), s32[]{:S(2)}) async-start(), calls=%async_computation.19 | async-start | bytes 5242880 | tf_op jit(solution)/shard_map/reduce_scatter | solution.py:276
  18.0 445.4 %copy-start.213 = (s32[256]{0:T(256)}, s32[256]{0:T(256)S(1)}, u32[]{:S(2)}) copy-start(s32[256]{0:T(256)S(1)} %get-tuple-element.165) | copy-start | bytes 3076
  18.1 328.1 %copy-start.224 = (pred[256]{0:T(512)(128)(4,1)}, pred[256]{0:T(512)(128)(4,1)S(1)}, u32[]{:S(2)}) copy-start(pred[256]{0:T(512)(128)(4,1)S(1)} %get-tuple-element.160) | copy-start | bytes 772
  18.1 328.1 %copy-start.227 = (pred[256]{0:T(512)(128)(4,1)}, pred[256]{0:T(512)(128)(4,1)S(1)}, u32[]{:S(2)}) copy-start(pred[256]{0:T(512)(128)(4,1)S(1)} %get-tuple-element.161) | copy-start | bytes 772
  18.1 328.1 %copy-start.221 = (f32[256]{0:T(256)}, f32[256]{0:T(256)S(1)}, u32[]{:S(2)}) copy-start(f32[256]{0:T(256)S(1)} %fusion.1011) | copy-start | bytes 3076
  18.1 328.1 %copy-start.230 = (pred[256]{0:T(512)(128)(4,1)}, pred[256]{0:T(512)(128)(4,1)S(1)}, u32[]{:S(2)}) copy-start(pred[256]{0:T(512)(128)(4,1)S(1)} %broadcast_compare_fusion.1) | copy-start | bytes 772
  19.1 31.7 %copy-start.1 = (f32[256,256]{1,0:T(8,128)S(1)}, f32[256,256]{1,0:T(8,128)}, u32[]{:S(2)}) copy-start(f32[256,256]{1,0:T(8,128)} %constant.379.clone) | copy-start | bytes 786436
  93.6 45.0 %copy-start.190 = (f32[1,1024]{1,0:T(1,128)S(1)}, f32[1,1024]{1,0:T(1,128)}, u32[]{:S(2)}) copy-start(f32[1,1024]{1,0:T(1,128)} %param.30) | copy-start | bytes 12292
  93.7 88.3 %all-gather.16.cloned.1.call-start = ((), (), s32[]{:S(2)}) async-start(), calls=%async_computation.20 | async-start | bytes 2621440 | tf_op jit(solution)/shard_map/all_gather | solution.py:246
  140.2 14.6 %collective-permute-start = (bf16[1,256,1024]{2,1,0:T(8,128)(2,1)S(1)}, bf16[1,256,1024]{2,1,0:T(8,128)(2,1)S(1)}, u32[]{:S(2)}, u32[]{:S(2)}) collective-permute-start(bf16[1,256,1024]{2,1,0:T(8,128)(2,1)S(1)} %fusion.628), channel_id=1, source_target_pairs={{0,16},{1,17},{2,18},{3,19},{4,20},{5,21},{6,22},{7,23},{8,24},{9,... | collective-permute-start | bytes 1572872 | tf_op jit(solution)/shard_map/ppermute | solution.py:20
  158.2 50.1 %all-gather.18.cloned.1.call-start = ((), (), s32[]{:S(2)}) async-start(), calls=%async_computation.21 | async-start | bytes 2621440 | tf_op jit(solution)/shard_map/all_gather | solution.py:247
  158.8 124.5 %reduce-scatter.21.cloned.1.call-start = ((), (), s32[]{:S(2)}) async-start(), calls=%async_computation.22 | async-start | bytes 5242880 | tf_op jit(solution)/shard_map/reduce_scatter | solution.py:276
  238.3 69.2 %all-gather.10.cloned.1.call-start = ((), (), s32[]{:S(2)}) async-start(), calls=%async_computation.16 | async-start | bytes 2621440 | tf_op jit(solution)/shard_map/all_gather | solution.py:155
  239.1 93.2 %all-gather.20.cloned.1.call-start = ((), (), s32[]{:S(2)}) async-start(), calls=%async_computation.23 | async-start | bytes 2621440 | tf_op jit(solution)/shard_map/all_gather | solution.py:246
  285.8 14.5 %collective-permute-start.1 = (bf16[1,256,1024]{2,1,0:T(8,128)(2,1)S(1)}, bf16[1,256,1024]{2,1,0:T(8,128)(2,1)S(1)}, u32[]{:S(2)}, u32[]{:S(2)}) collective-permute-start(bf16[1,256,1024]{2,1,0:T(8,128)(2,1)S(1)} %get-tuple-element.100), channel_id=1, source_target_pairs={{0,16},{1,17},{2,18},{3,19},{4,20},{5,21},{6,22},{7,23},{8,24},{9,... | collective-permute-start | bytes 1572872 | tf_op jit(solution)/shard_map/ppermute | solution.py:20
  303.8 180.6 %all-gather.22.cloned.1.call-start = ((), (), s32[]{:S(2)}) async-start(), calls=%async_computation.25 | async-start | bytes 2621440 | tf_op jit(solution)/shard_map/all_gather | solution.py:247
  304.0 380.4 %copy-start.62 = (f32[256,256]{0,1:T(8,128)}, f32[256,256]{0,1:T(8,128)S(1)}, u32[]{:S(2)}) copy-start(f32[256,256]{0,1:T(8,128)S(1)} %copy.61) | copy-start | bytes 786436
  310.8 205.2 %reduce-scatter.23.cloned.1.call-start = ((), (), s32[]{:S(2)}) async-start(), calls=%async_computation.24 | async-start | bytes 2621440 | tf_op jit(solution)/shard_map/reduce_scatter | solution.py:199
  460.6 14.6 %copy-start.140 = (bf16[1024,256]{1,0:T(8,128)(2,1)}, bf16[1024,256]{1,0:T(8,128)(2,1)S(1)}, u32[]{:S(2)}) copy-start(bf16[1024,256]{1,0:T(8,128)(2,1)S(1)} %fusion.541) | copy-start | bytes 1572868
  484.4 65.7 %reduce-scatter.25.cloned.1.call-start = ((), (), s32[]{:S(2)}) async-start(), calls=%async_computation.26 | async-start | bytes 2621440 | tf_op jit(solution)/shard_map/reduce_scatter | solution.py:202
  509.1 98.1 %all-gather.24.cloned.1.call-start = ((), (), s32[]{:S(2)}) async-start(), calls=%async_computation.27 | async-start | bytes 2621440 | tf_op jit(solution)/shard_map/all_gather | solution.py:155
  512.6 65.6 %copy-start.214 = (s32[256]{0:T(256)S(1)}, s32[256]{0:T(256)}, u32[]{:S(2)}) copy-start(s32[256]{0:T(256)} %copy-done.213) | copy-start | bytes 3076
  558.9 15.9 %collective-permute-start.2 = (bf16[1,256,1024]{2,1,0:T(8,128)(2,1)}, bf16[1,256,1024]{2,1,0:T(8,128)(2,1)}, u32[]{:S(2)}, u32[]{:S(2)}) collective-permute-start(bf16[1,256,1024]{2,1,0:T(8,128)(2,1)} %fusion.702), channel_id=1, source_target_pairs={{16,0},{17,1},{18,2},{19,3},{20,4},{21,5},{22,6},{23,7},{24,8},{25... | collective-permute-start | bytes 1572872 | tf_op jit(solution)/shard_map/ppermute | solution.py:20
  577.0 143.8 %reduce-scatter.27.cloned.1.call-start = ((), (), s32[]{:S(2)}) async-start(), calls=%async_computation.28 | async-start | bytes 2621440 | tf_op jit(solution)/shard_map/reduce_scatter | solution.py:199
  578.2 21.0 %copy-start.21 = (f32[16,4,64,64]{2,3,1,0:T(8,128)S(1)}, f32[16,4,64,64]{2,3,1,0:T(8,128)}, u32[]{:S(2)}) copy-start(f32[16,4,64,64]{2,3,1,0:T(8,128)} %copy-done.20) | copy-start | bytes 3145732
  578.2 21.0 %copy-start.52 = (bf16[1,1024,256]{2,1,0:T(8,128)(2,1)S(1)}, bf16[1,1024,256]{2,1,0:T(8,128)(2,1)}, u32[]{:S(2)}) copy-start(bf16[1,1024,256]{2,1,0:T(8,128)(2,1)} %get-tuple-element.105) | copy-start | bytes 1572868
  588.7 15.4 %copy-start.35 = (bf16[1,1,1024,256]{3,2,1,0:T(8,128)(2,1)S(1)}, bf16[1,1,1024,256]{3,2,1,0:T(8,128)(2,1)}, u32[]{:S(2)}) copy-start(bf16[1,1,1024,256]{3,2,1,0:T(8,128)(2,1)} %get-tuple-element.111) | copy-start | bytes 1572868
  611.7 13.2 %copy-start.44 = (f32[16,64,256]{2,1,0:T(8,128)}, f32[16,64,256]{2,1,0:T(8,128)S(1)}, u32[]{:S(2)}) copy-start(f32[16,64,256]{2,1,0:T(8,128)S(1)} %get-tuple-element.148) | copy-start | bytes 3145732
  690.1 65.2 %reduce-scatter.29.cloned.1.call-start = ((), (), s32[]{:S(2)}) async-start(), calls=%async_computation.29 | async-start | bytes 2621440 | tf_op jit(solution)/shard_map/reduce_scatter | solution.py:202
  690.2 15.0 %copy-start.218 = (bf16[1,1024,1024]{2,1,0:T(8,128)(2,1)S(1)}, bf16[1,1024,1024]{2,1,0:T(8,128)(2,1)}, u32[]{:S(2)}) copy-start(bf16[1,1024,1024]{2,1,0:T(8,128)(2,1)} %param.28) | copy-start | bytes 6291460
  708.9 128.7 %all-gather.26.cloned.1.call-start = ((), (), s32[]{:S(2)}) async-start(), calls=%async_computation.30 | async-start | bytes 2621440 | tf_op jit(solution)/shard_map/all_gather | solution.py:155
  718.7 47.9 %copy-start.193 = (f32[16,4,64]{2,1,0:T(4,128)S(1)}, f32[16,4,64]{2,1,0:T(4,128)}, u32[]{:S(2)}) copy-start(f32[16,4,64]{2,1,0:T(4,128)} %get-tuple-element.51) | copy-start | bytes 49156
  764.6 15.6 %collective-permute-start.3 = (bf16[1,256,1024]{2,1,0:T(8,128)(2,1)S(1)}, bf16[1,256,1024]{2,1,0:T(8,128)(2,1)S(1)}, u32[]{:S(2)}, u32[]{:S(2)}) collective-permute-start(bf16[1,256,1024]{2,1,0:T(8,128)(2,1)S(1)} %get-tuple-element.67), channel_id=1, source_target_pairs={{16,0},{17,1},{18,2},{19,3},{20,4},{21,5},{22,6},{23,7},{24,8},{25... | collective-permute-start | bytes 1572872 | tf_op jit(solution)/shard_map/ppermute | solution.py:20
  784.2 230.5 %reduce-scatter.35.cloned.1.call-start = ((), (), s32[]{:S(2)}) async-start(), calls=%async_computation.33 | async-start | bytes 5242880 | tf_op jit(solution)/shard_map/reduce_scatter | solution.py:276
  799.3 228.1 %reduce-scatter.49.cloned.1.call-start = ((), (), s32[]{:S(2)}) async-start(), calls=%async_computation.40 | async-start | bytes 20480
  805.5 18.5 %copy-start.19 = (f32[16,4,64,64]{2,3,1,0:T(8,128)S(1)}, f32[16,4,64,64]{2,3,1,0:T(8,128)}, u32[]{:S(2)}) copy-start(f32[16,4,64,64]{2,3,1,0:T(8,128)} %copy-done.18) | copy-start | bytes 3145732
  805.5 18.5 %copy-start.48 = (bf16[1,1024,256]{2,1,0:T(8,128)(2,1)S(1)}, bf16[1,1024,256]{2,1,0:T(8,128)(2,1)}, u32[]{:S(2)}) copy-start(bf16[1,1024,256]{2,1,0:T(8,128)(2,1)} %get-tuple-element.104) | copy-start | bytes 1572868
  815.0 13.8 %copy-start.152 = (bf16[1,1024,1024]{2,1,0:T(8,128)(2,1)S(1)}, bf16[1,1024,1024]{2,1,0:T(8,128)(2,1)}, u32[]{:S(2)}) copy-start(bf16[1,1024,1024]{2,1,0:T(8,128)(2,1)} %all-gather.12.cloned.1.call-done) | copy-start | bytes 6291460
  815.0 13.8 %copy-start.155 = (bf16[1,1024,1024]{2,1,0:T(8,128)(2,1)S(1)}, bf16[1,1024,1024]{2,1,0:T(8,128)(2,1)}, u32[]{:S(2)}) copy-start(bf16[1,1024,1024]{2,1,0:T(8,128)(2,1)} %all-gather.16.cloned.1.call-done) | copy-start | bytes 6291460
  815.0 13.8 %copy-start.158 = (bf16[1,1024,1024]{2,1,0:T(8,128)(2,1)S(1)}, bf16[1,1024,1024]{2,1,0:T(8,128)(2,1)}, u32[]{:S(2)}) copy-start(bf16[1,1024,1024]{2,1,0:T(8,128)(2,1)} %all-gather.20.cloned.1.call-done) | copy-start | bytes 6291460
  893.5 135.3 %reduce-scatter.43.cloned.1.call-start = ((), (), s32[]{:S(2)}) async-start(), calls=%async_computation.37 | async-start | bytes 655360 | tf_op jit(solution)/shard_map/reduce_scatter | solution.py:408
  907.4 123.0 %reduce-scatter.41.cloned.1.call-start = ((), (), s32[]{:S(2)}) async-start(), calls=%async_computation.36 | async-start | bytes 655360 | tf_op jit(solution)/shard_map/reduce_scatter | solution.py:405
  917.0 115.1 %reduce-scatter.39.cloned.1.call-start = ((), (), s32[]{:S(2)}) async-start(), calls=%async_computation.35 | async-start | bytes 655360 | tf_op jit(solution)/shard_map/reduce_scatter | solution.py:402
  931.0 102.8 %reduce-scatter.37.cloned.1.call-start = ((), (), s32[]{:S(2)}) async-start(), calls=%async_computation.34 | async-start | bytes 655360 | tf_op jit(solution)/shard_map/reduce_scatter | solution.py:399
  943.7 91.6 %reduce-scatter.33.cloned.1.call-start = ((), (), s32[]{:S(2)}) async-start(), calls=%async_computation.32 | async-start | bytes 2621440 | tf_op jit(solution)/shard_map/reduce_scatter | solution.py:202
  944.2 14.9 %copy-start.219 = (bf16[1,1024,1024]{2,1,0:T(8,128)(2,1)S(1)}, bf16[1,1024,1024]{2,1,0:T(8,128)(2,1)}, u32[]{:S(2)}) copy-start(bf16[1,1024,1024]{2,1,0:T(8,128)(2,1)} %param.28) | copy-start | bytes 6291460
  962.9 104.2 %reduce-scatter.31.cloned.1.call-start = ((), (), s32[]{:S(2)}) async-start(), calls=%async_computation.31 | async-start | bytes 2621440 | tf_op jit(solution)/shard_map/reduce_scatter | solution.py:199
  967.7 145.9 %reduce-scatter.47.cloned.1.call-start = ((), (), s32[]{:S(2)}) async-start(), calls=%async_computation.39 | async-start | bytes 2621440 | tf_op jit(solution)/shard_map/reduce_scatter | solution.py:417
  1004.6 154.6 %reduce-scatter.45.cloned.1.call-start = ((), (), s32[]{:S(2)}) async-start(), calls=%async_computation.38 | async-start | bytes 2621440 | tf_op jit(solution)/shard_map/reduce_scatter | solution.py:414
  1021.4 45.7 %copy-start.183 = (f32[1,1024]{1,0:T(1,128)S(1)}, f32[1,1024]{1,0:T(1,128)}, u32[]{:S(2)}) copy-start(f32[1,1024]{1,0:T(1,128)} %param.19) | copy-start | bytes 12292
  1021.5 45.6 %copy-start.185 = (f32[1,1024]{1,0:T(1,128)S(1)}, f32[1,1024]{1,0:T(1,128)}, u32[]{:S(2)}) copy-start(f32[1,1024]{1,0:T(1,128)} %param.21) | copy-start | bytes 12292
  1027.3 41.8 %copy-start.198 = (f32[1024]{0:T(1024)S(1)}, f32[1024]{0:T(1024)}, u32[]{:S(2)}) copy-start(f32[1024]{0:T(1024)} %get-tuple-element.45) | copy-start | bytes 12292
  1027.3 41.8 %copy-start.202 = (f32[1024]{0:T(1024)S(1)}, f32[1024]{0:T(1024)}, u32[]{:S(2)}) copy-start(f32[1024]{0:T(1024)} %get-tuple-element.46) | copy-start | bytes 12292
  1027.3 44.3 %copy-start.199 = (f32[1024]{0:T(1024)S(1)}, f32[1024]{0:T(1024)}, u32[]{:S(2)}) copy-start(f32[1024]{0:T(1024)} %get-tuple-element.15) | copy-start | bytes 12292
  1027.3 44.3 %copy-start.203 = (f32[1024]{0:T(1024)S(1)}, f32[1024]{0:T(1024)}, u32[]{:S(2)}) copy-start(f32[1024]{0:T(1024)} %get-tuple-element.17) | copy-start | bytes 12292
  1027.3 44.3 %copy-start.197 = (f32[1024]{0:T(1024)S(1)}, f32[1024]{0:T(1024)}, u32[]{:S(2)}) copy-start(f32[1024]{0:T(1024)} %get-tuple-element.50) | copy-start | bytes 12292
  1027.3 44.3 %copy-start.201 = (f32[1024]{0:T(1024)S(1)}, f32[1024]{0:T(1024)}, u32[]{:S(2)}) copy-start(f32[1024]{0:T(1024)} %get-tuple-element.49) | copy-start | bytes 12292
  1027.3 44.3 %copy-start.196 = (f32[1024]{0:T(1024)S(1)}, f32[1024]{0:T(1024)}, u32[]{:S(2)}) copy-start(f32[1024]{0:T(1024)} %get-tuple-element.28) | copy-start | bytes 12292
  1027.3 44.3 %copy-start.200 = (f32[1024]{0:T(1024)S(1)}, f32[1024]{0:T(1024)}, u32[]{:S(2)}) copy-start(f32[1024]{0:T(1024)} %get-tuple-element.30) | copy-start | bytes 12292
  1030.4 77.8 %copy-start.109 = (f32[1,1,1,256,1024]{4,3,2,1,0:T(8,128)S(1)}, f32[1,1,1,256,1024]{4,3,2,1,0:T(8,128)}, u32[]{:S(2)}) copy-start(f32[1,1,1,256,1024]{4,3,2,1,0:T(8,128)} %fusion.675) | copy-start | bytes 3145732
  (198 other events, 1059.2 us)
Sparse Core Ops, SparseCore 0:
  17.4 25.2 all-gather.11
  44.2 22.5 all-gather.13
  93.8 44.8 reduce-scatter.18
  158.3 23.5 all-gather.15
  184.0 22.5 all-gather.17
  238.4 44.8 reduce-scatter.20
  284.8 22.5 all-gather.9
  309.6 22.5 all-gather.19
  333.8 22.5 all-gather.21
  484.5 31.4 reduce-scatter.22
  518.7 31.3 reduce-scatter.24
  577.1 21.6 all-gather.23
  690.3 30.4 reduce-scatter.26
  723.9 31.3 reduce-scatter.28
  784.3 21.6 all-gather.25
  808.4 44.4 reduce-scatter.34
  893.6 17.9 reduce-scatter.48
  913.7 19.7 reduce-scatter.42
  935.8 19.9 reduce-scatter.40
  957.9 19.8 reduce-scatter.38
  980.1 19.9 reduce-scatter.36
  1002.6 29.7 reduce-scatter.32
  1035.6 31.4 reduce-scatter.30
  1069.2 44.3 reduce-scatter.46
  1116.0 43.2 reduce-scatter.44

commit v2 on v1

v2 whole, which is shorter than its diff:
```python
import functools
import math

import jax
import jax.numpy as jnp
import numpy as np
from jax import lax
from jax.experimental import pallas as pl
from jax.experimental.pallas import tpu as pltpu
from jax.sharding import PartitionSpec as P

ROT = 16
EPSILON = 1e-05
BLOCK = 256
CHUNK = 128
BF = jnp.bfloat16
F32 = jnp.float32
VMEM_BYTES = 60 * 1024 * 1024
ANY = pl.BlockSpec(memory_space=pl.ANY)
SMEM = pl.BlockSpec(memory_space=pltpu.SMEM)
VMEM = pl.BlockSpec(memory_space=pltpu.VMEM)


def host_tables(slot_rows, head_count, head_size):
    width = head_count * head_size
    halfway = ROT // 2
    column = np.arange(width) % head_size
    pair = np.where(column < halfway, column, column - halfway)
    inverse = np.exp(pair * (-2.0 * math.log(10000.0) / ROT))
    angles = np.arange(slot_rows)[:, None] * inverse[None, :]
    turned = (column < 2 * halfway)[None, :]
    cos_full = np.where(turned, np.cos(angles), 1.0)
    sin_full = np.where(turned, np.sin(angles), 0.0)
    order = np.arange(head_size)
    table = np.cos(np.pi * (order[None, :] + 0.5) * order[:, None] / head_size) * np.sqrt(2.0 / head_size)
    table = np.where(order[:, None] == 0, table * np.sqrt(0.5), table)
    partner = np.zeros((head_size, head_size))
    for i in range(halfway):
        partner[i + halfway, i] = -1.0
        partner[i, i + halfway] = 1.0
    eye = np.eye(head_count)
    dct = np.concatenate([np.kron(eye, table.T), np.kron(eye, partner @ table.T)], axis=0)
    high = dct.astype(np.float32).astype(BF)
    low = (dct - high.astype(np.float64)).astype(np.float32).astype(BF)
    lane_head = np.arange(width) // head_size
    heads = (np.arange(head_count)[:, None] == lane_head[None, :]).astype(np.float32)
    stacked = np.repeat(heads, CHUNK, axis=0)
    same = (lane_head[:, None] == lane_head[None, :]).astype(np.float32)
    return {
        "cos": cos_full.astype(np.float32),
        "sin": sin_full.astype(np.float32),
        "dct": np.stack([high, low]),
        "heads": stacked.astype(BF),
        "same": same.astype(np.float32),
    }


def dot(a, b):
    return jnp.dot(a, b, preferred_element_type=F32)


def dot_nt(a, b):
    return lax.dot_general(a, b, (((1,), (1,)), ((), ())), preferred_element_type=F32)


def dot_tn(a, b):
    return lax.dot_general(a, b, (((0,), (0,)), ((), ())), preferred_element_type=F32)


def split(x):
    high = x.astype(BF)
    return high, (x - high.astype(F32)).astype(BF)


def stack_heads(x, heads, head_count):
    return jnp.concatenate([x] * head_count, axis=0) * heads


def lanes_of_heads(x, head_count):
    rows = x.shape[0] // head_count
    return jnp.concatenate([x[h * rows:(h + 1) * rows] for h in range(head_count)], axis=1)


def gelu_parts(u):
    z = jnp.abs(u) * (1.0 / math.sqrt(2.0))
    t = 1.0 / (1.0 + 0.3275911 * z)
    e = jnp.exp(-0.5 * u * u)
    poly = t * (0.5 * 0.254829592 + t * (0.5 * -0.284496736 + t * (0.5 * 1.421413741 + t * (0.5 * -1.453152027 + t * (0.5 * 1.061405429)))))
    tail = poly * e
    cdf = jnp.where(u >= 0, 1.0 - tail, tail)
    return u * cdf, cdf + u * e * (1.0 / math.sqrt(2.0 * math.pi))


class Copies:
    def __init__(self, sems):
        self.sems = sems
        self.used = 0
        self.open = []

    def start(self, src, dst):
        copy = pltpu.make_async_copy(src, dst, self.sems.at[self.used])
        self.used += 1
        copy.start()
        return copy

    def out(self, src, dst):
        self.open.append(self.start(src, dst))

    def finish(self):
        for copy in self.open:
            copy.wait()


def forward_kernel(cfg, info, *refs):
    (wq, wk, wv, wo, wup, wdown, norms, scales, cos, sin, dct, heads, same) = refs[cfg["pieces"]:cfg["pieces"] + 13]
    h_in = refs[:cfg["pieces"]]
    refs = refs[cfg["pieces"] + 13 + cfg["alias"]:]
    (s_n1, s_n2, s_am, s_gp, s_qf, s_kf, s_v, s_mf, s_inv, s_st, s_kt, s_h, part) = refs[:13]
    (v_h, v_wqkv, v_wo, v_wup, v_wdown, v_norms, v_scales, v_cos, v_sin, v_dct, v_heads, v_same,
     o_n1, o_n2, o_am, o_gp, o_qf, o_kf, o_v, o_mf, o_inv, o_st, o_kt, o_part, state, total, sems, o_sems) = refs[13:]
    m = cfg["m"]
    rows = v_h.shape[0]
    e = v_wqkv.shape[1] // 3
    f = v_wup.shape[1]
    hc = cfg["heads"]
    blocks = rows // BLOCK
    count = BLOCK // CHUNK
    me = info[1]

    def outs(b):
        rb = pl.ds(pl.multiple_of(b * BLOCK, BLOCK), BLOCK)
        at = b ^ me
        pairs = [(o.at[rb], s.at[rb]) for o, s in (
            (o_n1, s_n1), (o_n2, s_n2), (o_am, s_am), (o_gp, s_gp), (o_qf, s_qf), (o_kf, s_kf), (o_v, s_v), (o_mf, s_mf), (o_inv, s_inv))]
        pairs.append((o_st.at[pl.ds(b * count, count)], s_st.at[pl.ds(b * count, count)]))
        pairs.append((o_kt.at[pl.ds(b * count, count)], s_kt.at[pl.ds(b * count, count)]))
        pairs.append((o_part.at[b], part.at[at & 1, at >> 1]))
        return [pltpu.make_async_copy(src, dst, o_sems.at[i, b]) for i, (src, dst) in enumerate(pairs)]

    @pl.when(info[0] == cfg["section"])
    def _():
        io = Copies(sems)
        if cfg["pieces"] == 1:
            h_copies = [io.start(h_in[0].at[m, 0], v_h)]
        else:
            h_copies = [io.start(h_in[k], v_h.at[pl.ds((me ^ k) * BLOCK, BLOCK)]) for k in range(cfg["pieces"])]
        h_copies += [io.start(norms, v_norms), io.start(scales, v_scales)]
        loads = [io.start(w.at[0], v_wqkv.at[:, pl.ds(i * e, e)]) for i, w in enumerate((wq, wk, wv))]
        loads += [io.start(cos, v_cos), io.start(sin, v_sin), io.start(dct, v_dct), io.start(heads, v_heads), io.start(same, v_same)]
        loads += [io.start(wup.at[0], v_wup)]
        loads += [io.start(wo.at[0], v_wo), io.start(wdown.at[0], v_wdown)]
        state[...] = jnp.zeros_like(state)
        total[...] = jnp.zeros_like(total)
        for copy in h_copies:
            copy.wait()

        def normed(b):
            rb = pl.ds(pl.multiple_of(b * BLOCK, BLOCK), BLOCK)
            hidden = v_h[rb].astype(F32)
            center = hidden - jnp.mean(hidden, axis=-1, keepdims=True)
            spread = jnp.mean(center * center, axis=-1, keepdims=True)
            xhat = center * lax.rsqrt(spread + EPSILON)
            o_n1[rb] = (xhat * v_norms[0:1, :] + v_norms[1:2, :]).astype(BF)
            o_n2[rb] = (xhat * v_norms[2:3, :] + v_norms[3:4, :]).astype(BF)

        @pl.loop(0, blocks)
        def _(b):
            normed(b)

        for copy in loads:
            copy.wait()
        if cfg["pieces"] > 1:
            io.out(v_h, s_h)

        @pl.loop(0, blocks)
        def _(b):
            rb = pl.ds(pl.multiple_of(b * BLOCK, BLOCK), BLOCK)
            qkv = dot(o_n1[rb], v_wqkv[...])
            cos_b = v_cos[rb]
            sin_b = v_sin[rb]

            def lift(x):
                pair = jnp.concatenate([x * cos_b, x * sin_b], axis=1)
                high, low = split(pair)
                coeffs = dot(high, v_dct[0]) + dot(low, v_dct[0]) + dot(high, v_dct[1])
                return v_scales[0:1, :] * jnp.exp(coeffs)

            q_feat = lift(qkv[:, :e])
            slot = lax.broadcasted_iota(jnp.int32, (BLOCK, e), 0) + b * BLOCK
            k_feat = jnp.where(slot < info[2 + m], lift(qkv[:, e:2 * e]), 0.0)
            value = qkv[:, 2 * e:].astype(BF)
            o_qf[rb] = q_feat
            o_kf[rb] = k_feat
            o_v[rb] = value
            q_b = q_feat.astype(BF)
            k_b = k_feat.astype(BF)
            row = lax.broadcasted_iota(jnp.int32, (CHUNK, hc * CHUNK), 0)
            col = lax.broadcasted_iota(jnp.int32, (CHUNK, hc * CHUNK), 1) % CHUNK
            causal = row >= col
            for c in range(count):
                rc = slice(c * CHUNK, (c + 1) * CHUNK)
                at = b * count + c
                q_c, k_c, v_c = q_b[rc], k_b[rc], value[rc]
                o_st[at] = state[...]
                o_kt[at] = total[...]
                weighted = (q_c.astype(F32) * total[0:1, :]).astype(BF)
                scores = jnp.where(causal, dot_nt(q_c, stack_heads(k_c, v_heads[...], hc)), 0.0).astype(BF)
                both = dot(scores, jnp.concatenate([stack_heads(v_c, v_heads[...], hc), v_heads[...]], axis=1))
                inverse = 1.0 / (both[:, e:] + dot(weighted, v_same[...].astype(BF)))
                mixed = (both[:, :e] + dot(q_c, state[...].astype(BF))) * inverse
                rg = pl.ds(pl.multiple_of(b * BLOCK + c * CHUNK, CHUNK), CHUNK)
                o_inv[rg] = inverse
                o_mf[rg] = mixed
                o_am[rg, f:] = mixed.astype(BF)
                state[...] += dot_tn(k_c, v_c) * v_same[...]
                total[...] += jnp.sum(k_c.astype(F32), axis=0, keepdims=True)
            up = dot(o_n2[rb], v_wup[...])
            act, slope = gelu_parts(up)
            o_am[rb, :f] = act.astype(BF)
            o_gp[rb] = slope.astype(BF)
            branch = dot(o_am[rb, f:], v_wo[...]) + dot(o_am[rb, :f], v_wdown[...])
            o_part[b] = branch.astype(BF)
            for copy in outs(b):
                copy.start()

        io.finish()

        @pl.loop(0, blocks)
        def _(b):
            for copy in outs(b):
                copy.wait()


def backward_kernel(cfg, info, *refs):
    np_ = cfg["pieces"]
    g_in = refs[:np_]
    (h_in, wq, wk, wv, wo, wup, wdown, norms, scales, cos, sin, dct, heads, same,
     s_am, s_gp, s_qf, s_kf, s_v, s_mf, s_inv, s_st, s_kt) = refs[np_:np_ + 23]
    refs = refs[np_ + 23 + cfg["alias"]:]
    (s_gb, s_gup, s_gqkv, part, sums) = refs[:5]
    (v_g, v_h, v_wqkv, v_wo, v_wup, v_wdown, v_norms, v_scales, v_cos, v_sin, v_dct, v_heads, v_same,
     i_gp, i_qf, i_kf, i_v, i_mf, i_inv, i_st, i_kt,
     o_gup, o_gqkv, o_part, o_sums, acc, acc_s, state, total, sems, o_sems) = refs[5:]
    m = cfg["m"]
    rows = v_h.shape[0]
    e = v_wqkv.shape[1] // 3
    hc = cfg["heads"]
    hd = e // hc
    d = v_h.shape[1]
    blocks = rows // BLOCK
    count = BLOCK // CHUNK
    me = info[1]

    def outs(b):
        rb = pl.ds(pl.multiple_of(b * BLOCK, BLOCK), BLOCK)
        at = b ^ me
        pairs = [(o_gup.at[rb], s_gup.at[rb]), (o_gqkv.at[rb], s_gqkv.at[rb]), (o_part.at[b], part.at[at & 1, at >> 1])]
        return [pltpu.make_async_copy(src, dst, o_sems.at[i, b]) for i, (src, dst) in enumerate(pairs)]

    @pl.when(info[0] == cfg["section"])
    def _():
        io = Copies(sems)
        if np_ == 1:
            loads = [io.start(g_in[0].at[m, 0], v_g)]
        else:
            loads = [io.start(g_in[k], v_g.at[pl.ds((me ^ k) * BLOCK, BLOCK)]) for k in range(np_)]
        h_src = h_in.at[m, 0] if cfg["h_rank"] == 4 else h_in
        loads += [io.start(wo.at[0], v_wo), io.start(wdown.at[0], v_wdown)]
        loads += [io.start(s_gp, i_gp)]
        loads += [io.start(s_mf, i_mf), io.start(s_inv, i_inv), io.start(heads, v_heads), io.start(same, v_same),
                 io.start(s_qf, i_qf), io.start(s_kf, i_kf), io.start(s_v, i_v), io.start(s_st, i_st), io.start(s_kt, i_kt)]
        loads += [io.start(cos, v_cos), io.start(sin, v_sin), io.start(dct, v_dct)]
        loads += [io.start(w.at[0], v_wqkv.at[:, pl.ds(i * e, e)]) for i, w in enumerate((wq, wk, wv))]
        loads += [io.start(wup.at[0], v_wup)]
        loads += [io.start(h_src, v_h), io.start(norms, v_norms), io.start(scales, v_scales)]
        state[...] = jnp.zeros_like(state)
        total[...] = jnp.zeros_like(total)
        acc[...] = jnp.zeros_like(acc)
        acc_s[...] = jnp.zeros_like(acc_s)
        for copy in loads:
            copy.wait()
        io.out(v_g, s_gb)

        def fold(x):
            return jnp.sum(x.reshape(x.shape[0] // 8, 8, x.shape[1]), axis=0)

        @pl.loop(0, blocks)
        def _(step):
            b = blocks - 1 - step
            rb = pl.ds(pl.multiple_of(b * BLOCK, BLOCK), BLOCK)
            g_b = v_g[rb]
            g_act = dot_nt(g_b, v_wdown[...])
            g_up = (g_act * i_gp[rb].astype(F32)).astype(BF)
            o_gup[rb] = g_up
            g_mixed = dot_nt(g_b, v_wo[...]).astype(BF).astype(F32)
            inverse = i_inv[rb]
            g_num = (g_mixed * inverse).astype(BF)
            high, low = split(g_num.astype(F32) * i_mf[rb])
            same_b = v_same[...].astype(BF)
            g_den = -(dot(high, same_b) + dot(low, same_b))
            gd_high, gd_low = split(g_den)
            q_feat = i_qf[rb]
            k_feat = i_kf[rb]
            value = i_v[rb]
            q_b = q_feat.astype(BF)
            k_b = k_feat.astype(BF)
            row = lax.broadcasted_iota(jnp.int32, (CHUNK, hc * CHUNK), 0)
            col = lax.broadcasted_iota(jnp.int32, (CHUNK, hc * CHUNK), 1) % CHUNK
            causal = row >= col
            row_t = lax.broadcasted_iota(jnp.int32, (hc * CHUNK, CHUNK), 0) % CHUNK
            col_t = lax.broadcasted_iota(jnp.int32, (hc * CHUNK, CHUNK), 1)
            causal_t = col_t >= row_t
            hm = v_heads[...]
            sel = hm * jnp.asarray(1.0 / hd, BF)
            gq_parts, gk_parts, gv_parts = [None] * count, [None] * count, [None] * count
            for c in reversed(range(count)):
                rc = slice(c * CHUNK, (c + 1) * CHUNK)
                at = b * count + c
                q_c, k_c, v_c, n_c, dh, dl = q_b[rc], k_b[rc], value[rc], g_num[rc], gd_high[rc], gd_low[rc]
                k_x = stack_heads(k_c, hm, hc)
                v_x = jnp.concatenate([stack_heads(v_c, hm, hc), sel, sel], axis=1)
                g_x = jnp.concatenate([n_c, dh, dl], axis=1)
                grid = jnp.where(causal, dot_nt(g_x, v_x), 0.0).astype(BF)
                grid_t = jnp.where(causal_t, dot_nt(v_x, g_x), 0.0).astype(BF)
                scores_t = jnp.where(causal_t, dot_nt(k_x, q_c), 0.0).astype(BF)
                before = jnp.concatenate(split(i_st[at]), axis=1)
                gq_parts[c] = dot(grid, k_x) + dot_nt(jnp.concatenate([n_c, n_c], axis=1), before) + g_den[rc] * i_kt[at][0:1, :]
                after = jnp.concatenate(split(state[...]), axis=1)
                gk_parts[c] = dot(lanes_of_heads(grid_t, hc), stack_heads(q_c, hm, hc)) + dot_nt(jnp.concatenate([v_c, v_c], axis=1), after) + total[0:1, :]
                gv_parts[c] = dot(lanes_of_heads(scores_t, hc), stack_heads(n_c, hm, hc)) + dot(k_c, after[:, :e])
                state[...] += dot_tn(q_c, n_c) * v_same[...]
                total[...] += jnp.sum(q_c.astype(F32) * g_den[rc], axis=0, keepdims=True)
            gc_q = jnp.concatenate(gq_parts, axis=0) * q_feat
            gc_k = jnp.concatenate(gk_parts, axis=0) * k_feat
            g_value = jnp.concatenate(gv_parts, axis=0)
            acc_s[...] += fold(gc_q + gc_k)
            cos_b = v_cos[rb]
            sin_b = v_sin[rb]

            def lower(gc):
                high, low = split(gc)
                both = dot_nt(high, v_dct[0]) + dot_nt(low, v_dct[0]) + dot_nt(high, v_dct[1])
                return cos_b * both[:, :e] + sin_b * both[:, e:]

            gqkv = jnp.concatenate([lower(gc_q), lower(gc_k), g_value], axis=1).astype(BF)
            o_gqkv[rb] = gqkv
            g_one = dot_nt(gqkv, v_wqkv[...])
            g_two = dot_nt(o_gup[rb], v_wup[...])
            hidden = v_h[rb].astype(F32)
            center = hidden - jnp.mean(hidden, axis=-1, keepdims=True)
            spread = jnp.mean(center * center, axis=-1, keepdims=True)
            rstd = lax.rsqrt(spread + EPSILON)
            xhat = center * rstd
            acc[0] += fold(g_one * xhat)
            acc[1] += fold(g_one)
            acc[2] += fold(g_two * xhat)
            acc[3] += fold(g_two)
            acc[4] += fold(v_g[rb].astype(F32))
            inner = g_one * v_norms[0:1, :] + g_two * v_norms[2:3, :]
            mean_t = jnp.mean(inner, axis=-1, keepdims=True)
            mean_x = jnp.mean(inner * xhat, axis=-1, keepdims=True)
            g_h = rstd * (inner - mean_t - xhat * mean_x)
            o_part[b] = g_h.astype(BF)
            for copy in outs(b):
                copy.start()

        for i in range(5):
            o_sums[i:i + 1, :] = jnp.sum(acc[i], axis=0, keepdims=True)
        o_sums[5:8, :] = jnp.zeros((3, d), F32)
        o_sums[5:6, :e] = jnp.sum(acc_s[...], axis=0, keepdims=True) / v_scales[0:1, :]
        io.out(o_sums, sums)
        io.finish()

        @pl.loop(0, blocks)
        def _(b):
            for copy in outs(b):
                copy.wait()


def like(shape, dtype):
    return jax.ShapeDtypeStruct(shape, dtype)


def forward_call(sizes, m, section, info, h_pieces, weights, tabs, store):
    rows, d, e, f, hc = sizes
    pieces = len(h_pieces)
    chunks = rows // CHUNK
    blocks = rows // BLOCK
    shapes = [
        like((rows, d), BF), like((rows, d), BF), like((rows, f + e), BF), like((rows, f), BF),
        like((rows, e), F32), like((rows, e), F32), like((rows, e), BF), like((rows, e), F32),
        like((rows, e), F32), like((chunks, e, e), F32), like((chunks, 8, e), F32), like((rows, d), BF),
    ]
    out_shapes = shapes + [like((2, 2, BLOCK, d), BF)]
    alias = len(store)
    operands = [info, *h_pieces, *weights, *tabs, *store]
    scratch = [
        pltpu.VMEM((rows, d), BF), pltpu.VMEM((d, 3 * e), BF), pltpu.VMEM((e, d), BF), pltpu.VMEM((d, f), BF), pltpu.VMEM((f, d), BF),
        pltpu.VMEM((8, d), F32), pltpu.VMEM((8, e), F32), pltpu.VMEM((rows, e), F32), pltpu.VMEM((rows, e), F32),
        pltpu.VMEM((2, 2 * e, e), BF), pltpu.VMEM((hc * CHUNK, e), BF), pltpu.VMEM((e, e), F32),
        pltpu.VMEM((rows, d), BF), pltpu.VMEM((rows, d), BF), pltpu.VMEM((rows, f + e), BF), pltpu.VMEM((rows, f), BF),
        pltpu.VMEM((rows, e), F32), pltpu.VMEM((rows, e), F32), pltpu.VMEM((rows, e), BF), pltpu.VMEM((rows, e), F32),
        pltpu.VMEM((rows, e), F32), pltpu.VMEM((chunks, e, e), F32), pltpu.VMEM((chunks, 8, e), F32), pltpu.VMEM((blocks, BLOCK, d), BF),
        pltpu.VMEM((e, e), F32), pltpu.VMEM((8, e), F32), pltpu.SemaphoreType.DMA((32,)), pltpu.SemaphoreType.DMA((12, blocks)),
    ]
    cfg = {"m": m, "section": section, "pieces": pieces, "heads": hc, "alias": alias}
    first = len(operands) - alias
    results = pl.pallas_call(
        functools.partial(forward_kernel, cfg),
        out_shape=out_shapes,
        in_specs=[SMEM] + [ANY] * (len(operands) - 1),
        out_specs=[ANY] * len(out_shapes),
        scratch_shapes=scratch,
        input_output_aliases={first + i: i for i in range(alias)},
        compiler_params=pltpu.CompilerParams(vmem_limit_bytes=VMEM_BYTES),
        cost_estimate=pl.CostEstimate(flops=2 * rows * d * (4 * e + 2 * f), bytes_accessed=25 * 2 ** 20, transcendentals=rows * (f + 2 * e)),
        name="forward",
    )(*operands)
    return list(results[:12]), results[12]


def backward_call(sizes, m, section, info, g_pieces, h_in, weights, tabs, store, back):
    rows, d, e, f, hc = sizes
    s_n1, s_n2, s_am, s_gp, s_qf, s_kf, s_v, s_mf, s_inv, s_st, s_kt, s_h = store
    pieces = len(g_pieces)
    chunks = rows // CHUNK
    blocks = rows // BLOCK
    shapes = [like((rows, d), BF), like((rows, f), BF), like((rows, 3 * e), BF)]
    out_shapes = shapes + [like((2, 2, BLOCK, d), BF), like((8, d), F32)]
    alias = len(back)
    operands = [info, *g_pieces, h_in, *weights, *tabs, s_am, s_gp, s_qf, s_kf, s_v, s_mf, s_inv, s_st, s_kt, *back]
    scratch = [
        pltpu.VMEM((rows, d), BF), pltpu.VMEM((rows, d), BF),
        pltpu.VMEM((d, 3 * e), BF), pltpu.VMEM((e, d), BF), pltpu.VMEM((d, f), BF), pltpu.VMEM((f, d), BF),
        pltpu.VMEM((8, d), F32), pltpu.VMEM((8, e), F32), pltpu.VMEM((rows, e), F32), pltpu.VMEM((rows, e), F32),
        pltpu.VMEM((2, 2 * e, e), BF), pltpu.VMEM((hc * CHUNK, e), BF), pltpu.VMEM((e, e), F32),
        pltpu.VMEM((rows, f), BF), pltpu.VMEM((rows, e), F32), pltpu.VMEM((rows, e), F32), pltpu.VMEM((rows, e), BF),
        pltpu.VMEM((rows, e), F32), pltpu.VMEM((rows, e), F32), pltpu.VMEM((chunks, e, e), F32), pltpu.VMEM((chunks, 8, e), F32),
        pltpu.VMEM((rows, f), BF), pltpu.VMEM((rows, 3 * e), BF), pltpu.VMEM((blocks, BLOCK, d), BF), pltpu.VMEM((8, d), F32),
        pltpu.VMEM((5, 8, d), F32), pltpu.VMEM((8, e), F32), pltpu.VMEM((e, e), F32), pltpu.VMEM((8, e), F32), pltpu.SemaphoreType.DMA((40,)), pltpu.SemaphoreType.DMA((3, blocks)),
    ]
    cfg = {"m": m, "section": section, "pieces": pieces, "heads": hc, "alias": alias, "h_rank": h_in.ndim}
    first = len(operands) - alias
    to = [0, 1, 2, 4]
    results = pl.pallas_call(
        functools.partial(backward_kernel, cfg),
        out_shape=out_shapes,
        in_specs=[SMEM] + [ANY] * (len(operands) - 1),
        out_specs=[ANY] * len(out_shapes),
        scratch_shapes=scratch,
        input_output_aliases={first + i: to[i] for i in range(alias)},
        compiler_params=pltpu.CompilerParams(vmem_limit_bytes=VMEM_BYTES),
        cost_estimate=pl.CostEstimate(flops=2 * rows * d * (4 * e + 2 * f), bytes_accessed=30 * 2 ** 20, transcendentals=0),
        name="backward",
    )(*operands)
    return [results[0], results[1], results[2], results[4]], results[3]


def body(tokens, cotangent, lengths, attn_gain, attn_bias, ffn_gain, ffn_bias, w_query, w_key, w_value, w_out, feat_scale, w_up, w_down, down_bias):
    section = lax.axis_index("section")
    tensor = lax.axis_index("tensor")
    teams = lax.axis_size("tensor")
    micro, _, rows, d = tokens.shape
    hc, hd = feat_scale.shape[1:]
    e = hc * hd
    f = w_up.shape[2]
    sizes = (rows, d, e, f, hc)
    share = rows // teams
    is_first = section == 0
    info = jnp.concatenate([jnp.stack([section, tensor]).astype(jnp.int32), lengths[:, 0]])
    norms = jnp.concatenate([attn_gain, attn_bias, ffn_gain, ffn_bias, jnp.zeros((4, d), F32)], axis=0)
    scales = jnp.broadcast_to(feat_scale.reshape(1, e), (8, e))
    made = host_tables(rows, hc, hd)
    tabs = [norms, scales] + [jnp.asarray(made[k]) for k in ("cos", "sin", "dct", "heads", "same")]
    weights = [w_query, w_key, w_value, w_out, w_up, w_down]
    both = ("section", "tensor")

    def swap(x, sec, bit):
        return lax.ppermute(x, both, [(sec * teams + i, sec * teams + (i ^ bit)) for i in range(teams)])

    def hand(x, source):
        return lax.ppermute(x, "section", [(source, 1 - source)])

    def reduce_rows(part, sec):
        near = part[0].astype(F32) + swap(part[1], sec, 1).astype(F32)
        return near[0] + swap(near[1].astype(BF), sec, 2).astype(F32)

    def gather_rows(own, sec):
        far = swap(own, sec, 2)
        return [own, swap(own, sec, 1), far, swap(far, sec, 1)]

    def own_rows(x, m):
        return lax.dynamic_slice(x[m, 0], (tensor * share, 0), (share, d)).astype(F32)

    stores, hidden = [], []
    for m in range(micro):
        store, part = forward_call(sizes, m, 0, info, [tokens], weights, tabs, [])
        stores.append(store)
        out = own_rows(tokens, m) + reduce_rows(part, 0) + down_bias[0]
        hidden.append(gather_rows(hand(out.astype(BF), 0), 1))
    tops, backs, grads = [], [], []
    for m in range(micro):
        stores[m], part = forward_call(sizes, m, 1, info, hidden[m], weights, tabs, stores[m])
        tops.append(hidden[m][0].astype(F32) + reduce_rows(part, 1) + down_bias[0])
        back, part = backward_call(sizes, m, 1, info, [cotangent], stores[m][11], weights, tabs, stores[m], [])
        backs.append(back)
        grad = own_rows(cotangent, m) + reduce_rows(part, 1)
        grads.append(gather_rows(hand(grad.astype(BF), 1), 0))
    bottoms = []
    for m in range(micro):
        backs[m], part = backward_call(sizes, m, 0, info, grads[m], tokens, weights, tabs, stores[m], backs[m])
        bottoms.append(grads[m][0].astype(F32) + reduce_rows(part, 0))
    ends = jnp.stack([jnp.where(is_first, bottoms[m], tops[m]) for m in range(micro)])[None, :, None]

    def weight_grad(lefts, rights):
        total = sum(dot_tn(left, right) for left, right in zip(lefts, rights))
        return lax.psum_scatter(total.astype(BF), "dp", scatter_dimension=0, tiled=True).astype(F32)

    gb = [back[0] for back in backs]
    down = weight_grad(gb, [store[2] for store in stores]).T
    up = weight_grad([store[1] for store in stores], [back[1] for back in backs])
    qkv = weight_grad([store[0] for store in stores], [back[2] for back in backs])
    small = sum(back[3] for back in backs)
    rows_small = lax.psum(lax.psum(small[:5], "tensor"), "dp")
    scale_small = lax.psum(small[5, :e], "dp").reshape(hc, hd)
    group = lax.axis_size("dp")
    place = lax.axis_index("dp")
    cut = lax.dynamic_slice(rows_small, (0, place * (d // group)), (5, d // group))
    scale_cut = lax.dynamic_slice(scale_small, (0, place * (hd // group)), (hc, hd // group))
    return (
        ends, cut[0:1], cut[1:2], cut[2:3], cut[3:4],
        qkv[None, :, :e], qkv[None, :, e:2 * e], qkv[None, :, 2 * e:], down[None, f:], scale_cut[None], up[None], down[None, :f],
        cut[4:5] / teams,
    )


def solution(mesh):
    return jax.shard_map(
        body,
        mesh=mesh,
        in_specs=(
            P(None, "dp", None, None), P(None, "dp", None, None), P(None, "dp"),
            P("section", None), P("section", None), P("section", None), P("section", None),
            P("section", None, "tensor"), P("section", None, "tensor"), P("section", None, "tensor"),
            P("section", "tensor", None), P("section", "tensor", None), P("section", None, "tensor"),
            P("section", "tensor", None), P("section", None),
        ),
        out_specs=(
            P("section", None, "dp", "tensor", None),
            P("section", "dp"), P("section", "dp"), P("section", "dp"), P("section", "dp"),
            P("section", "dp", "tensor"), P("section", "dp", "tensor"), P("section", "dp", "tensor"),
            P("section", "tensor", "dp"), P("section", "tensor", "dp"), P("section", "dp", "tensor"),
            P("section", "tensor", "dp"), P("section", "dp"),
        ),
        check_vma=False,
    )
```

time: 1180 us -> 615 us (0.52)
  matrix products: 505 us -> 23.7 us
  other arithmetic: 162 us -> 21.1 us
  Pallas kernels: 0 us -> 109 us
  waiting for transfers between devices: 365 us -> 307 us
  starting transfers between devices: 11.5 us -> 55.2 us
  local copies, waits for them, and re-layouts: 75.4 us -> 33.1 us
    dot_general x144 -> x6, matrix products: 505 us -> 23.7 us  [dot_tn(): lax.dot_general(a, b, (((0,), (0,)), ((), ())), preferred_element_type=F32)]
    ppermute x4 -> x32, waiting for transfers between devices: 48.9 us -> 253 us  [the longest x4 215 us: hand(): return lax.ppermute(x, 'section', [(source, 1 - source)])]
    reduce_scatter x15 -> x3, waiting for transfers between devices: 242 us -> 54.4 us  [weight_grad(): lax.psum_scatter(total.astype(BF), 'dp', scatter_dimension=0, tiled=True)]
    pallas_call x0 -> x8, Pallas kernels: none -> 109 us  [the longest x4 60.4 us: backward_call(): pl.pallas_call(functools.partial(backward_kernel, cfg), out_shape=out_sha...]
    all_gather x9 -> x0, waiting for transfers between devices: 71.4 us -> none  [the longest x3 68 us: body(): lax.all_gather(forward_norm_one, 'tensor', axis=1, tiled=True)]
    another operation x41 -> x2, other arithmetic: 68.9 us -> 6.02 us  [body(): jnp.stack([jnp.where(is_first, bottoms[m], tops[m]) for m in range(micro)])]
    ppermute x4 -> x32, starting transfers between devices: 9.36 us -> 54.8 us  [the longest x28 49.6 us: swap(): lax.ppermute(x, both, [(sec * teams + i, sec * teams + (i ^ bit)) for i i...]
    convert_element_type x16 -> x4, other arithmetic: 46.6 us -> 2.85 us  [the longest x2 1.56 us: body(): grads.append(gather_rows(hand(grad.astype(BF), 1), 0))]
  transfers between devices with their start and end apart: 29 -> 35, of which waited for: 17 -> 12; matrix products, arithmetic and copies ran while one was open for 47% -> 7% of each run, Pallas kernels for 0% -> 9%
where the time goes in v2:
time: 615 us; the launch traced here: 607 us
  waiting for transfers between devices  307 us (50%)
  Pallas kernels  109 us (18%)
  starting transfers between devices  55.2 us (9%)
  blocking collectives  41.8 us (7%)
  local copies, waits for them, and re-layouts  33.1 us (5%)
  matrix products  23.7 us (4%)
  other arithmetic  21.1 us (3%)
  between operations  15.3 us (2%)
    ppermute x4, waiting for transfers between devices, hand(): return lax.ppermute(x, 'section', [(source, 1 - source)])  215 us
    pallas_call x4, Pallas kernels, backward_call(): pl.pallas_call(functools.partial(backward_kernel, cfg), out_shape=out_sha...  60.4 us
    reduce_scatter x3, waiting for transfers between devices, weight_grad(): lax.psum_scatter(total.astype(BF), 'dp', scatter_dimension=0, tiled=True)  54.4 us
    ppermute x28, starting transfers between devices, swap(): lax.ppermute(x, both, [(sec * teams + i, sec * teams + (i ^ bit)) for i i...  49.6 us
    pallas_call x4, Pallas kernels, forward_call(): pl.pallas_call(functools.partial(forward_kernel, cfg), out_shape=out_shap...  48.8 us
    psum x2, blocking collectives, body(): rows_small = lax.psum(lax.psum(small[:5], 'tensor'), 'dp')  41.8 us
    ppermute x28, waiting for transfers between devices, swap(): lax.ppermute(x, both, [(sec * teams + i, sec * teams + (i ^ bit)) for i i...  37.2 us
    dot_general x6, matrix products, dot_tn(): lax.dot_general(a, b, (((0,), (0,)), ((), ())), preferred_element_type=F32)  23.7 us
  transfers between devices with their start and end apart: 35, of which 12 were waited for; matrix products, arithmetic and copies ran while one was open for 7% of the time, Pallas kernels for 9%

profile of v2, /device:TPU:0, one launch (start us, length us, event | category | flops | bytes accessed | tf_op | source)
XLA Modules:
  0.0 606.6 jit_solution(726899358115857678)
XLA Ops:
  9.2 1.4 concatenate.7.refs_7_.refs_10_.refs_8_.refs_11_
  11.2 23.0 %forward.4 = (bf16[1024,1024]{1,0:T(8,128)(2,1)}, bf16[1024,1024]{1,0:T(8,128)(2,1)}, bf16[1024,1280]{1,0:T(8,128)(2,1)}, bf16[1024,1024]{1,0:T(8,128)(2,1)}, f3...) custom-call(s32[4]{0:T(128)} %pad_add_fusion.info, ...), custom_call_target="tpu_custom_call" | custom-call | flops 6442450944 | bytes 26214400 | tf_op jit(solution)/shard_map/forward/pallas_call | solution.py:408
  34.2 1.4 slice_bitcast_fusion.16
  35.7 2.4 collective-permute-start
  38.1 2.3 collective-permute-done
  40.8 4.8 collective-permute-start.1
  45.6 4.1 fusion.37
  49.7 8.1 %collective-permute-done.1 = bf16[256,1024]{1,0:T(8,128)(2,1)S(1)} collective-permute-done((bf16[256,1024]{1,0:T(8,128)(2,1)S(1)}, bf16[256,1024]{1,0:T(8,128)(2,1)S(1)}, u32[]{:S(2)}, u32[]{:S(2)}) %collective-permute-start.1) | collective-permute-done | bytes 524320 | tf_op jit(solution)/shard_map/ppermute | solution.py:479
  58.1 1.3 collective-permute-start.2
  59.4 11.2 %collective-permute-done.2.refs_0_ = bf16[256,1024]{1,0:T(8,128)(2,1)S(1)} collective-permute-done((bf16[256,1024]{1,0:T(8,128)(2,1)S(1)}, bf16[256,1024]{1,0:T(8,128)(2,1)S(1)}, u32[]{:S(2)}, u32[]{:S(2)}) %collective-permute-start.2) | collective-permute-done | bytes 524320 | tf_op jit(solution)/shard_map/ppermute | solution.py:482
  73.8 1.4 forward.5
  75.2 1.4 backward.4
  76.6 1.4 slice_bitcast_fusion.15
  80.3 1.8 fusion.36
  83.7 96.0 %collective-permute-done.8.refs_0_ = bf16[256,1024]{1,0:T(8,128)(2,1)S(1)} collective-permute-done((bf16[256,1024]{1,0:T(8,128)(2,1)S(1)}, bf16[256,1024]{1,0:T(8,128)(2,1)S(1)}, u32[]{:S(2)}, u32[]{:S(2)}) %collective-permute-start.8) | collective-permute-done | bytes 524320 | tf_op jit(solution)/shard_map/ppermute | solution.py:482
  179.7 3.0 collective-permute-start.10
  182.7 23.0 %forward.6 = (bf16[1024,1024]{1,0:T(8,128)(2,1)}, bf16[1024,1024]{1,0:T(8,128)(2,1)}, bf16[1024,1280]{1,0:T(8,128)(2,1)}, bf16[1024,1024]{1,0:T(8,128)(2,1)}, f3...) custom-call(s32[4]{0:T(128)} %pad_add_fusion.info, ...), custom_call_target="tpu_custom_call" | custom-call | flops 6442450944 | bytes 26214400 | tf_op jit(solution)/shard_map/forward/pallas_call | solution.py:408
  205.8 2.1 collective-permute-start.9
  207.8 2.4 collective-permute-start.11
  211.6 1.9 collective-permute-start.16
  214.6 1.6 collective-permute-start.14
  217.2 28.8 %backward.5 = (bf16[1024,1024]{1,0:T(8,128)(2,1)}, bf16[1024,1024]{1,0:T(8,128)(2,1)}, bf16[1024,768]{1,0:T(8,128)(2,1)}, bf16[2,2,256,1024]{3,2,1,0:T(8,128)(2,1)}, f32[8,1024]{1,0:T(8,128)}) custom-call(s32[4]{0:T(128)} %pad_add_fusion.info, ...), custom_call_target="tpu_custom_call", output_to_operand_aliasing={{0}: (28, {}), {1}: (29, {}), {2}: (30, {}), {4}: (31, {})} | custom-call | flops 6442450944 | bytes 31457280 | tf_op jit(solution)/shard_map/backward/pallas_call | solution.py:445
  246.1 1.4 slice_bitcast_fusion.14
  247.5 2.5 collective-permute-start.12
  250.1 1.6 convert_add_fusion.3
  252.5 3.0 collective-permute-start.17
  255.5 1.6 convert_add_fusion.4
  258.1 1.6 collective-permute-start.15
  261.6 3.0 collective-permute-start.13
  264.6 5.0 collective-permute-done.17
  269.7 10.3 %collective-permute-done.13 = bf16[256,1024]{1,0:T(8,128)(2,1)} collective-permute-done((bf16[256,1024]{1,0:T(8,128)(2,1)}, bf16[256,1024]{1,0:T(8,128)(2,1)}, u32[]{:S(2)}, u32[]{:S(2)}) %collective-permute-start.13) | collective-permute-done | bytes 524320 | tf_op jit(solution)/shard_map/ppermute | solution.py:479
  280.0 3.9 fusion.18
  283.9 1.3 collective-permute-start.18
  285.2 10.8 %collective-permute-done.18.refs_0_ = bf16[256,1024]{1,0:T(8,128)(2,1)S(1)} collective-permute-done((bf16[256,1024]{1,0:T(8,128)(2,1)S(1)}, bf16[256,1024]{1,0:T(8,128)(2,1)S(1)}, u32[]{:S(2)}, u32[]{:S(2)}) %collective-permute-start.18) | collective-permute-done | bytes 524320 | tf_op jit(solution)/shard_map/ppermute | solution.py:482
  299.1 1.4 forward.7
  300.5 1.4 backward.6
  301.9 1.4 slice_bitcast_fusion.11
  305.3 1.3 fusion.9
  307.9 97.5 %collective-permute-done.24.refs_0_ = bf16[256,1024]{1,0:T(8,128)(2,1)S(1)} collective-permute-done((bf16[256,1024]{1,0:T(8,128)(2,1)S(1)}, bf16[256,1024]{1,0:T(8,128)(2,1)S(1)}, u32[]{:S(2)}, u32[]{:S(2)}) %collective-permute-start.24) | collective-permute-done | bytes 524320 | tf_op jit(solution)/shard_map/ppermute | solution.py:482
  405.4 2.9 collective-permute-start.26
  408.3 1.9 collective-permute-start.25
  410.3 9.6 %collective-permute-done.26.refs_2_ = bf16[256,1024]{1,0:T(8,128)(2,1)S(1)} collective-permute-done((bf16[256,1024]{1,0:T(8,128)(2,1)S(1)}, bf16[256,1024]{1,0:T(8,128)(2,1)S(1)}, u32[]{:S(2)}, u32[]{:S(2)}) %collective-permute-start.26) | collective-permute-done | bytes 524320 | tf_op jit(solution)/shard_map/ppermute | solution.py:479
  419.8 1.9 collective-permute-start.27
  421.8 1.9 collective-permute-done.27.refs_3_
  424.4 28.8 %backward.7 = (bf16[1024,1024]{1,0:T(8,128)(2,1)}, bf16[1024,1024]{1,0:T(8,128)(2,1)}, bf16[1024,768]{1,0:T(8,128)(2,1)}, bf16[2,2,256,1024]{3,2,1,0:T(8,128)(2,1)}, f32[8,1024]{1,0:T(8,128)}) custom-call(s32[4]{0:T(128)} %pad_add_fusion.info, ...), custom_call_target="tpu_custom_call", output_to_operand_aliasing={{0}: (28, {}), {1}: (29, {}), {2}: (30, {}), {4}: (31, {})} | custom-call | flops 6442450944 | bytes 31457280 | tf_op jit(solution)/shard_map/backward/pallas_call | solution.py:445
  453.3 3.5 fusion.38
  456.8 3.2 add_convert_fusion.2
  460.1 4.2 fusion.40
  464.3 3.9 add_convert_fusion.1
  468.6 4.7 fusion.39
  473.3 4.2 add_convert_fusion
  477.6 1.6 copy-done.18
  480.2 2.0 collective-permute-start.28
  483.6 1.6 collective-permute-start.31
  485.6 1.3 copy-done.3
  487.8 3.0 collective-permute-start.29
  491.0 20.2 %psum.21 = f32[5,1024]{1,0:T(8,128)S(1)} all-reduce(f32[5,1024]{1,0:T(8,128)S(1)} %bitcast.186), channel_id=1, replica_groups=mesh['section'=2,'dp'=4,'tensor'=4] {'tensor'}, use_global_device_ids=true, to_apply=%region_0.1 | all-reduce | flops 5120 | bytes 40960 | tf_op jit(solution)/shard_map/psum | solution.py:524
  511.2 21.5 %all-reduce = (f32[5,1024]{1,0:T(8,128)S(1)}, f32[4,64]{1,0:T(4,128)S(1)}) all-reduce(f32[5,1024]{1,0:T(8,128)S(1)} %psum.21, f32[4,64]{1,0:T(4,128)S(1)} %reshape.67), channel_id=1, replica_groups=mesh['section'=2,'dp'=4,'tensor'=4] {'dp'}, use_global_device_ids=true, to_apply=%region_1.2 | all-reduce | flops 5376 | bytes 43008 | tf_op jit(solution)/shard_map/psum | solution.py:524
  534.1 2.1 fusion.4
  536.2 1.5 maximum_bitcast_fusion
  539.6 3.5 reduce-scatter.8.cloned.1.call-done
  543.2 2.1 bitcast_convert_fusion
  545.3 50.9 %reduce-scatter.6.cloned.1.call-done = bf16[256,1280]{1,0:T(8,128)(2,1)} async-done(((bf16[1024,1280]{1,0:T(8,128)(2,1)}), bf16[256,1280]{1,0:T(8,128)(2,1)}) %reduce-scatter.6.cloned.1.call-update) | async-done | bytes 655376 | tf_op jit(solution)/shard_map/reduce_scatter | solution.py:517
  597.5 1.3 copy.67
  (169 shorter events, 33.9 us)
Async XLA Ops:
  7.2 530.5 %reduce-scatter.4.cloned.1.call-start = ((), (), s32[]{:S(2)}) async-start(), calls=%async_computation.3 | async-start | bytes 1966080 | tf_op jit(solution)/shard_map/reduce_scatter | solution.py:517
  34.2 6.1 %copy-start.25 = (bf16[2,2,256,1024]{3,2,1,0:T(8,128)(2,1)S(1)}, bf16[2,2,256,1024]{3,2,1,0:T(8,128)(2,1)}, u32[]{:S(2)}) copy-start(bf16[2,2,256,1024]{3,2,1,0:T(8,128)(2,1)} %get-tuple-element.85) | copy-start | bytes 6291460
  35.7 4.7 collective-permute-start
  40.8 17.0 %collective-permute-start.1 = (bf16[256,1024]{1,0:T(8,128)(2,1)S(1)}, bf16[256,1024]{1,0:T(8,128)(2,1)S(1)}, u32[]{:S(2)}, u32[]{:S(2)}) collective-permute-start(bf16[256,1024]{1,0:T(8,128)(2,1)S(1)} %fusion.28), channel_id=1, source_target_pairs={{0,2},{1,3},{2,0},{3,1},{4,6},{5,7},{6,4},{7,5},{8,10},{9,11},{10,... | collective-permute-start | bytes 1572872 | tf_op jit(solution)/shard_map/ppermute | solution.py:479
  45.6 12.2 %copy-start.46 = (f32[1,1024]{1,0:T(1,128)S(1)}, f32[1,1024]{1,0:T(1,128)}, u32[]{:S(2)}) copy-start(f32[1,1024]{1,0:T(1,128)} %param.34) | copy-start | bytes 12292
  58.1 12.5 %collective-permute-start.2 = (bf16[256,1024]{1,0:T(8,128)(2,1)S(1)}, bf16[256,1024]{1,0:T(8,128)(2,1)S(1)}, u32[]{:S(2)}, u32[]{:S(2)}) collective-permute-start(bf16[256,1024]{1,0:T(8,128)(2,1)S(1)} %fusion.27), channel_id=1, source_target_pairs={{0,16},{1,17},{2,18},{3,19},{4,20},{5,21},{6,22},{7,23},{8,24},{9,... | collective-permute-start | bytes 1572872 | tf_op jit(solution)/shard_map/ppermute | solution.py:482
  70.6 1.4 collective-permute-start.4
  71.3 1.4 collective-permute-start.3
  72.0 0.7 collective-permute-start.5
  78.1 0.9 collective-permute-start.6
  79.4 2.7 collective-permute-start.7
  82.4 97.3 %collective-permute-start.8 = (bf16[256,1024]{1,0:T(8,128)(2,1)S(1)}, bf16[256,1024]{1,0:T(8,128)(2,1)S(1)}, u32[]{:S(2)}, u32[]{:S(2)}) collective-permute-start(bf16[256,1024]{1,0:T(8,128)(2,1)S(1)} %fusion.23), channel_id=1, source_target_pairs={{16,0},{17,1},{18,2},{19,3},{20,4},{21,5},{22,6},{23,7},{24,8},{25... | collective-permute-start | bytes 1572872 | tf_op jit(solution)/shard_map/ppermute | solution.py:482
  179.7 26.0 %copy-start.13 = (bf16[256,1024]{1,0:T(8,128)(2,1)}, bf16[256,1024]{1,0:T(8,128)(2,1)S(1)}, u32[]{:S(2)}) copy-start(bf16[256,1024]{1,0:T(8,128)(2,1)S(1)} %collective-permute-done.8.refs_0_) | copy-start | bytes 1572868
  179.7 28.1 %collective-permute-start.10 = (bf16[256,1024]{1,0:T(8,128)(2,1)S(1)}, bf16[256,1024]{1,0:T(8,128)(2,1)S(1)}, u32[]{:S(2)}, u32[]{:S(2)}) collective-permute-start(bf16[256,1024]{1,0:T(8,128)(2,1)S(1)} %collective-permute-done.8.refs_0_), channel_id=1, source_target_pairs={{0,2},{1,3},{2,0},{3,1},{4,6},{5,7},{6,4},{7,5},{8,10},{9,11},{10,... | collective-permute-start | bytes 1572872 | tf_op jit(solution)/shard_map/ppermute | solution.py:479
  205.8 7.7 %copy-start.20 = (bf16[2,2,256,1024]{3,2,1,0:T(8,128)(2,1)S(1)}, bf16[2,2,256,1024]{3,2,1,0:T(8,128)(2,1)}, u32[]{:S(2)}) copy-start(bf16[2,2,256,1024]{3,2,1,0:T(8,128)(2,1)} %get-tuple-element.114) | copy-start | bytes 6291460
  205.8 10.5 %collective-permute-start.9 = (bf16[256,1024]{1,0:T(8,128)(2,1)S(1)}, bf16[256,1024]{1,0:T(8,128)(2,1)S(1)}, u32[]{:S(2)}, u32[]{:S(2)}) collective-permute-start(bf16[256,1024]{1,0:T(8,128)(2,1)S(1)} %collective-permute-done.8.refs_0_), channel_id=1, source_target_pairs={{0,1},{1,0},{2,3},{3,2},{4,5},{5,4},{6,7},{7,6},{8,9},{9,8},{10,11... | collective-permute-start | bytes 1572872 | tf_op jit(solution)/shard_map/ppermute | solution.py:479
  207.8 6.7 %copy-start.32 = (bf16[256,1024]{1,0:T(8,128)(2,1)}, bf16[256,1024]{1,0:T(8,128)(2,1)S(1)}, u32[]{:S(2)}) copy-start(bf16[256,1024]{1,0:T(8,128)(2,1)S(1)} %collective-permute-done.10.refs_2_) | copy-start | bytes 1572868
  207.8 8.4 %collective-permute-start.11 = (bf16[256,1024]{1,0:T(8,128)(2,1)S(1)}, bf16[256,1024]{1,0:T(8,128)(2,1)S(1)}, u32[]{:S(2)}, u32[]{:S(2)}) collective-permute-start(bf16[256,1024]{1,0:T(8,128)(2,1)S(1)} %collective-permute-done.10.refs_2_), channel_id=1, source_target_pairs={{0,1},{1,0},{2,3},{3,2},{4,5},{5,4},{6,7},{7,6},{8,9},{9,8},{10,11... | collective-permute-start | bytes 1572872 | tf_op jit(solution)/shard_map/ppermute | solution.py:479
  211.6 38.5 %collective-permute-start.16 = (bf16[2,256,1024]{2,1,0:T(8,128)(2,1)S(1)}, bf16[2,256,1024]{2,1,0:T(8,128)(2,1)}, u32[]{:S(2)}, u32[]{:S(2)}) collective-permute-start(bf16[2,256,1024]{2,1,0:T(8,128)(2,1)S(1)} %slice_bitcast_fusion.12), channel_id=1, source_target_pairs={{0,1},{1,0},{2,3},{3,2},{4,5},{5,4},{6,7},{7,6},{8,9},{9,8},{10,11... | collective-permute-start | bytes 3145736 | tf_op jit(solution)/shard_map/ppermute | solution.py:479
  214.6 40.9 %collective-permute-start.14 = (bf16[2,256,1024]{2,1,0:T(8,128)(2,1)}, bf16[2,256,1024]{2,1,0:T(8,128)(2,1)}, u32[]{:S(2)}, u32[]{:S(2)}) collective-permute-start(bf16[2,256,1024]{2,1,0:T(8,128)(2,1)} %slice_bitcast_fusion.13), channel_id=1, source_target_pairs={{16,17},{17,16},{18,19},{19,18},{20,21},{21,20},{22,23},{23,22},{2... | collective-permute-start | bytes 3145736 | tf_op jit(solution)/shard_map/ppermute | solution.py:479
  246.1 4.0 copy-start.23
  247.5 8.0 %copy-start.21 = (bf16[2,2,256,1024]{3,2,1,0:T(8,128)(2,1)S(1)}, bf16[2,2,256,1024]{3,2,1,0:T(8,128)(2,1)}, u32[]{:S(2)}) copy-start(bf16[2,2,256,1024]{3,2,1,0:T(8,128)(2,1)} %get-tuple-element.114) | copy-start | bytes 6291460
  247.5 12.2 %collective-permute-start.12 = (bf16[2,256,1024]{2,1,0:T(8,128)(2,1)S(1)}, bf16[2,256,1024]{2,1,0:T(8,128)(2,1)S(1)}, u32[]{:S(2)}, u32[]{:S(2)}) collective-permute-start(bf16[2,256,1024]{2,1,0:T(8,128)(2,1)S(1)} %slice_bitcast_fusion.14), channel_id=1, source_target_pairs={{0,1},{1,0},{2,3},{3,2},{4,5},{5,4},{6,7},{7,6},{8,9},{9,8},{10,11... | collective-permute-start | bytes 3145736 | tf_op jit(solution)/shard_map/ppermute | solution.py:479
  252.5 7.2 %copy-start.24 = (bf16[2,2,256,1024]{3,2,1,0:T(8,128)(2,1)S(1)}, bf16[2,2,256,1024]{3,2,1,0:T(8,128)(2,1)}, u32[]{:S(2)}) copy-start(bf16[2,2,256,1024]{3,2,1,0:T(8,128)(2,1)} %get-tuple-element.113) | copy-start | bytes 6291460
  252.5 17.1 %collective-permute-start.17 = (bf16[256,1024]{1,0:T(8,128)(2,1)}, bf16[256,1024]{1,0:T(8,128)(2,1)}, u32[]{:S(2)}, u32[]{:S(2)}) collective-permute-start(bf16[256,1024]{1,0:T(8,128)(2,1)} %fusion.32), channel_id=1, source_target_pairs={{0,2},{1,3},{2,0},{3,1},{4,6},{5,7},{6,4},{7,5},{8,10},{9,11},{10,... | collective-permute-start | bytes 1572872 | tf_op jit(solution)/shard_map/ppermute | solution.py:479
  257.1 3.0 copy-start.4
  258.1 21.9 %copy-start.12 = (bf16[256,1024]{1,0:T(8,128)(2,1)S(1)}, bf16[256,1024]{1,0:T(8,128)(2,1)}, u32[]{:S(2)}) copy-start(bf16[256,1024]{1,0:T(8,128)(2,1)} %copy-done.11) | copy-start | bytes 1572868
  258.1 21.9 %copy-start.14 = (bf16[256,1024]{1,0:T(8,128)(2,1)S(1)}, bf16[256,1024]{1,0:T(8,128)(2,1)}, u32[]{:S(2)}) copy-start(bf16[256,1024]{1,0:T(8,128)(2,1)} %copy-done.13) | copy-start | bytes 1572868
  258.1 11.5 %collective-permute-start.15 = (bf16[256,1024]{1,0:T(8,128)(2,1)}, bf16[256,1024]{1,0:T(8,128)(2,1)}, u32[]{:S(2)}, u32[]{:S(2)}) collective-permute-start(bf16[256,1024]{1,0:T(8,128)(2,1)} %fusion.31), channel_id=1, source_target_pairs={{16,18},{17,19},{18,16},{19,17},{20,22},{21,23},{22,20},{23,21},{2... | collective-permute-start | bytes 1572872 | tf_op jit(solution)/shard_map/ppermute | solution.py:479
  261.6 18.4 %collective-permute-start.13 = (bf16[256,1024]{1,0:T(8,128)(2,1)}, bf16[256,1024]{1,0:T(8,128)(2,1)}, u32[]{:S(2)}, u32[]{:S(2)}) collective-permute-start(bf16[256,1024]{1,0:T(8,128)(2,1)} %fusion.30), channel_id=1, source_target_pairs={{0,2},{1,3},{2,0},{3,1},{4,6},{5,7},{6,4},{7,5},{8,10},{9,11},{10,... | collective-permute-start | bytes 1572872 | tf_op jit(solution)/shard_map/ppermute | solution.py:479
  283.9 12.1 %collective-permute-start.18 = (bf16[256,1024]{1,0:T(8,128)(2,1)S(1)}, bf16[256,1024]{1,0:T(8,128)(2,1)S(1)}, u32[]{:S(2)}, u32[]{:S(2)}) collective-permute-start(bf16[256,1024]{1,0:T(8,128)(2,1)S(1)} %get-tuple-element.185), channel_id=1, source_target_pairs={{0,16},{1,17},{2,18},{3,19},{4,20},{5,21},{6,22},{7,23},{8,24},{9,... | collective-permute-start | bytes 1572872 | tf_op jit(solution)/shard_map/ppermute | solution.py:482
  296.0 1.4 collective-permute-start.20
  296.7 1.4 collective-permute-start.19
  297.4 0.7 collective-permute-start.21
  303.3 0.7 collective-permute-start.22
  304.6 0.7 collective-permute-start.23
  306.6 98.8 %collective-permute-start.24 = (bf16[256,1024]{1,0:T(8,128)(2,1)S(1)}, bf16[256,1024]{1,0:T(8,128)(2,1)S(1)}, u32[]{:S(2)}, u32[]{:S(2)}) collective-permute-start(bf16[256,1024]{1,0:T(8,128)(2,1)S(1)} %fusion.9), channel_id=1, source_target_pairs={{16,0},{17,1},{18,2},{19,3},{20,4},{21,5},{22,6},{23,7},{24,8},{25... | collective-permute-start | bytes 1572872 | tf_op jit(solution)/shard_map/ppermute | solution.py:482
  405.4 19.0 %copy-start.9 = (bf16[256,1024]{1,0:T(8,128)(2,1)}, bf16[256,1024]{1,0:T(8,128)(2,1)S(1)}, u32[]{:S(2)}) copy-start(bf16[256,1024]{1,0:T(8,128)(2,1)S(1)} %collective-permute-done.24.refs_0_) | copy-start | bytes 1572868
  405.4 14.4 %collective-permute-start.26 = (bf16[256,1024]{1,0:T(8,128)(2,1)S(1)}, bf16[256,1024]{1,0:T(8,128)(2,1)S(1)}, u32[]{:S(2)}, u32[]{:S(2)}) collective-permute-start(bf16[256,1024]{1,0:T(8,128)(2,1)S(1)} %collective-permute-done.24.refs_0_), channel_id=1, source_target_pairs={{0,2},{1,3},{2,0},{3,1},{4,6},{5,7},{6,4},{7,5},{8,10},{9,11},{10,... | collective-permute-start | bytes 1572872 | tf_op jit(solution)/shard_map/ppermute | solution.py:479
  408.3 13.4 %collective-permute-start.25 = (bf16[256,1024]{1,0:T(8,128)(2,1)S(1)}, bf16[256,1024]{1,0:T(8,128)(2,1)S(1)}, u32[]{:S(2)}, u32[]{:S(2)}) collective-permute-start(bf16[256,1024]{1,0:T(8,128)(2,1)S(1)} %collective-permute-done.24.refs_0_), channel_id=1, source_target_pairs={{0,1},{1,0},{2,3},{3,2},{4,5},{5,4},{6,7},{7,6},{8,9},{9,8},{10,11... | collective-permute-start | bytes 1572872 | tf_op jit(solution)/shard_map/ppermute | solution.py:479
  419.8 4.6 copy-start.35
  419.8 3.8 collective-permute-start.27
  421.7 2.7 copy-start.39
  424.4 28.8 %copy-start.28 = (bf16[1024,1024]{1,0:T(8,128)(2,1)S(1)}, bf16[1024,1024]{1,0:T(8,128)(2,1)}, u32[]{:S(2)}) copy-start(bf16[1024,1024]{1,0:T(8,128)(2,1)} %get-tuple-element.149) | copy-start | bytes 6291460
  453.3 3.5 copy-start.29
  453.3 3.5 copy-start.31
  456.8 3.3 copy-start.17
  460.0 83.1 %reduce-scatter.8.cloned.1.call-start = ((), (), s32[]{:S(2)}) async-start(), calls=%async_computation.5 | async-start | bytes 2621440 | tf_op jit(solution)/shard_map/reduce_scatter | solution.py:517
  460.1 4.2 copy-start.16
  460.1 4.2 copy-start.30
  464.3 4.3 copy-start.1
  468.3 127.9 %reduce-scatter.6.cloned.1.call-start = ((), (), s32[]{:S(2)}) async-start(), calls=%async_computation.4 | async-start | bytes 3276800 | tf_op jit(solution)/shard_map/reduce_scatter | solution.py:517
  468.6 4.7 copy-start.2
  468.6 4.7 copy-start.15
  477.6 2.5 copy-start.22
  479.2 3.1 copy-start.19
  479.2 3.0 collective-permute-start.30
  480.2 5.0 collective-permute-start.28
  483.6 7.3 %copy-start.44 = (f32[8,1024]{1,0:T(8,128)S(1)}, f32[8,1024]{1,0:T(8,128)}, u32[]{:S(2)}) copy-start(f32[8,1024]{1,0:T(8,128)} %get-tuple-element.145) | copy-start | bytes 98308
  483.6 7.3 %copy-start.45 = (f32[8,1024]{1,0:T(8,128)S(1)}, f32[8,1024]{1,0:T(8,128)}, u32[]{:S(2)}) copy-start(f32[8,1024]{1,0:T(8,128)} %get-tuple-element.146) | copy-start | bytes 98308
  483.6 50.5 %copy-start.8 = (bf16[256,1024]{1,0:T(8,128)(2,1)S(1)}, bf16[256,1024]{1,0:T(8,128)(2,1)}, u32[]{:S(2)}) copy-start(bf16[256,1024]{1,0:T(8,128)(2,1)} %copy-done.7) | copy-start | bytes 1572868
  483.6 50.5 %copy-start.10 = (bf16[256,1024]{1,0:T(8,128)(2,1)S(1)}, bf16[256,1024]{1,0:T(8,128)(2,1)}, u32[]{:S(2)}) copy-start(bf16[256,1024]{1,0:T(8,128)(2,1)} %copy-done.9) | copy-start | bytes 1572868
  483.6 50.5 %collective-permute-start.31 = (bf16[256,1024]{1,0:T(8,128)(2,1)}, bf16[256,1024]{1,0:T(8,128)(2,1)}, u32[]{:S(2)}, u32[]{:S(2)}) collective-permute-start(bf16[256,1024]{1,0:T(8,128)(2,1)} %fusion.35), channel_id=1, source_target_pairs={{16,18},{17,19},{18,16},{19,17},{20,22},{21,23},{22,20},{23,21},{2... | collective-permute-start | bytes 1572872 | tf_op jit(solution)/shard_map/ppermute | solution.py:479
  487.8 46.3 %collective-permute-start.29 = (bf16[256,1024]{1,0:T(8,128)(2,1)}, bf16[256,1024]{1,0:T(8,128)(2,1)}, u32[]{:S(2)}, u32[]{:S(2)}) collective-permute-start(bf16[256,1024]{1,0:T(8,128)(2,1)} %fusion.34), channel_id=1, source_target_pairs={{0,2},{1,3},{2,0},{3,1},{4,6},{5,7},{6,4},{7,5},{8,10},{9,11},{10,... | collective-permute-start | bytes 1572872 | tf_op jit(solution)/shard_map/ppermute | solution.py:479
  (18 other events, 25.6 us)
Sparse Core Ops, SparseCore 0:
  460.1 34.7 reduce-scatter.3
  497.2 45.9 reduce-scatter.7
  545.6 50.5 reduce-scatter.5

commit v3 on v2

v3 whole, which is shorter than its diff:
```python
import functools
import math

import jax
import jax.numpy as jnp
import numpy as np
from jax import lax
from jax.experimental import pallas as pl
from jax.experimental.pallas import tpu as pltpu
from jax.sharding import PartitionSpec as P

ROT = 16
EPSILON = 1e-05
BLOCK = 512
CHUNK = 128
WIDE = 512
BF = jnp.bfloat16
F32 = jnp.float32
VMEM_BYTES = 60 * 1024 * 1024
ANY = pl.BlockSpec(memory_space=pl.ANY)


def host_tables(slot_rows, head_count, head_size):
    width = head_count * head_size
    halfway = ROT // 2
    column = np.arange(2 * head_size) % head_size
    pair = np.where(column < halfway, column, column - halfway)
    inverse = np.exp(pair * (-2.0 * math.log(10000.0) / ROT))
    angles = np.arange(slot_rows)[:, None] * inverse[None, :]
    turned = (column < 2 * halfway)[None, :]
    sign = np.where(column < halfway, -1.0, 1.0)[None, :]
    cos_full = np.where(turned, np.cos(angles), 1.0)
    sin_full = np.where(turned, sign * np.sin(angles), 0.0)
    order = np.arange(head_size)
    table = np.cos(np.pi * (order[None, :] + 0.5) * order[:, None] / head_size) * np.sqrt(2.0 / head_size)
    table = np.where(order[:, None] == 0, table * np.sqrt(0.5), table)
    dct = np.kron(np.eye(head_count), table.T)
    high = dct.astype(np.float32).astype(BF)
    low = (dct - high.astype(np.float64)).astype(np.float32).astype(BF)
    lane_head = np.arange(width) // head_size
    heads = (np.arange(head_count)[:, None] == lane_head[None, :]).astype(np.float32)
    same = (lane_head[:, None] == lane_head[None, :]).astype(np.float32)
    return {
        "turn": np.stack([cos_full, sin_full]).astype(np.float32),
        "dct": np.stack([high, low]),
        "heads": np.repeat(heads, CHUNK, axis=0).astype(BF),
        "same": same.astype(np.float32),
    }


def dot(a, b):
    return jnp.dot(a, b, preferred_element_type=F32)


def dot_nt(a, b):
    return lax.dot_general(a, b, (((1,), (1,)), ((), ())), preferred_element_type=F32)


def dot_tn(a, b):
    return lax.dot_general(a, b, (((0,), (0,)), ((), ())), preferred_element_type=F32)


def split(x):
    high = x.astype(BF)
    return high, (x - high.astype(F32)).astype(BF)


def stack_heads(x, heads, head_count):
    return jnp.concatenate([x] * head_count, axis=0) * heads


def lanes_of_heads(x, head_count):
    rows = x.shape[0] // head_count
    return jnp.concatenate([x[h * rows:(h + 1) * rows] for h in range(head_count)], axis=1)


def gelu_parts(u):
    cdf = 0.5 + 0.5 * lax.erf(u * (1.0 / math.sqrt(2.0)))
    return u * cdf, cdf + u * (jnp.exp(-0.5 * u * u) * (1.0 / math.sqrt(2.0 * math.pi)))


def partner(x, head_size):
    half = ROT // 2
    lane = lax.broadcasted_iota(jnp.int32, x.shape, 1) & (head_size - 1)
    return jnp.where(lane < half, pltpu.roll(x, x.shape[1] - half, 1), pltpu.roll(x, half, 1))


def standardize(hidden):
    center = hidden - jnp.mean(hidden, axis=-1, keepdims=True)
    spread = jnp.mean(center * center, axis=-1, keepdims=True)
    rstd = lax.rsqrt(spread + EPSILON)
    return center * rstd, rstd


def rows_at(b, size, base=0):
    return pl.ds(pl.multiple_of(b * size + base, size), size)


def flat_scales(ref, head_count):
    return jnp.concatenate([ref[h:h + 1, :] for h in range(head_count)], axis=1)


class Routed:
    def __init__(self, src, keep, send, at, sem):
        self.near = pltpu.make_async_copy(src, keep.at[at >> 1], sem)
        self.far = pltpu.make_async_copy(src, send.at[at >> 1], sem)
        self.at = at

    def start(self):
        @pl.when((self.at & 1) == 0)
        def _():
            self.near.start()

        @pl.when((self.at & 1) != 0)
        def _():
            self.far.start()

    def wait(self):
        self.near.wait()


class Copies:
    def __init__(self, sems):
        self.sems = sems
        self.used = 0

    def start(self, *pairs):
        made = []
        for src, dst in pairs:
            copy = pltpu.make_async_copy(src, dst, self.sems.at[self.used])
            self.used += 1
            copy.start()
            made.append(copy)
        return made


def wait(copies):
    for copy in copies:
        copy.wait()


def looped_out(pairs, sems, first, b):
    return [pltpu.make_async_copy(src, dst, sems.at[first + i, b]) for i, (src, dst) in enumerate(pairs)]


def forward_kernel(cfg, order, *refs):
    pieces, base, share, origin, e, f, hc = (cfg[k] for k in ("pieces", "base", "share", "origin", "e", "f", "hc"))
    hd = e // hc
    carried = cfg["carried"]
    refs = list(refs)

    def take(n):
        out = refs[:n]
        del refs[:n]
        return out

    h_in = take(pieces)
    wq, wk, wv, wo, wup, wdown, *norms, scales, turn, dct, heads, same, lengths = take(16)
    cotangent = None if cfg["branch"] else take(1)[0]
    c_in = take(2 if carried else 0)
    take(cfg["alias"])
    s_n1, s_n2, s_am, s_gp, s_qf, s_kf, s_v, s_mf, s_inv, s_st, s_kt, s_h, own, c_st, c_kt = take(15)
    keep, send = take(2) if cfg["branch"] else (None, None)
    s_mix = None if cfg["branch"] else take(1)[0]
    (v_h, v_wqkv, v_wo, v_wup, v_wdown, v_norms, v_scales, v_turn, v_dct, v_heads, v_same,
     o_n1, o_n2, o_am, o_gp, o_qf, o_kf, o_v, o_mf, o_inv, o_st, o_kt, o_part, state, total, v_len, v_g, o_mix, sems, o_sems) = refs
    rows = v_h.shape[0]
    blocks = rows // BLOCK
    wides = rows // WIDE
    count = BLOCK // CHUNK
    me = lax.axis_index("tensor")

    def outs_a(b):
        rb, ro = rows_at(b, BLOCK), rows_at(b, BLOCK, base)
        return looped_out([(o_n1.at[rb], s_n1.at[ro]), (o_n2.at[rb], s_n2.at[ro])], o_sems, 0, b)

    def outs_b(b):
        rb, ro = rows_at(b, BLOCK), rows_at(b, BLOCK, base)
        cb, co = pl.ds(b * count, count), pl.ds(b * count + base // CHUNK, count)
        return looped_out([(o.at[rb], s.at[ro]) for o, s in ((o_qf, s_qf), (o_kf, s_kf), (o_v, s_v), (o_mf, s_mf), (o_inv, s_inv))]
                          + [(o_st.at[cb], s_st.at[co]), (o_kt.at[cb], s_kt.at[co])], o_sems, 2, b)

    def outs_c(b):
        rb, ro = rows_at(b, WIDE), rows_at(b, WIDE, base)
        copies = looped_out([(o_am.at[rb], s_am.at[ro]), (o_gp.at[rb], s_gp.at[ro])] + ([] if cfg["branch"] else [(o_mix.at[rb], s_mix.at[ro])]), o_sems, 9, b)
        for i in range(WIDE // share if cfg["branch"] else 0):
            at = (b * (WIDE // share) + i + origin) ^ me
            copies.append(Routed(o_part.at[rows_at(b * (WIDE // share) + i, share)], keep, send, at, o_sems.at[11 + i, b]))
        return copies

    @pl.when(lax.axis_index("section") == cfg["section"])
    def _():
        io = Copies(sems)
        if pieces == 1:
            in_h = io.start((h_in[0].at[cfg["m"], 0, pl.ds(base, rows)] if len(h_in[0].shape) == 4 else h_in[0], v_h))
        else:
            halves = pieces // 4
            in_h = io.start(*[(h_in[h * 4 + k], v_h.at[rows_at((me ^ k) * halves + h, rows // pieces)]) for h in range(halves) for k in range(4)])
        in_h += io.start(*[(norm, v_norms.at[i]) for i, norm in enumerate(norms)], (scales.at[0], v_scales))
        in_b = io.start(*[(w.at[0], v_wqkv.at[:, pl.ds(i * e, e)]) for i, w in enumerate((wq, wk, wv))], (turn.at[:, pl.ds(base, rows)], v_turn),
                        (dct, v_dct), (heads, v_heads), (same, v_same), (lengths, v_len))
        if carried:
            in_b += io.start((c_in[0], state), (c_in[1], total))
        else:
            state[...] = jnp.zeros_like(state)
            total[...] = jnp.zeros_like(total)
        in_c = io.start((wup.at[0], v_wup), (wo.at[0], v_wo), (wdown.at[0], v_wdown),
                        *([] if cfg["branch"] else [(cotangent.at[cfg["m"], 0], v_g)]))
        wait(in_h)
        out_h = io.start(*([(v_h, s_h.at[pl.ds(base, rows)])] if cfg["section"] else []), (v_h.at[rows_at(me, rows // 4)], own))

        @pl.loop(0, blocks)
        def _(b):
            rb = rows_at(b, BLOCK)
            xhat, _ = standardize(v_h[rb].astype(F32))
            o_n1[rb] = (xhat * v_norms[0] + v_norms[1]).astype(BF)
            o_n2[rb] = (xhat * v_norms[2] + v_norms[3]).astype(BF)
            for copy in outs_a(b):
                copy.start()

        wait(in_b)

        @pl.loop(0, blocks)
        def _(b):
            rb = rows_at(b, BLOCK)
            qkv = dot(o_n1[rb], v_wqkv[...])
            cos_b = jnp.concatenate([jnp.concatenate([v_turn[0, rb]] * (hc // 2), axis=1)] * 2, axis=0)
            sin_b = jnp.concatenate([jnp.concatenate([v_turn[1, rb]] * (hc // 2), axis=1)] * 2, axis=0)
            pair = jnp.concatenate([qkv[:, :e], qkv[:, e:2 * e]], axis=0)
            high, low = split(pair * cos_b + partner(pair, hd) * sin_b)
            feats = flat_scales(v_scales, hc) * jnp.exp(dot(high, v_dct[0]) + dot(low, v_dct[0]) + dot(high, v_dct[1]))
            q_feat = feats[:BLOCK]
            slot = lax.broadcasted_iota(jnp.int32, (BLOCK, e), 0) + (b * BLOCK + base)
            k_feat = jnp.where(slot < v_len[cfg["m"]:cfg["m"] + 1, :], feats[BLOCK:], 0.0)
            value = qkv[:, 2 * e:].astype(BF)
            o_qf[rb] = q_feat
            o_kf[rb] = k_feat
            o_v[rb] = value
            q_b = q_feat.astype(BF)
            k_b = k_feat.astype(BF)
            row = lax.broadcasted_iota(jnp.int32, (CHUNK, hc * CHUNK), 0)
            col = lax.broadcasted_iota(jnp.int32, (CHUNK, hc * CHUNK), 1) & (CHUNK - 1)
            causal = row >= col
            for c in range(count):
                rc = slice(c * CHUNK, (c + 1) * CHUNK)
                at = b * count + c
                q_c, k_c, v_c = q_b[rc], k_b[rc], value[rc]
                o_st[at] = state[...]
                o_kt[at] = total[...]
                weighted = (q_c.astype(F32) * total[0:1, :]).astype(BF)
                scores = jnp.where(causal, dot_nt(q_c, stack_heads(k_c, v_heads[...], hc)), 0.0).astype(BF)
                both = dot(scores, jnp.concatenate([stack_heads(v_c, v_heads[...], hc), v_heads[...]], axis=1))
                inverse = 1.0 / (both[:, e:] + dot(weighted, v_same[...].astype(BF)))
                mixed = (both[:, :e] + dot(q_c, state[...].astype(BF))) * inverse
                rg = rows_at(at, CHUNK)
                o_inv[rg] = inverse
                o_mf[rg] = mixed
                o_am[rg, f:] = mixed.astype(BF)
                state[...] += dot_tn(k_c, v_c) * v_same[...]
                total[...] += jnp.sum(k_c.astype(F32), axis=0, keepdims=True)
            for copy in outs_b(b):
                copy.start()

        out_s = io.start((state, c_st), (total, c_kt))
        wait(in_c)

        @pl.loop(0, wides)
        def _(b):
            rb = rows_at(b, WIDE)
            act, slope = gelu_parts(dot(o_n2[rb], v_wup[...]))
            o_am[rb, :f] = act.astype(BF)
            if not cfg["branch"]:
                slope = slope * dot_nt(v_g[rb], v_wdown[...])
                o_mix[rb] = dot_nt(v_g[rb], v_wo[...]).astype(BF)
            o_gp[rb] = slope.astype(BF)
            if cfg["branch"]:
                o_part[rb] = (dot(o_am[rb, f:], v_wo[...]) + dot(o_am[rb, :f], v_wdown[...])).astype(BF)
            for copy in outs_c(b):
                copy.start()

        wait(out_h + out_s)

        @pl.loop(0, blocks)
        def _(b):
            wait(outs_a(b) + outs_b(b))

        @pl.loop(0, wides)
        def _(b):
            wait(outs_c(b))


def backward_kernel(cfg, order, *refs):
    base, share, e, f, hc = (cfg[k] for k in ("base", "share", "e", "f", "hc"))
    hd = e // hc
    carried = cfg["carried"]
    refs = list(refs)

    def take(n):
        out = refs[:n]
        del refs[:n]
        return out

    g_in = take(cfg["grads"])
    h_in, wq, wk, wv, wo, wup, wdown, *norms, scales, turn, dct, heads, same, _ = take(17)
    s_qf, s_kf, s_v, s_mf, s_inv, s_st, s_kt = take(7)
    opened = cfg["opened"]
    (in_gup, in_mix) = take(2) if opened else (None, None)
    c_in = take(2 if carried else 0)
    s_gp = take(cfg["alias"])[0] if not opened else None
    s_gup = take(1)[0] if not opened else None
    s_gqkv, keep, send, own, sums, c_st, c_kt = take(7)
    (v_g, v_h, v_wqkv, v_wo, v_wup, v_wdown, v_norms, v_scales, v_turn, v_dct, v_heads, v_same,
     i_gp, i_qf, i_kf, i_v, i_mf, i_inv, i_st, i_kt,
     o_gup, o_gqkv, o_part, o_sums, mixes, acc, acc_s, state, total, sems, o_sems) = refs
    rows, d = v_h.shape
    blocks = rows // BLOCK
    wides = rows // WIDE
    chunks = rows // CHUNK
    count = BLOCK // CHUNK
    me = lax.axis_index("tensor")

    def place(x):
        return x.at[cfg["m"], 0, pl.ds(base, rows)] if len(x.shape) == 4 else x.at[pl.ds(base, rows)]

    def outs_a(b):
        rb, ro = rows_at(b, WIDE), rows_at(b, WIDE, base)
        return [] if opened else looped_out([(o_gup.at[rb], s_gup.at[ro])], o_sems, 0, b)

    def outs_b(b):
        rb, ro = rows_at(b, BLOCK), rows_at(b, BLOCK, base)
        return looped_out([(o_gqkv.at[rb], s_gqkv.at[ro])], o_sems, 1, b)

    def outs_c(b):
        copies = []
        for i in range(BLOCK // share):
            at = (b * (BLOCK // share) + i) ^ me
            copies.append(Routed(o_part.at[rows_at(b * (BLOCK // share) + i, share)], keep, send, at, o_sems.at[2 + i, b]))
        return copies

    @pl.when(lax.axis_index("section") == cfg["section"])
    def _():
        io = Copies(sems)
        some = pl.ds(base, rows)
        some_chunks = pl.ds(base // CHUNK, chunks)
        in_g = [(place(g_in[0]), v_g)] if len(g_in) == 1 else [(g, v_g.at[pl.ds(i * g.shape[0], g.shape[0])]) for i, g in enumerate(g_in)]
        in_a = io.start(*in_g, *([(in_gup.at[some], o_gup), (in_mix.at[some], mixes)] if opened else
                                [(wdown.at[0], v_wdown), (wo.at[0], v_wo), (s_gp.at[some], i_gp)]))
        in_b = io.start((s_mf.at[some], i_mf), (s_inv.at[some], i_inv), (s_qf.at[some], i_qf), (s_kf.at[some], i_kf), (s_v.at[some], i_v),
                        (s_st.at[some_chunks], i_st), (s_kt.at[some_chunks], i_kt), (heads, v_heads), (same, v_same),
                        (turn.at[:, some], v_turn), (dct, v_dct))
        if carried:
            in_b += io.start((c_in[0], state), (c_in[1], total))
        else:
            state[...] = jnp.zeros_like(state)
            total[...] = jnp.zeros_like(total)
        in_c = io.start(*[(w.at[0], v_wqkv.at[:, pl.ds(i * e, e)]) for i, w in enumerate((wq, wk, wv))], (wup.at[0], v_wup), (place(h_in), v_h),
                        *[(norm, v_norms.at[i]) for i, norm in enumerate(norms)], (scales.at[0], v_scales))
        acc[...] = jnp.zeros_like(acc)
        acc_s[...] = jnp.zeros_like(acc_s)
        wait(in_a)
        out_s = io.start((v_g.at[rows_at(me, rows // 4)], own))

        def fold(x):
            return jnp.sum(x.reshape(x.shape[0] // 8, 8, x.shape[1]), axis=0)

        @pl.loop(0, 0 if opened else wides)
        def _(b):
            rb = rows_at(b, WIDE)
            g_b = v_g[rb]
            o_gup[rb] = (dot_nt(g_b, v_wdown[...]) * i_gp[rb].astype(F32)).astype(BF)
            mixes[rb] = dot_nt(g_b, v_wo[...]).astype(BF)
            for copy in outs_a(b):
                copy.start()

        wait(in_b)

        @pl.loop(0, blocks)
        def _(step):
            b = blocks - 1 - step
            rb = rows_at(b, BLOCK)
            g_num = (mixes[rb].astype(F32) * i_inv[rb]).astype(BF)
            high, low = split(g_num.astype(F32) * i_mf[rb])
            same_b = v_same[...].astype(BF)
            g_den = -(dot(high, same_b) + dot(low, same_b))
            gd_high, gd_low = split(g_den)
            q_feat = i_qf[rb]
            k_feat = i_kf[rb]
            value = i_v[rb]
            q_b = q_feat.astype(BF)
            k_b = k_feat.astype(BF)
            row = lax.broadcasted_iota(jnp.int32, (CHUNK, hc * CHUNK), 0)
            col = lax.broadcasted_iota(jnp.int32, (CHUNK, hc * CHUNK), 1) & (CHUNK - 1)
            causal = row >= col
            row_t = lax.broadcasted_iota(jnp.int32, (hc * CHUNK, CHUNK), 0) & (CHUNK - 1)
            col_t = lax.broadcasted_iota(jnp.int32, (hc * CHUNK, CHUNK), 1)
            causal_t = col_t >= row_t
            hm = v_heads[...]
            sel = hm * jnp.asarray(1.0 / hd, BF)
            gq_parts, gk_parts, gv_parts = [None] * count, [None] * count, [None] * count
            for c in reversed(range(count)):
                rc = slice(c * CHUNK, (c + 1) * CHUNK)
                at = b * count + c
                q_c, k_c, v_c, n_c, dh, dl = q_b[rc], k_b[rc], value[rc], g_num[rc], gd_high[rc], gd_low[rc]
                k_x = stack_heads(k_c, hm, hc)
                spread = jnp.concatenate([jnp.broadcast_to(g_den[rc, h * hd:h * hd + 1], (CHUNK, CHUNK)) for h in range(hc)], axis=1)
                grid = jnp.where(causal, dot_nt(n_c, stack_heads(v_c, hm, hc)) + spread, 0.0).astype(BF)
                grid_s = jnp.concatenate([grid[:, h * CHUNK:(h + 1) * CHUNK] for h in range(hc)], axis=0)
                scores_t = jnp.where(causal_t, dot_nt(k_x, q_c), 0.0).astype(BF)
                before = jnp.concatenate(split(i_st[at]), axis=1)
                gq_parts[c] = dot(grid, k_x) + dot_nt(jnp.concatenate([n_c, n_c], axis=1), before) + g_den[rc] * i_kt[at][0:1, :]
                after = jnp.concatenate(split(state[...]), axis=1)
                gk_parts[c] = dot_tn(grid_s, stack_heads(q_c, hm, hc)) + dot_nt(jnp.concatenate([v_c, v_c], axis=1), after) + total[0:1, :]
                gv_parts[c] = dot(lanes_of_heads(scores_t, hc), stack_heads(n_c, hm, hc)) + dot(k_c, after[:, :e])
                state[...] += dot_tn(q_c, n_c) * v_same[...]
                total[...] += jnp.sum(q_c.astype(F32) * g_den[rc], axis=0, keepdims=True)
            gc_q = jnp.concatenate(gq_parts, axis=0) * q_feat
            gc_k = jnp.concatenate(gk_parts, axis=0) * k_feat
            g_value = jnp.concatenate(gv_parts, axis=0)
            acc_s[...] += fold(gc_q + gc_k)
            cos_b = jnp.concatenate([jnp.concatenate([v_turn[0, rb]] * (hc // 2), axis=1)] * 2, axis=0)
            sin_b = jnp.concatenate([jnp.concatenate([v_turn[1, rb]] * (hc // 2), axis=1)] * 2, axis=0)
            turned = dot_nt(jnp.concatenate([gc_q, gc_k], axis=0).astype(BF), v_dct[0])
            g_qk = turned * cos_b - partner(turned, hd) * sin_b
            o_gqkv[rb] = jnp.concatenate([g_qk[:BLOCK], g_qk[BLOCK:], g_value], axis=1).astype(BF)
            for copy in outs_b(b):
                copy.start()

        out_s += io.start((state, c_st), (total, c_kt))
        wait(in_c)

        @pl.loop(0, blocks)
        def _(b):
            rb = rows_at(b, BLOCK)
            g_one = dot_nt(o_gqkv[rb], v_wqkv[...])
            g_two = dot_nt(o_gup[rb], v_wup[...])
            xhat, rstd = standardize(v_h[rb].astype(F32))
            acc[0] += fold(g_one * xhat)
            acc[1] += fold(g_one)
            acc[2] += fold(g_two * xhat)
            acc[3] += fold(g_two)
            acc[4] += fold(v_g[rb].astype(F32))
            inner = g_one * v_norms[0] + g_two * v_norms[2]
            mean_t = jnp.mean(inner, axis=-1, keepdims=True)
            mean_x = jnp.mean(inner * xhat, axis=-1, keepdims=True)
            o_part[rb] = (rstd * (inner - mean_t - xhat * mean_x)).astype(BF)
            for copy in outs_c(b):
                copy.start()

        for i in range(5):
            o_sums[i:i + 1, :] = jnp.sum(acc[i], axis=0, keepdims=True)
        o_sums[5:8, :] = jnp.zeros((3, d), F32)
        o_sums[5:6, :e] = jnp.sum(acc_s[...], axis=0, keepdims=True) / flat_scales(v_scales, hc)
        out_s += io.start((o_sums, sums))
        wait(out_s)

        @pl.loop(0, 0 if opened else wides)
        def _(b):
            wait(outs_a(b))

        @pl.loop(0, blocks)
        def _(b):
            wait(outs_b(b) + outs_c(b))


def like(shape, dtype):
    return jax.ShapeDtypeStruct(shape, dtype)


def forward_call(sizes, m, section, order, pieces, weights, tabs, store, span=None, carry=(), parts=(), ends=False, cotangent=None):
    rows, d, e, f, hc = sizes
    base, end = span or (0, rows)
    some = end - base
    share = rows // 4 if ends or some == rows else some // 4
    chunks = rows // CHUNK
    own = some // CHUNK
    shapes = [
        like((rows, d), BF), like((rows, d), BF), like((rows, f + e), BF), like((rows, f), BF),
        like((rows, e), F32), like((rows, e), F32), like((rows, e), BF), like((rows, e), F32),
        like((rows, e), F32), like((chunks, e, e), F32), like((chunks, 8, e), F32), like((rows, d), BF),
        like((some // 4, d), BF), like((e, e), F32), like((8, e), F32),
    ] + ([like((2, share, d), BF)] * 2 if section == 0 else [like((rows, e), BF)])
    through = list(store) + list(parts)
    operands = [order, *pieces, *weights, *tabs, *([] if section == 0 else [cotangent]), *carry, *through]
    scratch = [pltpu.VMEM(shape, dtype) for shape, dtype in (
        ((some, d), BF), ((d, 3 * e), BF), ((e, d), BF), ((d, f), BF), ((f, d), BF),
        ((4, 1, d), F32), ((hc, e // hc), F32), ((2, some, 2 * (e // hc)), F32), ((2, e, e), BF), ((hc * CHUNK, e), BF), ((e, e), F32),
        ((some, d), BF), ((some, d), BF), ((some, f + e), BF), ((some, f), BF),
        ((some, e), F32), ((some, e), F32), ((some, e), BF), ((some, e), F32),
        ((some, e), F32), ((own, e, e), F32), ((own, 8, e), F32), ((some, d), BF),
        ((e, e), F32), ((8, e), F32))]
    scratch += [pltpu.VMEM(tabs[-1].shape, jnp.int32), pltpu.VMEM((some, d), BF), pltpu.VMEM((some, e), BF), pltpu.SemaphoreType.DMA((32,)), pltpu.SemaphoreType.DMA((16, some // BLOCK))]
    cfg = {"m": m, "section": section, "pieces": len(pieces), "base": base, "share": share, "origin": base // share if ends else 0,
           "e": e, "f": f, "hc": hc, "carried": bool(carry), "alias": len(through), "branch": section == 0}
    first = len(operands) - len(through)
    results = pl.pallas_call(
        functools.partial(forward_kernel, cfg),
        out_shape=shapes,
        in_specs=[ANY] * len(operands),
        out_specs=[ANY] * len(shapes),
        scratch_shapes=scratch,
        input_output_aliases={first + i: i for i in range(len(through))},
        compiler_params=pltpu.CompilerParams(vmem_limit_bytes=VMEM_BYTES),
        cost_estimate=pl.CostEstimate(flops=2 * some * d * (4 * e + 2 * f), bytes_accessed=25 * 2 ** 20, transcendentals=some * (f + 2 * e)),
        name="forward",
    )(*operands)
    return list(results[:12]), results[12], list(results[15:])


def backward_call(sizes, m, section, order, g_in, h_in, weights, tabs, store, back, span=None, carry=(), opened=()):
    rows, d, e, f, hc = sizes
    base, end = span or (0, rows)
    some = end - base
    share = some // 4
    own = some // CHUNK
    shapes = [like((rows, f), BF)] * (not opened) + [like((rows, 3 * e), BF), like((2, share, d), BF), like((2, share, d), BF), like((some // 4, d), BF), like((8, d), F32), like((e, e), F32), like((8, e), F32)]
    operands = [order, *g_in, h_in, *weights, *tabs, *store[4:11], *opened, *carry, *back]
    scratch = [pltpu.VMEM(shape, dtype) for shape, dtype in (
        ((some, d), BF), ((some, d), BF), ((d, 3 * e), BF), ((e, d), BF), ((d, f), BF), ((f, d), BF),
        ((4, 1, d), F32), ((hc, e // hc), F32), ((2, some, 2 * (e // hc)), F32), ((2, e, e), BF), ((hc * CHUNK, e), BF), ((e, e), F32),
        ((some, f), BF), ((some, e), F32), ((some, e), F32), ((some, e), BF),
        ((some, e), F32), ((some, e), F32), ((own, e, e), F32), ((own, 8, e), F32),
        ((some, f), BF), ((some, 3 * e), BF), ((some, d), BF), ((8, d), F32),
        ((some, e), BF), ((5, 8, d), F32), ((8, e), F32), ((e, e), F32), ((8, e), F32))]
    scratch += [pltpu.SemaphoreType.DMA((40,)), pltpu.SemaphoreType.DMA((4, some // BLOCK))]
    cfg = {"m": m, "section": section, "base": base, "share": share, "e": e, "f": f, "hc": hc, "carried": bool(carry), "alias": len(back), "grads": len(g_in), "opened": bool(opened)}
    first = len(operands) - len(back)
    results = pl.pallas_call(
        functools.partial(backward_kernel, cfg),
        out_shape=shapes,
        in_specs=[ANY] * len(operands),
        out_specs=[ANY] * len(shapes),
        scratch_shapes=scratch,
        input_output_aliases={first + i: i for i in range(len(back))},
        compiler_params=pltpu.CompilerParams(vmem_limit_bytes=VMEM_BYTES),
        cost_estimate=pl.CostEstimate(flops=2 * some * d * (4 * e + 2 * f), bytes_accessed=30 * 2 ** 20, transcendentals=0),
        name="backward",
    )(*operands)
    head = 1 if opened else 2
    return list(results[:head]), list(results[head:head + 3]), results[head + 3], list(results[head + 4:])


def down_kernel(cfg, order, *refs):
    count, first, m = cfg["pieces"], cfg["first"], cfg["m"]
    refs = list(refs)

    def take(n):
        out = refs[:n]
        del refs[:n]
        return out

    pieces = take(count)
    (am,) = take(1)
    acc_in = take(0 if first else 1)
    take(cfg["alias"])
    outs = take(2 if count == 4 else 1)
    v_g, v_am, v_acc, v_out, sems, o_sems = refs
    rows, d = v_g.shape
    me = lax.axis_index("tensor")

    def tile(b):
        return rows_at(b, BLOCK)

    def sent(b):
        return pltpu.make_async_copy((v_acc if first else v_out).at[tile(b)], outs[0].at[tile(b)], o_sems.at[b])

    @pl.when(lax.axis_index("section") == cfg["section"])
    def _():
        io = Copies(sems)
        if count == 4:
            loads = io.start(*[(pieces[k], v_g.at[rows_at(me ^ k, rows // 4)]) for k in range(4)])
        else:
            loads = io.start((pieces[0].at[m, 0] if len(pieces[0].shape) == 4 else pieces[0], v_g))
        loads += io.start((am, v_am))
        if not first:
            loads += io.start((acc_in[0], v_acc))
        wait(loads)
        kept = io.start((v_g, outs[1])) if count == 4 else []

        @pl.loop(0, d // BLOCK)
        def _(b):
            product = dot_tn(v_g[:, tile(b)], v_am[...])
            if first:
                v_acc[tile(b)] = product.astype(BF)
            else:
                v_out[tile(b)] = (v_acc[tile(b)].astype(F32) + product).astype(BF)
            sent(b).start()

        wait(kept)

        @pl.loop(0, d // BLOCK)
        def _(b):
            sent(b).wait()


def branch_kernel(order, am, wo, wdown, keep, send, v_am, v_wo, v_wdown, o_part, sems, o_sems):
    rows, d = o_part.shape
    f = v_wdown.shape[0]
    share = rows // 4
    me = lax.axis_index("tensor")

    def outs(b):
        copies = []
        for i in range(WIDE // share):
            at = (b * (WIDE // share) + i) ^ me
            copies.append(Routed(o_part.at[rows_at(b * (WIDE // share) + i, share)], keep, send, at, o_sems.at[i, b]))
        return copies

    @pl.when(lax.axis_index("section") == 1)
    def _():
        wait(Copies(sems).start((am, v_am), (wo.at[0], v_wo), (wdown.at[0], v_wdown)))

        @pl.loop(0, rows // WIDE)
        def _(b):
            rb = rows_at(b, WIDE)
            o_part[rb] = (dot(v_am[rb, f:], v_wo[...]) + dot(v_am[rb, :f], v_wdown[...])).astype(BF)
            for copy in outs(b):
                copy.start()

        @pl.loop(0, rows // WIDE)
        def _(b):
            wait(outs(b))


def branch_call(order, am, w_out, w_down):
    rows, wide = am.shape
    _, f, d = w_down.shape
    return pl.pallas_call(
        branch_kernel,
        out_shape=[like((2, rows // 4, d), BF)] * 2,
        in_specs=[ANY] * 4,
        out_specs=[ANY] * 2,
        scratch_shapes=[pltpu.VMEM((rows, wide), BF), pltpu.VMEM((wide - f, d), BF), pltpu.VMEM((f, d), BF), pltpu.VMEM((rows, d), BF),
                        pltpu.SemaphoreType.DMA((3,)), pltpu.SemaphoreType.DMA((2, rows // WIDE))],
        compiler_params=pltpu.CompilerParams(vmem_limit_bytes=VMEM_BYTES),
        cost_estimate=pl.CostEstimate(flops=0, bytes_accessed=0, transcendentals=0),
        name="branch",
    )(order, am, w_out, w_down)


def arrange_kernel(order, *refs):
    pieces, (out, held, sems) = refs[:4], refs[4:]
    me = lax.axis_index("tensor")

    @pl.when(lax.axis_index("section") == 0)
    def _():
        io = Copies(sems)
        wait(io.start(*[(pieces[k], held.at[rows_at(me ^ k, pieces[k].shape[0])]) for k in range(4)]))
        wait(io.start((held, out)))


def arrange_call(order, pieces):
    share, d = pieces[0].shape
    return pl.pallas_call(
        arrange_kernel,
        out_shape=[like((4 * share, d), BF)],
        in_specs=[ANY] * 5,
        out_specs=[ANY],
        scratch_shapes=[pltpu.VMEM((4 * share, d), BF), pltpu.SemaphoreType.DMA((5,))],
        cost_estimate=pl.CostEstimate(flops=0, bytes_accessed=0, transcendentals=0),
        name="arrange",
    )(order, *pieces)


def unpack_kernel(packed, *outs):
    at = 0
    for out in outs:
        out[0] = packed[:, at:at + out.shape[2]].astype(F32)
        at += out.shape[2]


def unpack_call(packed, widths):
    rows = packed.shape[0]
    whole = pl.BlockSpec(memory_space=pltpu.VMEM)
    return pl.pallas_call(
        unpack_kernel,
        out_shape=[like((1, rows, width), F32) for width in widths],
        in_specs=[whole],
        out_specs=[whole] * len(widths),
        name="unpack",
    )(packed)


def down_call(m, section, order, pieces, am, acc=None, through=None):
    rows, wide = am.shape
    d = pieces[0].shape[-1]
    first = acc is None
    operands = [order, *pieces, am] + ([] if first else [acc]) + ([] if through is None else [through])
    cfg = {"pieces": len(pieces), "first": first, "section": section, "m": m, "alias": int(through is not None)}
    shapes = [like((d, wide), BF)] + [like((rows, d), BF)] * (len(pieces) == 4)
    return pl.pallas_call(
        functools.partial(down_kernel, cfg),
        out_shape=shapes,
        in_specs=[ANY] * len(operands),
        out_specs=[ANY] * len(shapes),
        scratch_shapes=[pltpu.VMEM((rows, d), BF), pltpu.VMEM((rows, wide), BF), pltpu.VMEM((d, wide), BF), pltpu.VMEM((d, wide), BF),
                        pltpu.SemaphoreType.DMA((len(pieces) + 5,)), pltpu.SemaphoreType.DMA((d // BLOCK,))],
        input_output_aliases={} if through is None else {len(operands) - 1: 0},
        compiler_params=pltpu.CompilerParams(vmem_limit_bytes=VMEM_BYTES),
        cost_estimate=pl.CostEstimate(flops=0 if first else 2 * rows * d * wide, bytes_accessed=0 if first else 12 * 2 ** 20, transcendentals=0),
        name="down",
    )(*operands)


def body(tokens, cotangent, lengths, attn_gain, attn_bias, ffn_gain, ffn_bias, w_query, w_key, w_value, w_out, feat_scale, w_up, w_down, down_bias):
    section = lax.axis_index("section")
    tensor = lax.axis_index("tensor")
    teams = lax.axis_size("tensor")
    micro, _, rows, d = tokens.shape
    hc, hd = feat_scale.shape[1:]
    e = hc * hd
    f = w_up.shape[2]
    sizes = (rows, d, e, f, hc)
    whole, early, late = (0, rows), (0, rows // 2), (rows // 2, rows)
    made = host_tables(rows, hc, hd)
    tabs = [attn_gain, attn_bias, ffn_gain, ffn_bias, feat_scale] + [jnp.asarray(made[k]) for k in ("turn", "dct", "heads", "same")] + [lengths]
    weights = [w_query, w_key, w_value, w_out, w_up, w_down]
    both = ("section", "tensor")
    order = attn_gain

    def swap(x, sec, bit):
        sections = range(2) if sec is None else (sec,)
        return lax.ppermute(x, both, [(k * teams + i, k * teams + (i ^ bit)) for k in sections for i in range(teams)])

    def hand(x, source):
        return lax.ppermute(x, "section", [(source, 1 - source)])

    def gather_rows(own, sec):
        far = swap(own, sec, 2)
        return [own, swap(own, sec, 1), far, swap(far, sec, 1)]

    def tie(x, *after):
        return lax.optimization_barrier((x, *after))[0]

    def tie_all(*values):
        return lax.optimization_barrier(values)

    def near_sum(parts, sec):
        keep, send = parts
        got = swap(send, sec, 1)
        return keep[0].astype(F32) + got[0].astype(F32), (keep[1].astype(F32) + got[1].astype(F32)).astype(BF)

    def relay(parts, source):
        near, sent = near_sum(parts, source)
        near = (near + down_bias[0] if source == 0 else near).astype(BF)
        pairs = [[(source * teams + i, (1 - source) * teams + (i ^ bit)) for i in range(teams)] for bit in (0, 2)]
        return [lax.ppermute(near, both, pairs[0]), lax.ppermute(sent, both, pairs[1])], (near, sent)

    def own_rows(x):
        return lax.dynamic_index_in_dim(x.reshape(teams, rows // teams, d), tensor, 0, keepdims=False)

    def whole_rows(own):
        return lax.all_gather(own, "tensor", axis=0, tiled=True)

    def summed(start, took):
        return start.astype(F32) + took[0].astype(F32) + took[1].astype(F32)

    def all_sum(x, axis):
        size, bit = lax.axis_size(axis), 1
        if size & (size - 1):
            return lax.psum(x, axis)
        while bit < size:
            x = x + lax.ppermute(x, axis, [(i, i ^ bit) for i in range(size)])
            bit *= 2
        return x

    def weight_grad(pairs):
        return sum(dot_tn(left, right) for left, right in pairs)

    def scatter(total):
        return lax.psum_scatter(total, "dp", scatter_dimension=0, tiled=True)

    def forward(m, sec, after, pieces, store, **more):
        return forward_call(sizes, m, sec, tie(order, after), pieces, weights, tabs, store, **more)

    def backward(m, sec, after, g_in, h_in, store, back, **more):
        return backward_call(sizes, m, sec, tie(order, after), g_in, h_in, weights, tabs, store, back, **more)

    store_0, _, parts = forward_call(sizes, 0, 0, order, [tokens], weights, tabs, [])
    took, after = relay(parts, 0)
    store_1, _, parts = forward_call(sizes, 1, 0, tie(order, *after), [tokens], weights, tabs, [])
    own_t, *took, parts[0], parts[1] = tie_all(own_rows(tokens[0, 0]), *took, *parts)
    row_0 = summed(own_t, took).astype(BF)
    far_rows = swap(row_0, 1, 2)
    took, after = relay(parts, 0)
    near_rows = swap(tie(row_0, *after), 1, 1)
    far_rows, near_rows = tie_all(far_rows, near_rows)
    store_0, own_0, mix_0 = forward_call(sizes, 0, 1, tie(order, *after), [row_0, near_rows, far_rows, swap(far_rows, 1, 1)], weights, tabs, store_0, cotangent=cotangent)
    own_c = [own_rows(cotangent[m, 0]) for m in range(2)]
    *took, own_0, own_t, own_c[0], own_c[1] = tie_all(*took, own_0, own_rows(tokens[1, 0]), *own_c)
    row_1 = summed(own_t, took).astype(BF)
    rows_1 = whole_rows(row_1)
    back_0, parts, sums_0, _ = backward(0, 1, row_1, [cotangent], store_0[11], store_0, [], opened=[store_0[3], *mix_0])
    took_0, after = relay(parts[:2], 1)
    rows_1 = tie(rows_1, *after)
    store_1, own_1, mix_1 = forward_call(sizes, 1, 1, tie(order, *after), [rows_1], weights, tabs, store_1, cotangent=cotangent)
    *took_0, own_1 = tie_all(*took_0, own_1)
    grad_0 = summed(own_c[0], took_0).astype(BF)
    gb_0 = whole_rows(grad_0)
    back_1, parts, sums_1, _ = backward(1, 1, grad_0, [cotangent], store_1[11], store_1, [], opened=[store_1[3], *mix_1])
    took_1, after = relay(parts[:2], 1)
    gb_0, after = tie_all(gb_0, tie(order, *after))
    ends_0 = [*branch_call(after, store_0[2], w_out, w_down), own_0]
    ends_1 = [*branch_call(after, store_1[2], w_out, w_down), own_1]
    back_0, ends_0, sums_0, _ = backward(0, 0, gb_0, [gb_0], tokens, store_0, [store_0[3], *back_0, *ends_0, sums_0])
    *took_1, ends_0[0] = tie_all(*took_1, ends_0[0])
    grad_1 = summed(own_c[1], took_1).astype(BF)
    far_rows = swap(grad_1, 0, 2)
    (acc,) = down_call(0, 0, tie(order, grad_1), [gb_0], store_0[2])
    near_rows = swap(grad_1, 0, 1)
    (acc_b,) = down_call(0, 1, tie(order, acc), [cotangent], store_0[2])
    (down_sum,) = down_call(1, 1, order, [cotangent], store_1[2], acc_b)
    far_rows, near_rows, down_sum = tie_all(far_rows, near_rows, down_sum)
    down_sum, gb_1 = down_call(1, 0, order, [grad_1, near_rows, far_rows, swap(far_rows, 0, 1)], store_1[2], acc, down_sum)
    down = scatter(down_sum)
    back_1, ends_1, sums_1, _ = backward(1, 0, down_sum, [gb_1], tokens, store_1, [store_1[3], *back_1, *ends_1, sums_1])
    rest_sum = jnp.concatenate([
        weight_grad([(store_0[1], back_0[0]), (store_1[1], back_1[0])]).astype(BF),
        weight_grad([(store_0[0], back_0[1]), (store_1[0], back_1[1])]).astype(BF)], axis=1)
    down, rest_sum = tie_all(down, rest_sum)
    rest = scatter(rest_sum)
    up, query, key, value = unpack_call(rest, (f, e, e, e))
    shift = jnp.where(section == 0, 0.0, down_bias[0])
    ends = []
    for parts in (ends_0, ends_1):
        keep, send, own, _ = tie_all(*parts, rest_sum)
        near, sent = near_sum((keep, send), None)
        ends.append(own.astype(F32) + near + swap(sent, None, 2).astype(F32) + shift)
    ends = jnp.stack(ends)[None, :, None]
    down = down.astype(F32).T
    small = all_sum(sums_0 + sums_1, "dp")
    group = lax.axis_size("dp")
    place = lax.axis_index("dp")
    cut = all_sum(lax.dynamic_slice(small, (0, place * (d // group)), (5, d // group)), "tensor")
    scale_cut = lax.dynamic_slice(small[5, :e].reshape(hc, hd), (0, place * (hd // group)), (hc, hd // group))
    return (
        ends, cut[0:1], cut[1:2], cut[2:3], cut[3:4],
        query, key, value, down[None, f:], scale_cut[None], up, down[None, :f],
        cut[4:5] / teams,
    )


def solution(mesh):
    return jax.shard_map(
        body,
        mesh=mesh,
        in_specs=(
            P(None, "dp", None, None), P(None, "dp", None, None), P(None, "dp"),
            P("section", None), P("section", None), P("section", None), P("section", None),
            P("section", None, "tensor"), P("section", None, "tensor"), P("section", None, "tensor"),
            P("section", "tensor", None), P("section", "tensor", None), P("section", None, "tensor"),
            P("section", "tensor", None), P("section", None),
        ),
        out_specs=(
            P("section", None, "dp", "tensor", None),
            P("section", "dp"), P("section", "dp"), P("section", "dp"), P("section", "dp"),
            P("section", "dp", "tensor"), P("section", "dp", "tensor"), P("section", "dp", "tensor"),
            P("section", "tensor", "dp"), P("section", "tensor", "dp"), P("section", "dp", "tensor"),
            P("section", "tensor", "dp"), P("section", "dp"),
        ),
        check_vma=False,
    )
```

time: 615 us -> 381 us (0.62)
  waiting for transfers between devices: 307 us -> 165 us
  blocking collectives: 41.8 us -> 0 us
  local copies, waits for them, and re-layouts: 33.1 us -> 13.4 us
  Pallas kernels: 109 us -> 95.8 us
  matrix products: 23.7 us -> 10.5 us
    ppermute x32 -> x26, waiting for transfers between devices: 253 us -> 85.8 us  [the longest x4 27.9 us: relay(): lax.ppermute(sent, both, pairs[1])]
    psum x2 -> x0, blocking collectives: 41.8 us -> none  [body(): rows_small = lax.psum(lax.psum(small[:5], 'tensor'), 'dp')]
    all_gather x0 -> x2, waiting for transfers between devices: none -> 36.3 us  [whole_rows(): return lax.all_gather(own, 'tensor', axis=0, tiled=True)]
    pallas_call x8 -> x15, Pallas kernels: 109 us -> 95.8 us  [the longest x4 40.8 us: backward_call(): pl.pallas_call(functools.partial(backward_kernel, cfg), out_shape=shapes,...]
    dot_general x6 -> x4, matrix products: 23.7 us -> 10.5 us  [dot_tn(): lax.dot_general(a, b, (((0,), (0,)), ((), ())), preferred_element_type=F32)]
    convert_element_type x4 -> x12, other arithmetic: 2.85 us -> 15.6 us  [the longest x6 9.53 us: near_sum(): (keep[1].astype(F32) + got[1].astype(F32)).astype(BF)]
    reduce_scatter x3 -> x2, waiting for transfers between devices: 54.4 us -> 43.3 us  [scatter(): return lax.psum_scatter(total, 'dp', scatter_dimension=0, tiled=True)]
    squeeze x8 -> x3, local copies, waits for them, and re-layouts: 8.29 us -> 0.16 us  [own_rows(): lax.dynamic_index_in_dim(x.reshape(teams, rows // teams, d), tensor, 0, k...]
  transfers between devices with their start and end apart: 35 -> 30, of which waited for: 12 -> 19; matrix products, arithmetic and copies ran while one was open for 7% -> 11% of each run, Pallas kernels for 9% -> 18%
where the time goes in v3:
time: 381 us; the launch traced here: 374 us
  waiting for transfers between devices  165 us (43%)
  Pallas kernels  95.8 us (25%)
  starting transfers between devices  51.7 us (14%)
  other arithmetic  22.6 us (6%)
  between operations  15 us (4%)
  local copies, waits for them, and re-layouts  13.4 us (4%)
  matrix products  10.5 us (3%)
    reduce_scatter x2, waiting for transfers between devices, scatter(): return lax.psum_scatter(total, 'dp', scatter_dimension=0, tiled=True)  43.3 us
    pallas_call x4, Pallas kernels, backward_call(): pl.pallas_call(functools.partial(backward_kernel, cfg), out_shape=shapes,...  40.8 us
    pallas_call x4, Pallas kernels, forward_call(): pl.pallas_call(functools.partial(forward_kernel, cfg), out_shape=shapes,...  37.6 us
    all_gather x2, waiting for transfers between devices, whole_rows(): return lax.all_gather(own, 'tensor', axis=0, tiled=True)  36.3 us
    ppermute x4, waiting for transfers between devices, relay(): lax.ppermute(sent, both, pairs[1])  27.9 us
    ppermute x4, waiting for transfers between devices, relay(): lax.ppermute(near, both, pairs[0])  25.7 us
    ppermute x4, starting transfers between devices, relay(): lax.ppermute(near, both, pairs[0])  23.3 us
    ppermute x14, waiting for transfers between devices, swap(): lax.ppermute(x, both, [(k * teams + i, k * teams + (i ^ bit)) for k in se...  22.6 us
  transfers between devices with their start and end apart: 30, of which 19 were waited for; matrix products, arithmetic and copies ran while one was open for 11% of the time, Pallas kernels for 18%

profile of v3, /device:TPU:0, one launch (start us, length us, event | category | flops | bytes accessed | tf_op | source)
XLA Modules:
  0.0 374.4 jit_solution(2788470178414706142)
XLA Ops:
  7.2 1.3 copy.69.refs_16_.refs_19_.refs_17_
  8.5 18.0 %forward.4 = (bf16[1024,1024]{1,0:T(8,128)(2,1)}, bf16[1024,1024]{1,0:T(8,128)(2,1)}, bf16[1024,1280]{1,0:T(8,128)(2,1)}, bf16[1024,1024]{1,0:T(8,128)(2,1)}, f3...) custom-call(f32[1,1024]{1,0:T(1,128)} %refs_8_.15, ...), custom_call_target="tpu_custom_call" | custom-call | flops 6442450944 | bytes 26214400 | tf_op jit(solution)/shard_map/forward/pallas_call | solution.py:495
  26.5 2.3 collective-permute-start
  28.9 2.8 fusion.17
  31.7 1.2 fusion.7
  32.9 2.1 collective-permute-start.1
  35.0 1.2 fusion.8
  36.3 2.1 collective-permute-start.2
  38.4 18.1 %forward.5 = (bf16[1024,1024]{1,0:T(8,128)(2,1)}, bf16[1024,1024]{1,0:T(8,128)(2,1)}, bf16[1024,1280]{1,0:T(8,128)(2,1)}, bf16[1024,1024]{1,0:T(8,128)(2,1)}, f3...) custom-call(f32[1,1024]{1,0:T(1,128)} %refs_8_.15, ...), custom_call_target="tpu_custom_call" | custom-call | flops 6442450944 | bytes 26214400 | tf_op jit(solution)/shard_map/forward/pallas_call | solution.py:495
  57.2 1.9 collective-permute-start.3
  59.1 1.5 add_convert_fusion.11.refs_0_
  62.0 1.0 fusion.9
  63.0 1.0 fusion.6
  66.0 18.6 %collective-permute-start.4 = (bf16[256,1024]{1,0:T(8,128)(2,1)}, bf16[256,1024]{1,0:T(8,128)(2,1)S(1)}, u32[]{:S(2)}, u32[]{:S(2)}) collective-permute-start(bf16[256,1024]{1,0:T(8,128)(2,1)} %fusion.6), channel_id=1, source_target_pairs={{0,16},{1,17},{2,18},{3,19},{4,20},{5,21},{6,22},{7,23},{8,24},{9,... | collective-permute-start | bytes 1572872 | tf_op jit(solution)/shard_map/ppermute | solution.py:746
  84.7 1.3 collective-permute-start.5
  87.6 9.6 %collective-permute-done.4 = bf16[256,1024]{1,0:T(8,128)(2,1)S(1)} collective-permute-done((bf16[256,1024]{1,0:T(8,128)(2,1)}, bf16[256,1024]{1,0:T(8,128)(2,1)S(1)}, u32[]{:S(2)}, u32[]{:S(2)}) %collective-permute-start.4) | collective-permute-done | bytes 524320 | tf_op jit(solution)/shard_map/ppermute | solution.py:746
  97.2 10.8 %collective-permute-done.5 = bf16[256,1024]{1,0:T(8,128)(2,1)S(1)} collective-permute-done((bf16[256,1024]{1,0:T(8,128)(2,1)}, bf16[256,1024]{1,0:T(8,128)(2,1)S(1)}, u32[]{:S(2)}, u32[]{:S(2)}) %collective-permute-start.5) | collective-permute-done | bytes 524320 | tf_op jit(solution)/shard_map/ppermute | solution.py:746
  108.0 1.0 add_convert_fusion.10
  110.7 1.6 fusion.11
  112.3 1.3 collective-permute-start.11
  113.6 1.3 collective-permute-start.10
  114.9 19.0 %all-gather.3.cloned.1.call-done.refs_0_ = bf16[1024,1024]{1,0:T(8,128)(2,1)} async-done(((bf16[256,1024]{1,0:T(8,128)(2,1)}), bf16[1024,1024]{1,0:T(8,128)(2,1)}) %all-gather.3.cloned.1.call-update) | async-done | bytes 2097168 | tf_op jit(solution)/shard_map/all_gather | solution.py:752
  134.7 16.3 %collective-permute-done.11 = bf16[256,1024]{1,0:T(8,128)(2,1)S(1)} collective-permute-done((bf16[256,1024]{1,0:T(8,128)(2,1)S(1)}, bf16[256,1024]{1,0:T(8,128)(2,1)S(1)}, u32[]{:S(2)}, u32[]{:S(2)}) %collective-permute-start.11) | collective-permute-done | bytes 524320 | tf_op jit(solution)/shard_map/ppermute | solution.py:746
  151.1 9.6 %collective-permute-done.10 = bf16[256,1024]{1,0:T(8,128)(2,1)S(1)} collective-permute-done((bf16[256,1024]{1,0:T(8,128)(2,1)S(1)}, bf16[256,1024]{1,0:T(8,128)(2,1)S(1)}, u32[]{:S(2)}, u32[]{:S(2)}) %collective-permute-start.10) | collective-permute-done | bytes 524320 | tf_op jit(solution)/shard_map/ppermute | solution.py:746
  160.6 1.1 add_convert_fusion.7
  161.8 1.0 backward.5
  163.6 1.6 fusion.13
  165.2 1.3 collective-permute-start.14
  166.5 1.3 collective-permute-start.13
  167.8 17.2 %all-gather.5.cloned.1.call-done.refs_0_ = bf16[1024,1024]{1,0:T(8,128)(2,1)} async-done(((bf16[256,1024]{1,0:T(8,128)(2,1)}), bf16[1024,1024]{1,0:T(8,128)(2,1)}) %all-gather.5.cloned.1.call-update) | async-done | bytes 2097168 | tf_op jit(solution)/shard_map/all_gather | solution.py:752
  185.1 19.4 %backward.6 = (bf16[1024,1024]{1,0:T(8,128)(2,1)}, bf16[1024,768]{1,0:T(8,128)(2,1)}, bf16[2,256,1024]{2,1,0:T(8,128)(2,1)}, bf16[2,256,1024]{2,1,0:T(8,128)(2,1...) custom-call(f32[1,1024]{1,0:T(1,128)} %refs_8_.15, ...), custom_call_target="tpu_custom_call", output_to_operand_aliasing={{0}: (26, {}), {1}: (27, {}), {2}: (28, {}), {3}: (29, {}),... | custom-call | flops 6442450944 | bytes 31457280 | tf_op jit(solution)/shard_map/backward/pallas_call | solution.py:527
  204.5 6.6 %collective-permute-done.13 = bf16[256,1024]{1,0:T(8,128)(2,1)S(1)} collective-permute-done((bf16[256,1024]{1,0:T(8,128)(2,1)S(1)}, bf16[256,1024]{1,0:T(8,128)(2,1)S(1)}, u32[]{:S(2)}, u32[]{:S(2)}) %collective-permute-start.13) | collective-permute-done | bytes 524320 | tf_op jit(solution)/shard_map/ppermute | solution.py:746
  211.4 1.9 collective-permute-start.16
  213.3 3.6 collective-permute-start.15
  216.9 6.9 %down.4.refs_5_ = bf16[1024,1280]{1,0:T(8,128)(2,1)} custom-call(f32[1,1024]{1,0:T(1,128)} %refs_8_.15, bf16[1024,1024]{1,0:T(8,128)(2,1)} %all-gather.5.cloned.1.call-done.refs_0_, bf16[1024,1280]{1,0:T(8,128)(2,1)} %get-tuple-element.222.am.refs_1_), custom_call_target="tpu_custom_call" | custom-call | tf_op jit(solution)/shard_map/down/pallas_call | solution.py:690
  224.0 5.6 %collective-permute-done.15.refs_2_ = bf16[256,1024]{1,0:T(8,128)(2,1)S(1)} collective-permute-done((bf16[256,1024]{1,0:T(8,128)(2,1)S(1)}, bf16[256,1024]{1,0:T(8,128)(2,1)S(1)}, u32[]{:S(2)}, u32[]{:S(2)}) %collective-permute-start.15) | collective-permute-done | bytes 524320 | tf_op jit(solution)/shard_map/ppermute | solution.py:722
  229.5 1.9 collective-permute-start.17
  231.4 1.9 collective-permute-done.17.refs_3_
  234.1 7.8 %down.7 = (bf16[1024,1280]{1,0:T(8,128)(2,1)}, bf16[1024,1024]{1,0:T(8,128)(2,1)}) custom-call(f32[1,1024]{1,0:T(1,128)} %refs_8_.15, bf16[256,1024]{1,0:T(8,128)(2,1)} %copy-done.10, bf16[256,1024]{1,0:T(8,128)(2,1)} %copy-done.19, bf16[256,1024]{1,0:T(8,128)(2,1)} %copy-done.20, bf16[256,1024]{1,0:T(8,128)(2,1)} %copy-done.21, ...), custom_call_target="tpu_custom_call", output_to_operand_aliasing={{0}: (7, {})} | custom-call | flops 2684354560 | bytes 12582912 | tf_op jit(solution)/shard_map/down/pallas_call | solution.py:690
  242.1 19.6 %backward.7 = (bf16[1024,1024]{1,0:T(8,128)(2,1)}, bf16[1024,768]{1,0:T(8,128)(2,1)}, bf16[2,256,1024]{2,1,0:T(8,128)(2,1)}, bf16[2,256,1024]{2,1,0:T(8,128)(2,1...) custom-call(f32[1,1024]{1,0:T(1,128)} %refs_8_.15, ...), custom_call_target="tpu_custom_call", output_to_operand_aliasing={{0}: (26, {}), {1}: (27, {}), {2}: (28, {}), {3}: (29, {}),... | custom-call | flops 6442450944 | bytes 31457280 | tf_op jit(solution)/shard_map/backward/pallas_call | solution.py:527
  261.6 3.5 fusion.19
  265.2 2.4 fusion.18
  267.7 2.0 add_convert_fusion.1
  269.9 2.6 add_convert_fusion
  272.4 2.1 pad_maximum_fusion
  274.5 20.2 %reduce-scatter.3.cloned.1.call-done = bf16[256,1280]{1,0:T(8,128)(2,1)} async-done(((bf16[1024,1280]{1,0:T(8,128)(2,1)}), bf16[256,1280]{1,0:T(8,128)(2,1)}) %reduce-scatter.3.cloned.1.call-update) | async-done | bytes 655376 | tf_op jit(solution)/shard_map/reduce_scatter | solution.py:770
  295.6 3.3 collective-permute-done.22
  298.9 2.1 collective-permute-start.23
  300.9 3.1 collective-permute-done.23
  304.7 1.7 collective-permute-done.24
  306.4 1.5 collective-permute-start.25
  308.5 1.5 collective-permute-done.25
  310.7 2.0 fusion.14
  312.7 1.5 collective-permute-start.19
  314.2 2.0 fusion.15
  316.9 1.1 slice_bitcast_fusion
  318.0 2.5 copy.83
  321.2 1.8 copy.82
  323.0 4.8 %collective-permute-done.19 = bf16[256,1024]{1,0:T(8,128)(2,1)} collective-permute-done((bf16[256,1024]{1,0:T(8,128)(2,1)}, bf16[256,1024]{1,0:T(8,128)(2,1)}, u32[]{:S(2)}, u32[]{:S(2)}) %collective-permute-start.19) | collective-permute-done | bytes 524320 | tf_op jit(solution)/shard_map/ppermute | solution.py:722
  327.9 9.8 %collective-permute-done.21 = bf16[256,1024]{1,0:T(8,128)(2,1)} collective-permute-done((bf16[256,1024]{1,0:T(8,128)(2,1)}, bf16[256,1024]{1,0:T(8,128)(2,1)}, u32[]{:S(2)}, u32[]{:S(2)}) %collective-permute-start.21) | collective-permute-done | bytes 524320 | tf_op jit(solution)/shard_map/ppermute | solution.py:722
  337.7 2.7 fusion.5
  340.4 1.5 maximum_bitcast_fusion
  341.9 23.1 %reduce-scatter.5.cloned.1.call-done.packed = bf16[256,1792]{1,0:T(8,128)(2,1)} async-done(((bf16[1024,1792]{1,0:T(8,128)(2,1)}), bf16[256,1792]{1,0:T(8,128)(2,1)}) %reduce-scatter.5.cloned.1.call-update) | async-done | bytes 917520 | tf_op jit(solution)/shard_map/reduce_scatter | solution.py:770
  365.0 2.4 unpack.1
  (106 shorter events, 14.7 us)
Async XLA Ops:
  7.2 126.7 %all-gather.3.cloned.1.call-start = ((), (), s32[]{:S(2)}) async-start(), calls=%async_computation.2 | async-start | bytes 2621440 | tf_op jit(solution)/shard_map/all_gather | solution.py:752
  26.5 5.2 %collective-permute-start = (bf16[2,256,1024]{2,1,0:T(8,128)(2,1)}, bf16[2,256,1024]{2,1,0:T(8,128)(2,1)}, u32[]{:S(2)}, u32[]{:S(2)}) collective-permute-start(bf16[2,256,1024]{2,1,0:T(8,128)(2,1)} %get-tuple-element.144), channel_id=1, source_target_pairs={{0,1},{1,0},{2,3},{3,2},{4,5},{5,4},{6,7},{7,6},{8,9},{9,8},{10,11... | collective-permute-start | bytes 3145736 | tf_op jit(solution)/shard_map/ppermute | solution.py:722
  28.8 2.8 copy-start.12
  28.9 2.8 copy-start.24
  32.9 23.5 %collective-permute-start.1 = (bf16[256,1024]{1,0:T(8,128)(2,1)S(1)}, bf16[256,1024]{1,0:T(8,128)(2,1)}, u32[]{:S(2)}, u32[]{:S(2)}) collective-permute-start(bf16[256,1024]{1,0:T(8,128)(2,1)S(1)} %fusion.7), channel_id=1, source_target_pairs={{0,16},{1,17},{2,18},{3,19},{4,20},{5,21},{6,22},{7,23},{8,24},{9,... | collective-permute-start | bytes 1572872 | tf_op jit(solution)/shard_map/ppermute | solution.py:746
  36.3 20.9 %collective-permute-start.2 = (bf16[256,1024]{1,0:T(8,128)(2,1)S(1)}, bf16[256,1024]{1,0:T(8,128)(2,1)}, u32[]{:S(2)}, u32[]{:S(2)}) collective-permute-start(bf16[256,1024]{1,0:T(8,128)(2,1)S(1)} %fusion.8), channel_id=1, source_target_pairs={{0,18},{1,19},{2,16},{3,17},{4,22},{5,23},{6,20},{7,21},{8,26},{9,... | collective-permute-start | bytes 1572872 | tf_op jit(solution)/shard_map/ppermute | solution.py:746
  56.5 5.5 %copy-start.13 = (bf16[2,256,1024]{2,1,0:T(8,128)(2,1)S(1)}, bf16[2,256,1024]{2,1,0:T(8,128)(2,1)}, u32[]{:S(2)}) copy-start(bf16[2,256,1024]{2,1,0:T(8,128)(2,1)} %get-tuple-element.148) | copy-start | bytes 3145732
  57.2 4.8 %collective-permute-start.3 = (bf16[2,256,1024]{2,1,0:T(8,128)(2,1)}, bf16[2,256,1024]{2,1,0:T(8,128)(2,1)S(1)}, u32[]{:S(2)}, u32[]{:S(2)}) collective-permute-start(bf16[2,256,1024]{2,1,0:T(8,128)(2,1)} %get-tuple-element.149), channel_id=1, source_target_pairs={{0,1},{1,0},{2,3},{3,2},{4,5},{5,4},{6,7},{7,6},{8,9},{9,8},{10,11... | collective-permute-start | bytes 3145736 | tf_op jit(solution)/shard_map/ppermute | solution.py:722
  60.6 4.9 %copy-start.5 = (bf16[256,1024]{1,0:T(8,128)(2,1)}, bf16[256,1024]{1,0:T(8,128)(2,1)S(1)}, u32[]{:S(2)}) copy-start(bf16[256,1024]{1,0:T(8,128)(2,1)S(1)} %add_convert_fusion.11.refs_0_) | copy-start | bytes 1572868
  60.6 4.9 %copy-start = (bf16[2,1,1024,1024]{3,2,1,0:T(8,128)(2,1)S(1)}, bf16[2,1,1024,1024]{3,2,1,0:T(8,128)(2,1)}, u32[]{:S(2)}) copy-start(bf16[2,1,1024,1024]{3,2,1,0:T(8,128)(2,1)} %refs_0_.11) | copy-start | bytes 12582916
  60.6 4.1 %collective-permute-start.6 = (bf16[256,1024]{1,0:T(8,128)(2,1)S(1)}, bf16[256,1024]{1,0:T(8,128)(2,1)S(1)}, u32[]{:S(2)}, u32[]{:S(2)}) collective-permute-start(bf16[256,1024]{1,0:T(8,128)(2,1)S(1)} %add_convert_fusion.11.refs_0_), channel_id=1, source_target_pairs={{16,18},{17,19},{18,16},{19,17},{20,22},{21,23},{22,20},{23,21},{2... | collective-permute-start | bytes 1572872 | tf_op jit(solution)/shard_map/ppermute | solution.py:722
  64.0 0.7 collective-permute-start.7
  64.7 1.3 copy-start.16
  64.7 1.2 copy-start.17
  64.7 21.3 %collective-permute-start.8 = (bf16[256,1024]{1,0:T(8,128)(2,1)S(1)}, bf16[256,1024]{1,0:T(8,128)(2,1)S(1)}, u32[]{:S(2)}, u32[]{:S(2)}) collective-permute-start(bf16[256,1024]{1,0:T(8,128)(2,1)S(1)} %collective-permute-done.6.refs_2_), channel_id=1, source_target_pairs={{16,17},{17,16},{18,19},{19,18},{20,21},{21,20},{22,23},{23,22},{2... | collective-permute-start | bytes 1572872 | tf_op jit(solution)/shard_map/ppermute | solution.py:722
  66.0 31.1 %collective-permute-start.4 = (bf16[256,1024]{1,0:T(8,128)(2,1)}, bf16[256,1024]{1,0:T(8,128)(2,1)S(1)}, u32[]{:S(2)}, u32[]{:S(2)}) collective-permute-start(bf16[256,1024]{1,0:T(8,128)(2,1)} %fusion.6), channel_id=1, source_target_pairs={{0,16},{1,17},{2,18},{3,19},{4,20},{5,21},{6,22},{7,23},{8,24},{9,... | collective-permute-start | bytes 1572872 | tf_op jit(solution)/shard_map/ppermute | solution.py:746
  84.7 23.3 %collective-permute-start.5 = (bf16[256,1024]{1,0:T(8,128)(2,1)}, bf16[256,1024]{1,0:T(8,128)(2,1)S(1)}, u32[]{:S(2)}, u32[]{:S(2)}) collective-permute-start(bf16[256,1024]{1,0:T(8,128)(2,1)} %fusion.9), channel_id=1, source_target_pairs={{0,18},{1,19},{2,16},{3,17},{4,22},{5,23},{6,20},{7,21},{8,26},{9,... | collective-permute-start | bytes 1572872 | tf_op jit(solution)/shard_map/ppermute | solution.py:746
  86.0 0.8 copy-start.18
  109.1 75.9 %all-gather.5.cloned.1.call-start = ((), (), s32[]{:S(2)}) async-start(), calls=%async_computation.3 | async-start | bytes 2621440 | tf_op jit(solution)/shard_map/all_gather | solution.py:752
  109.9 0.7 collective-permute-start.9
  112.3 38.8 %collective-permute-start.11 = (bf16[256,1024]{1,0:T(8,128)(2,1)S(1)}, bf16[256,1024]{1,0:T(8,128)(2,1)S(1)}, u32[]{:S(2)}, u32[]{:S(2)}) collective-permute-start(bf16[256,1024]{1,0:T(8,128)(2,1)S(1)} %get-tuple-element.292), channel_id=1, source_target_pairs={{16,2},{17,3},{18,0},{19,1},{20,6},{21,7},{22,4},{23,5},{24,10},{2... | collective-permute-start | bytes 1572872 | tf_op jit(solution)/shard_map/ppermute | solution.py:746
  113.6 47.1 %collective-permute-start.10 = (bf16[256,1024]{1,0:T(8,128)(2,1)S(1)}, bf16[256,1024]{1,0:T(8,128)(2,1)S(1)}, u32[]{:S(2)}, u32[]{:S(2)}) collective-permute-start(bf16[256,1024]{1,0:T(8,128)(2,1)S(1)} %get-tuple-element.293), channel_id=1, source_target_pairs={{16,0},{17,1},{18,2},{19,3},{20,4},{21,5},{22,6},{23,7},{24,8},{25... | collective-permute-start | bytes 1572872 | tf_op jit(solution)/shard_map/ppermute | solution.py:746
  161.7 133.0 %reduce-scatter.3.cloned.1.call-start = ((), (), s32[]{:S(2)}) async-start(), calls=%async_computation.4 | async-start | bytes 3276800 | tf_op jit(solution)/shard_map/reduce_scatter | solution.py:770
  162.8 0.7 collective-permute-start.12
  165.2 39.3 %collective-permute-start.14 = (bf16[256,1024]{1,0:T(8,128)(2,1)S(1)}, bf16[256,1024]{1,0:T(8,128)(2,1)S(1)}, u32[]{:S(2)}, u32[]{:S(2)}) collective-permute-start(bf16[256,1024]{1,0:T(8,128)(2,1)S(1)} %get-tuple-element.290), channel_id=1, source_target_pairs={{16,2},{17,3},{18,0},{19,1},{20,6},{21,7},{22,4},{23,5},{24,10},{2... | collective-permute-start | bytes 1572872 | tf_op jit(solution)/shard_map/ppermute | solution.py:746
  166.5 44.6 %collective-permute-start.13 = (bf16[256,1024]{1,0:T(8,128)(2,1)S(1)}, bf16[256,1024]{1,0:T(8,128)(2,1)S(1)}, u32[]{:S(2)}, u32[]{:S(2)}) collective-permute-start(bf16[256,1024]{1,0:T(8,128)(2,1)S(1)} %get-tuple-element.291), channel_id=1, source_target_pairs={{16,0},{17,1},{18,2},{19,3},{20,4},{21,5},{22,6},{23,7},{24,8},{25... | collective-permute-start | bytes 1572872 | tf_op jit(solution)/shard_map/ppermute | solution.py:746
  211.4 12.4 %copy-start.10 = (bf16[256,1024]{1,0:T(8,128)(2,1)}, bf16[256,1024]{1,0:T(8,128)(2,1)S(1)}, u32[]{:S(2)}) copy-start(bf16[256,1024]{1,0:T(8,128)(2,1)S(1)} %add_convert_fusion.4.refs_0_) | copy-start | bytes 1572868
  211.4 12.6 %collective-permute-start.16 = (bf16[256,1024]{1,0:T(8,128)(2,1)S(1)}, bf16[256,1024]{1,0:T(8,128)(2,1)S(1)}, u32[]{:S(2)}, u32[]{:S(2)}) collective-permute-start(bf16[256,1024]{1,0:T(8,128)(2,1)S(1)} %add_convert_fusion.4.refs_0_), channel_id=1, source_target_pairs={{0,1},{1,0},{2,3},{3,2},{4,5},{5,4},{6,7},{7,6},{8,9},{9,8},{10,11... | collective-permute-start | bytes 1572872 | tf_op jit(solution)/shard_map/ppermute | solution.py:722
  213.3 16.2 %collective-permute-start.15 = (bf16[256,1024]{1,0:T(8,128)(2,1)S(1)}, bf16[256,1024]{1,0:T(8,128)(2,1)S(1)}, u32[]{:S(2)}, u32[]{:S(2)}) collective-permute-start(bf16[256,1024]{1,0:T(8,128)(2,1)S(1)} %add_convert_fusion.4.refs_0_), channel_id=1, source_target_pairs={{0,2},{1,3},{2,0},{3,1},{4,6},{5,7},{6,4},{7,5},{8,10},{9,11},{10,... | collective-permute-start | bytes 1572872 | tf_op jit(solution)/shard_map/ppermute | solution.py:722
  224.0 9.4 %copy-start.19 = (bf16[256,1024]{1,0:T(8,128)(2,1)}, bf16[256,1024]{1,0:T(8,128)(2,1)S(1)}, u32[]{:S(2)}) copy-start(bf16[256,1024]{1,0:T(8,128)(2,1)S(1)} %collective-permute-done.16.refs_1_) | copy-start | bytes 1572868
  229.5 3.8 %copy-start.20 = (bf16[256,1024]{1,0:T(8,128)(2,1)}, bf16[256,1024]{1,0:T(8,128)(2,1)S(1)}, u32[]{:S(2)}) copy-start(bf16[256,1024]{1,0:T(8,128)(2,1)S(1)} %collective-permute-done.15.refs_2_) | copy-start | bytes 1572868
  229.5 3.8 %collective-permute-start.17 = (bf16[256,1024]{1,0:T(8,128)(2,1)S(1)}, bf16[256,1024]{1,0:T(8,128)(2,1)S(1)}, u32[]{:S(2)}, u32[]{:S(2)}) collective-permute-start(bf16[256,1024]{1,0:T(8,128)(2,1)S(1)} %collective-permute-done.15.refs_2_), channel_id=1, source_target_pairs={{0,1},{1,0},{2,3},{3,2},{4,5},{5,4},{6,7},{7,6},{8,9},{9,8},{10,11... | collective-permute-start | bytes 1572872 | tf_op jit(solution)/shard_map/ppermute | solution.py:722
  233.3 0.8 copy-start.21
  241.9 123.1 %reduce-scatter.5.cloned.1.call-start = ((), (), s32[]{:S(2)}) async-start(), calls=%async_computation.5 | async-start | bytes 4587520 | tf_op jit(solution)/shard_map/reduce_scatter | solution.py:770
  242.0 19.6 %copy-start.6 = (bf16[1024,1024]{1,0:T(8,128)(2,1)S(1)}, bf16[1024,1024]{1,0:T(8,128)(2,1)}, u32[]{:S(2)}) copy-start(bf16[1024,1024]{1,0:T(8,128)(2,1)} %get-tuple-element.254) | copy-start | bytes 6291460
  261.6 3.5 copy-start.1
  261.6 3.5 copy-start.7
  265.1 2.5 copy-start.8
  265.1 2.5 copy-start.11
  267.6 2.0 copy-start.2
  267.6 2.2 copy-start.9
  274.5 20.3 %copy-start.22 = (f32[8,1024]{1,0:T(8,128)S(1)}, f32[8,1024]{1,0:T(8,128)}, u32[]{:S(2)}) copy-start(f32[8,1024]{1,0:T(8,128)} %get-tuple-element.266) | copy-start | bytes 98308
  274.5 20.3 %copy-start.23 = (f32[8,1024]{1,0:T(8,128)S(1)}, f32[8,1024]{1,0:T(8,128)}, u32[]{:S(2)}) copy-start(f32[8,1024]{1,0:T(8,128)} %get-tuple-element.267) | copy-start | bytes 98308
  274.5 29.5 %copy-start.14 = (bf16[2,256,1024]{2,1,0:T(8,128)(2,1)S(1)}, bf16[2,256,1024]{2,1,0:T(8,128)(2,1)}, u32[]{:S(2)}) copy-start(bf16[2,256,1024]{2,1,0:T(8,128)(2,1)} %get-tuple-element.265) | copy-start | bytes 3145732
  274.5 36.2 %copy-start.4 = (bf16[2,256,1024]{2,1,0:T(8,128)(2,1)S(1)}, bf16[2,256,1024]{2,1,0:T(8,128)(2,1)}, u32[]{:S(2)}) copy-start(bf16[2,256,1024]{2,1,0:T(8,128)(2,1)} %get-tuple-element.258) | copy-start | bytes 3145732
  274.5 39.7 %copy-start.3 = (bf16[2,256,1024]{2,1,0:T(8,128)(2,1)S(1)}, bf16[2,256,1024]{2,1,0:T(8,128)(2,1)}, u32[]{:S(2)}) copy-start(bf16[2,256,1024]{2,1,0:T(8,128)(2,1)} %get-tuple-element.264) | copy-start | bytes 3145732
  294.8 15.9 %collective-permute-start.18 = (bf16[2,256,1024]{2,1,0:T(8,128)(2,1)}, bf16[2,256,1024]{2,1,0:T(8,128)(2,1)}, u32[]{:S(2)}, u32[]{:S(2)}) collective-permute-start(bf16[2,256,1024]{2,1,0:T(8,128)(2,1)} %get-tuple-element.259), channel_id=1, source_target_pairs={{0,1},{1,0},{2,3},{3,2},{16,17},{17,16},{18,19},{19,18},{4,5},{5,4... | collective-permute-start | bytes 3145736 | tf_op jit(solution)/shard_map/ppermute | solution.py:722
  294.9 4.0 %collective-permute-start.22 = (f32[8,1024]{1,0:T(8,128)S(1)}, f32[8,1024]{1,0:T(8,128)S(1)}, u32[]{:S(2)}, u32[]{:S(2)}) collective-permute-start(f32[8,1024]{1,0:T(8,128)S(1)} %add.201), channel_id=1, source_target_pairs={{0,4},{4,0},{8,12},{12,8},{1,5},{5,1},{9,13},{13,9},{2,6},{6,2},{1... | collective-permute-start | bytes 98312 | tf_op jit(solution)/shard_map/ppermute | solution.py:762
  298.9 5.2 %collective-permute-start.23 = (f32[8,1024]{1,0:T(8,128)S(1)}, f32[8,1024]{1,0:T(8,128)S(1)}, u32[]{:S(2)}, u32[]{:S(2)}) collective-permute-start(f32[8,1024]{1,0:T(8,128)S(1)} %add.202), channel_id=1, source_target_pairs={{0,8},{4,12},{8,0},{12,4},{1,9},{5,13},{9,1},{13,5},{2,10},{6,14},... | collective-permute-start | bytes 98312 | tf_op jit(solution)/shard_map/ppermute | solution.py:762
  304.0 10.2 %collective-permute-start.20 = (bf16[2,256,1024]{2,1,0:T(8,128)(2,1)S(1)}, bf16[2,256,1024]{2,1,0:T(8,128)(2,1)}, u32[]{:S(2)}, u32[]{:S(2)}) collective-permute-start(bf16[2,256,1024]{2,1,0:T(8,128)(2,1)S(1)} %copy-done.14), channel_id=1, source_target_pairs={{0,1},{1,0},{2,3},{3,2},{16,17},{17,16},{18,19},{19,18},{4,5},{5,4... | collective-permute-start | bytes 3145736 | tf_op jit(solution)/shard_map/ppermute | solution.py:722
  304.1 2.3 collective-permute-start.24
  304.7 12.1 %copy-start.15 = (bf16[256,1280]{1,0:T(8,128)(2,1)S(1)}, bf16[256,1280]{1,0:T(8,128)(2,1)}, u32[]{:S(2)}) copy-start(bf16[256,1280]{1,0:T(8,128)(2,1)} %reduce-scatter.3.cloned.1.call-done) | copy-start | bytes 1966084
  306.4 3.7 collective-permute-start.25
  312.7 15.2 %collective-permute-start.19 = (bf16[256,1024]{1,0:T(8,128)(2,1)}, bf16[256,1024]{1,0:T(8,128)(2,1)}, u32[]{:S(2)}, u32[]{:S(2)}) collective-permute-start(bf16[256,1024]{1,0:T(8,128)(2,1)} %fusion.14), channel_id=1, source_target_pairs={{0,2},{1,3},{2,0},{3,1},{16,18},{17,19},{18,16},{19,17},{4,6},{5,7... | collective-permute-start | bytes 1572872 | tf_op jit(solution)/shard_map/ppermute | solution.py:722
  316.2 21.5 %collective-permute-start.21 = (bf16[256,1024]{1,0:T(8,128)(2,1)}, bf16[256,1024]{1,0:T(8,128)(2,1)}, u32[]{:S(2)}, u32[]{:S(2)}) collective-permute-start(bf16[256,1024]{1,0:T(8,128)(2,1)} %fusion.15), channel_id=1, source_target_pairs={{0,2},{1,3},{2,0},{3,1},{16,18},{17,19},{18,16},{19,17},{4,6},{5,7... | collective-permute-start | bytes 1572872 | tf_op jit(solution)/shard_map/ppermute | solution.py:722
Sparse Core Ops, SparseCore 0:
  109.2 24.6 all-gather.2
  161.8 23.1 all-gather.4
  242.0 52.6 reduce-scatter.2
  296.9 68.0 reduce-scatter.4

commit v4 on v3

--- a/solution.py
+++ b/solution.py
@@ -784,7 +784,7 @@
     took, after = relay(parts, 0)
     near_rows = swap(tie(row_0, *after), 1, 1)
     far_rows, near_rows = tie_all(far_rows, near_rows)
-    store_0, own_0, mix_0 = forward_call(sizes, 0, 1, tie(order, *after), [row_0, near_rows, far_rows, swap(far_rows, 1, 1)], weights, tabs, store_0, cotangent=cotangent)
+    store_0, own_0, mix_0 = forward_call(sizes, 0, 1, tie(order, *after, took[0]), [row_0, near_rows, far_rows, swap(far_rows, 1, 1)], weights, tabs, store_0, cotangent=cotangent)
     own_c = [own_rows(cotangent[m, 0]) for m in range(2)]
     *took, own_0, own_t, own_c[0], own_c[1] = tie_all(*took, own_0, own_rows(tokens[1, 0]), *own_c)
     row_1 = summed(own_t, took).astype(BF)

time: 381 us -> 375 us (0.984)
    ppermute x4, starting transfers between devices: 23.3 us -> 12.1 us  [relay(): lax.ppermute(near, both, pairs[0])]
    ppermute x4, waiting for transfers between devices: 25.7 us -> 15.3 us  [relay(): lax.ppermute(near, both, pairs[0])]
    ppermute x4, starting transfers between devices: 6.02 us -> 15.4 us  [relay(): lax.ppermute(sent, both, pairs[1])]
    all_gather x2, waiting for transfers between devices: 36.3 us -> 42.1 us  [whole_rows(): return lax.all_gather(own, 'tensor', axis=0, tiled=True)]
    unnamed x53 -> x57, local copies, waits for them, and re-layouts: 7.47 us -> 7.64 us
  transfers between devices with their start and end apart: 30 -> 30, of which waited for: 19 -> 18; matrix products, arithmetic and copies ran while one was open for 11% -> 10% of each run, Pallas kernels for 18% -> 18%
where the time goes in v4:
time: 375 us; the launch traced here: 368 us
  waiting for transfers between devices  162 us (43%)
  Pallas kernels  96 us (26%)
  starting transfers between devices  50.3 us (13%)
  other arithmetic  21.2 us (6%)
  between operations  15 us (4%)
  local copies, waits for them, and re-layouts  13.6 us (4%)
  matrix products  10.5 us (3%)
    reduce_scatter x2, waiting for transfers between devices, scatter(): return lax.psum_scatter(total, 'dp', scatter_dimension=0, tiled=True)  43.4 us
    all_gather x2, waiting for transfers between devices, whole_rows(): return lax.all_gather(own, 'tensor', axis=0, tiled=True)  42.1 us
    pallas_call x4, Pallas kernels, backward_call(): pl.pallas_call(functools.partial(backward_kernel, cfg), out_shape=shapes,...  40.8 us
    pallas_call x4, Pallas kernels, forward_call(): pl.pallas_call(functools.partial(forward_kernel, cfg), out_shape=shapes,...  37.8 us
    ppermute x4, waiting for transfers between devices, relay(): lax.ppermute(sent, both, pairs[1])  28.6 us
    ppermute x14, waiting for transfers between devices, swap(): lax.ppermute(x, both, [(k * teams + i, k * teams + (i ^ bit)) for k in se...  22.7 us
    ppermute x14, starting transfers between devices, swap(): lax.ppermute(x, both, [(k * teams + i, k * teams + (i ^ bit)) for k in se...  17.9 us
    ppermute x4, starting transfers between devices, relay(): lax.ppermute(sent, both, pairs[1])  15.4 us
  transfers between devices with their start and end apart: 30, of which 18 were waited for; matrix products, arithmetic and copies ran while one was open for 10% of the time, Pallas kernels for 18%

profile of v4, /device:TPU:0, one launch (start us, length us, event | category | flops | bytes accessed | tf_op | source)
XLA Modules:
  0.0 368.3 jit_solution(4049741358146344428)
XLA Ops:
  7.2 1.3 copy.69.refs_16_.refs_19_.refs_17_
  8.5 18.0 %forward.4 = (bf16[1024,1024]{1,0:T(8,128)(2,1)}, bf16[1024,1024]{1,0:T(8,128)(2,1)}, bf16[1024,1280]{1,0:T(8,128)(2,1)}, bf16[1024,1024]{1,0:T(8,128)(2,1)}, f3...) custom-call(f32[1,1024]{1,0:T(1,128)} %refs_8_.15, ...), custom_call_target="tpu_custom_call" | custom-call | flops 6442450944 | bytes 26214400 | tf_op jit(solution)/shard_map/forward/pallas_call | solution.py:495
  26.5 2.3 collective-permute-start
  28.8 2.8 fusion.17
  31.7 1.0 fusion.7
  32.7 2.1 collective-permute-start.1
  34.8 1.0 fusion.8
  35.8 1.3 collective-permute-start.2
  37.1 18.2 %forward.5 = (bf16[1024,1024]{1,0:T(8,128)(2,1)}, bf16[1024,1024]{1,0:T(8,128)(2,1)}, bf16[1024,1280]{1,0:T(8,128)(2,1)}, bf16[1024,1024]{1,0:T(8,128)(2,1)}, f3...) custom-call(f32[1,1024]{1,0:T(1,128)} %refs_8_.15, ...), custom_call_target="tpu_custom_call" | custom-call | flops 6442450944 | bytes 26214400 | tf_op jit(solution)/shard_map/forward/pallas_call | solution.py:495
  55.4 1.9 collective-permute-done.2
  57.3 1.9 collective-permute-start.3
  59.2 1.3 add_convert_fusion.11.refs_0_
  62.0 1.0 fusion.9
  63.9 7.4 %collective-permute-start.4 = (bf16[256,1024]{1,0:T(8,128)(2,1)S(1)}, bf16[256,1024]{1,0:T(8,128)(2,1)S(1)}, u32[]{:S(2)}, u32[]{:S(2)}) collective-permute-start(bf16[256,1024]{1,0:T(8,128)(2,1)S(1)} %fusion.6), channel_id=1, source_target_pairs={{0,16},{1,17},{2,18},{3,19},{4,20},{5,21},{6,22},{7,23},{8,24},{9,... | collective-permute-start | bytes 1572872 | tf_op jit(solution)/shard_map/ppermute | solution.py:746
  72.7 11.5 %collective-permute-start.5 = (bf16[256,1024]{1,0:T(8,128)(2,1)}, bf16[256,1024]{1,0:T(8,128)(2,1)S(1)}, u32[]{:S(2)}, u32[]{:S(2)}) collective-permute-start(bf16[256,1024]{1,0:T(8,128)(2,1)} %fusion.9), channel_id=1, source_target_pairs={{0,18},{1,19},{2,16},{3,17},{4,22},{5,23},{6,20},{7,21},{8,26},{9,... | collective-permute-start | bytes 1572872 | tf_op jit(solution)/shard_map/ppermute | solution.py:746
  84.2 0.9 copy-done.18
  86.0 10.3 %collective-permute-done.5 = bf16[256,1024]{1,0:T(8,128)(2,1)S(1)} collective-permute-done((bf16[256,1024]{1,0:T(8,128)(2,1)}, bf16[256,1024]{1,0:T(8,128)(2,1)S(1)}, u32[]{:S(2)}, u32[]{:S(2)}) %collective-permute-start.5) | collective-permute-done | bytes 524320 | tf_op jit(solution)/shard_map/ppermute | solution.py:746
  96.3 1.0 add_convert_fusion.10
  99.0 1.6 fusion.11
  100.6 1.3 collective-permute-start.11
  101.9 1.3 collective-permute-start.10
  103.2 24.5 %all-gather.3.cloned.1.call-done.refs_0_ = bf16[1024,1024]{1,0:T(8,128)(2,1)} async-done(((bf16[256,1024]{1,0:T(8,128)(2,1)}), bf16[1024,1024]{1,0:T(8,128)(2,1)}) %all-gather.3.cloned.1.call-update) | async-done | bytes 2097168 | tf_op jit(solution)/shard_map/all_gather | solution.py:752
  128.5 16.3 %collective-permute-done.11 = bf16[256,1024]{1,0:T(8,128)(2,1)S(1)} collective-permute-done((bf16[256,1024]{1,0:T(8,128)(2,1)S(1)}, bf16[256,1024]{1,0:T(8,128)(2,1)S(1)}, u32[]{:S(2)}, u32[]{:S(2)}) %collective-permute-start.11) | collective-permute-done | bytes 524320 | tf_op jit(solution)/shard_map/ppermute | solution.py:746
  144.9 9.3 %collective-permute-done.10 = bf16[256,1024]{1,0:T(8,128)(2,1)S(1)} collective-permute-done((bf16[256,1024]{1,0:T(8,128)(2,1)S(1)}, bf16[256,1024]{1,0:T(8,128)(2,1)S(1)}, u32[]{:S(2)}, u32[]{:S(2)}) %collective-permute-start.10) | collective-permute-done | bytes 524320 | tf_op jit(solution)/shard_map/ppermute | solution.py:746
  154.1 1.1 add_convert_fusion.7
  155.3 1.0 backward.5
  157.1 1.6 fusion.13
  158.7 1.3 collective-permute-start.14
  160.0 1.3 collective-permute-start.13
  161.3 17.6 %all-gather.5.cloned.1.call-done.refs_0_ = bf16[1024,1024]{1,0:T(8,128)(2,1)} async-done(((bf16[256,1024]{1,0:T(8,128)(2,1)}), bf16[1024,1024]{1,0:T(8,128)(2,1)}) %all-gather.5.cloned.1.call-update) | async-done | bytes 2097168 | tf_op jit(solution)/shard_map/all_gather | solution.py:752
  179.0 19.4 %backward.6 = (bf16[1024,1024]{1,0:T(8,128)(2,1)}, bf16[1024,768]{1,0:T(8,128)(2,1)}, bf16[2,256,1024]{2,1,0:T(8,128)(2,1)}, bf16[2,256,1024]{2,1,0:T(8,128)(2,1...) custom-call(f32[1,1024]{1,0:T(1,128)} %refs_8_.15, ...), custom_call_target="tpu_custom_call", output_to_operand_aliasing={{0}: (26, {}), {1}: (27, {}), {2}: (28, {}), {3}: (29, {}),... | custom-call | flops 6442450944 | bytes 31457280 | tf_op jit(solution)/shard_map/backward/pallas_call | solution.py:527
  198.4 6.1 %collective-permute-done.13 = bf16[256,1024]{1,0:T(8,128)(2,1)S(1)} collective-permute-done((bf16[256,1024]{1,0:T(8,128)(2,1)S(1)}, bf16[256,1024]{1,0:T(8,128)(2,1)S(1)}, u32[]{:S(2)}, u32[]{:S(2)}) %collective-permute-start.13) | collective-permute-done | bytes 524320 | tf_op jit(solution)/shard_map/ppermute | solution.py:746
  204.8 1.9 collective-permute-start.16
  206.7 4.0 %collective-permute-start.15 = (bf16[256,1024]{1,0:T(8,128)(2,1)S(1)}, bf16[256,1024]{1,0:T(8,128)(2,1)S(1)}, u32[]{:S(2)}, u32[]{:S(2)}) collective-permute-start(bf16[256,1024]{1,0:T(8,128)(2,1)S(1)} %add_convert_fusion.4.refs_0_), channel_id=1, source_target_pairs={{0,2},{1,3},{2,0},{3,1},{4,6},{5,7},{6,4},{7,5},{8,10},{9,11},{10,... | collective-permute-start | bytes 1572872 | tf_op jit(solution)/shard_map/ppermute | solution.py:722
  210.7 6.8 %down.4.refs_5_ = bf16[1024,1280]{1,0:T(8,128)(2,1)} custom-call(f32[1,1024]{1,0:T(1,128)} %refs_8_.15, bf16[1024,1024]{1,0:T(8,128)(2,1)} %all-gather.5.cloned.1.call-done.refs_0_, bf16[1024,1280]{1,0:T(8,128)(2,1)} %get-tuple-element.222.am.refs_1_), custom_call_target="tpu_custom_call" | custom-call | tf_op jit(solution)/shard_map/down/pallas_call | solution.py:690
  217.8 5.5 %collective-permute-done.15.refs_2_ = bf16[256,1024]{1,0:T(8,128)(2,1)S(1)} collective-permute-done((bf16[256,1024]{1,0:T(8,128)(2,1)S(1)}, bf16[256,1024]{1,0:T(8,128)(2,1)S(1)}, u32[]{:S(2)}, u32[]{:S(2)}) %collective-permute-start.15) | collective-permute-done | bytes 524320 | tf_op jit(solution)/shard_map/ppermute | solution.py:722
  223.3 1.9 collective-permute-start.17
  225.2 1.9 collective-permute-done.17.refs_3_
  227.9 7.8 %down.7 = (bf16[1024,1280]{1,0:T(8,128)(2,1)}, bf16[1024,1024]{1,0:T(8,128)(2,1)}) custom-call(f32[1,1024]{1,0:T(1,128)} %refs_8_.15, bf16[256,1024]{1,0:T(8,128)(2,1)} %copy-done.10, bf16[256,1024]{1,0:T(8,128)(2,1)} %copy-done.19, bf16[256,1024]{1,0:T(8,128)(2,1)} %copy-done.20, bf16[256,1024]{1,0:T(8,128)(2,1)} %copy-done.21, ...), custom_call_target="tpu_custom_call", output_to_operand_aliasing={{0}: (7, {})} | custom-call | flops 2684354560 | bytes 12582912 | tf_op jit(solution)/shard_map/down/pallas_call | solution.py:690
  235.8 19.6 %backward.7 = (bf16[1024,1024]{1,0:T(8,128)(2,1)}, bf16[1024,768]{1,0:T(8,128)(2,1)}, bf16[2,256,1024]{2,1,0:T(8,128)(2,1)}, bf16[2,256,1024]{2,1,0:T(8,128)(2,1...) custom-call(f32[1,1024]{1,0:T(1,128)} %refs_8_.15, ...), custom_call_target="tpu_custom_call", output_to_operand_aliasing={{0}: (26, {}), {1}: (27, {}), {2}: (28, {}), {3}: (29, {}),... | custom-call | flops 6442450944 | bytes 31457280 | tf_op jit(solution)/shard_map/backward/pallas_call | solution.py:527
  255.5 3.5 fusion.19
  259.0 2.4 fusion.18
  261.4 2.0 add_convert_fusion.1
  263.6 2.6 add_convert_fusion
  266.2 2.1 pad_maximum_fusion
  268.3 20.3 %reduce-scatter.3.cloned.1.call-done = bf16[256,1280]{1,0:T(8,128)(2,1)} async-done(((bf16[1024,1280]{1,0:T(8,128)(2,1)}), bf16[256,1280]{1,0:T(8,128)(2,1)}) %reduce-scatter.3.cloned.1.call-update) | async-done | bytes 655376 | tf_op jit(solution)/shard_map/reduce_scatter | solution.py:770
  289.5 3.3 collective-permute-done.22
  292.7 2.1 collective-permute-start.23
  294.9 3.1 collective-permute-done.23
  298.6 1.7 collective-permute-done.24
  300.3 1.5 collective-permute-start.25
  302.4 1.5 collective-permute-done.25
  304.6 2.0 fusion.14
  306.6 1.5 collective-permute-start.19
  308.1 2.0 fusion.15
  310.8 1.1 slice_bitcast_fusion
  311.9 2.5 copy.83
  315.1 1.8 copy.82
  316.9 4.9 %collective-permute-done.19 = bf16[256,1024]{1,0:T(8,128)(2,1)} collective-permute-done((bf16[256,1024]{1,0:T(8,128)(2,1)}, bf16[256,1024]{1,0:T(8,128)(2,1)}, u32[]{:S(2)}, u32[]{:S(2)}) %collective-permute-start.19) | collective-permute-done | bytes 524320 | tf_op jit(solution)/shard_map/ppermute | solution.py:722
  321.8 9.8 %collective-permute-done.21 = bf16[256,1024]{1,0:T(8,128)(2,1)} collective-permute-done((bf16[256,1024]{1,0:T(8,128)(2,1)}, bf16[256,1024]{1,0:T(8,128)(2,1)}, u32[]{:S(2)}, u32[]{:S(2)}) %collective-permute-start.21) | collective-permute-done | bytes 524320 | tf_op jit(solution)/shard_map/ppermute | solution.py:722
  331.6 2.7 fusion.5
  334.3 1.5 maximum_bitcast_fusion
  335.8 23.1 %reduce-scatter.5.cloned.1.call-done.packed = bf16[256,1792]{1,0:T(8,128)(2,1)} async-done(((bf16[1024,1792]{1,0:T(8,128)(2,1)}), bf16[256,1792]{1,0:T(8,128)(2,1)}) %reduce-scatter.5.cloned.1.call-update) | async-done | bytes 917520 | tf_op jit(solution)/shard_map/reduce_scatter | solution.py:770
  358.9 2.4 unpack.1
  (110 shorter events, 13.6 us)
Async XLA Ops:
  7.2 120.5 %all-gather.3.cloned.1.call-start = ((), (), s32[]{:S(2)}) async-start(), calls=%async_computation.2 | async-start | bytes 2621440 | tf_op jit(solution)/shard_map/all_gather | solution.py:752
  26.5 5.1 %collective-permute-start = (bf16[2,256,1024]{2,1,0:T(8,128)(2,1)}, bf16[2,256,1024]{2,1,0:T(8,128)(2,1)S(1)}, u32[]{:S(2)}, u32[]{:S(2)}) collective-permute-start(bf16[2,256,1024]{2,1,0:T(8,128)(2,1)} %get-tuple-element.144), channel_id=1, source_target_pairs={{0,1},{1,0},{2,3},{3,2},{4,5},{5,4},{6,7},{7,6},{8,9},{9,8},{10,11... | collective-permute-start | bytes 3145736 | tf_op jit(solution)/shard_map/ppermute | solution.py:722
  28.8 2.8 copy-start.12
  28.8 2.8 copy-start.26
  32.7 22.7 %collective-permute-start.1 = (bf16[256,1024]{1,0:T(8,128)(2,1)}, bf16[256,1024]{1,0:T(8,128)(2,1)}, u32[]{:S(2)}, u32[]{:S(2)}) collective-permute-start(bf16[256,1024]{1,0:T(8,128)(2,1)} %fusion.7), channel_id=1, source_target_pairs={{0,16},{1,17},{2,18},{3,19},{4,20},{5,21},{6,22},{7,23},{8,24},{9,... | collective-permute-start | bytes 1572872 | tf_op jit(solution)/shard_map/ppermute | solution.py:746
  35.8 21.5 %collective-permute-start.2 = (bf16[256,1024]{1,0:T(8,128)(2,1)}, bf16[256,1024]{1,0:T(8,128)(2,1)S(1)}, u32[]{:S(2)}, u32[]{:S(2)}) collective-permute-start(bf16[256,1024]{1,0:T(8,128)(2,1)} %fusion.8), channel_id=1, source_target_pairs={{0,18},{1,19},{2,16},{3,17},{4,22},{5,23},{6,20},{7,21},{8,26},{9,... | collective-permute-start | bytes 1572872 | tf_op jit(solution)/shard_map/ppermute | solution.py:746
  55.3 6.7 %copy-start.13 = (bf16[2,256,1024]{2,1,0:T(8,128)(2,1)S(1)}, bf16[2,256,1024]{2,1,0:T(8,128)(2,1)}, u32[]{:S(2)}) copy-start(bf16[2,256,1024]{2,1,0:T(8,128)(2,1)} %get-tuple-element.148) | copy-start | bytes 3145732
  57.3 4.8 %collective-permute-start.3 = (bf16[2,256,1024]{2,1,0:T(8,128)(2,1)}, bf16[2,256,1024]{2,1,0:T(8,128)(2,1)S(1)}, u32[]{:S(2)}, u32[]{:S(2)}) collective-permute-start(bf16[2,256,1024]{2,1,0:T(8,128)(2,1)} %get-tuple-element.149), channel_id=1, source_target_pairs={{0,1},{1,0},{2,3},{3,2},{4,5},{5,4},{6,7},{7,6},{8,9},{9,8},{10,11... | collective-permute-start | bytes 3145736 | tf_op jit(solution)/shard_map/ppermute | solution.py:722
  60.5 11.7 %copy-start.5 = (bf16[256,1024]{1,0:T(8,128)(2,1)}, bf16[256,1024]{1,0:T(8,128)(2,1)S(1)}, u32[]{:S(2)}) copy-start(bf16[256,1024]{1,0:T(8,128)(2,1)S(1)} %add_convert_fusion.11.refs_0_) | copy-start | bytes 1572868
  60.5 11.7 %copy-start = (bf16[2,1,1024,1024]{3,2,1,0:T(8,128)(2,1)S(1)}, bf16[2,1,1024,1024]{3,2,1,0:T(8,128)(2,1)}, u32[]{:S(2)}) copy-start(bf16[2,1,1024,1024]{3,2,1,0:T(8,128)(2,1)} %refs_0_.11) | copy-start | bytes 12582916
  60.5 10.8 %collective-permute-start.6 = (bf16[256,1024]{1,0:T(8,128)(2,1)S(1)}, bf16[256,1024]{1,0:T(8,128)(2,1)S(1)}, u32[]{:S(2)}, u32[]{:S(2)}) collective-permute-start(bf16[256,1024]{1,0:T(8,128)(2,1)S(1)} %add_convert_fusion.11.refs_0_), channel_id=1, source_target_pairs={{16,18},{17,19},{18,16},{19,17},{20,22},{21,23},{22,20},{23,21},{2... | collective-permute-start | bytes 1572872 | tf_op jit(solution)/shard_map/ppermute | solution.py:722
  63.2 8.1 %collective-permute-start.7 = (bf16[256,1024]{1,0:T(8,128)(2,1)S(1)}, bf16[256,1024]{1,0:T(8,128)(2,1)S(1)}, u32[]{:S(2)}, u32[]{:S(2)}) collective-permute-start(bf16[256,1024]{1,0:T(8,128)(2,1)S(1)} %add_convert_fusion.11.refs_0_), channel_id=1, source_target_pairs={{16,17},{17,16},{18,19},{19,18},{20,21},{21,20},{22,23},{23,22},{2... | collective-permute-start | bytes 1572872 | tf_op jit(solution)/shard_map/ppermute | solution.py:722
  63.9 20.3 %collective-permute-start.4 = (bf16[256,1024]{1,0:T(8,128)(2,1)S(1)}, bf16[256,1024]{1,0:T(8,128)(2,1)S(1)}, u32[]{:S(2)}, u32[]{:S(2)}) collective-permute-start(bf16[256,1024]{1,0:T(8,128)(2,1)S(1)} %fusion.6), channel_id=1, source_target_pairs={{0,16},{1,17},{2,18},{3,19},{4,20},{5,21},{6,22},{7,23},{8,24},{9,... | collective-permute-start | bytes 1572872 | tf_op jit(solution)/shard_map/ppermute | solution.py:746
  71.4 1.3 copy-start.16
  71.4 1.3 copy-start.17
  71.4 12.8 %collective-permute-start.8 = (bf16[256,1024]{1,0:T(8,128)(2,1)S(1)}, bf16[256,1024]{1,0:T(8,128)(2,1)S(1)}, u32[]{:S(2)}, u32[]{:S(2)}) collective-permute-start(bf16[256,1024]{1,0:T(8,128)(2,1)S(1)} %collective-permute-done.6.refs_2_), channel_id=1, source_target_pairs={{16,17},{17,16},{18,19},{19,18},{20,21},{21,20},{22,23},{23,22},{2... | collective-permute-start | bytes 1572872 | tf_op jit(solution)/shard_map/ppermute | solution.py:722
  72.7 23.6 %collective-permute-start.5 = (bf16[256,1024]{1,0:T(8,128)(2,1)}, bf16[256,1024]{1,0:T(8,128)(2,1)S(1)}, u32[]{:S(2)}, u32[]{:S(2)}) collective-permute-start(bf16[256,1024]{1,0:T(8,128)(2,1)} %fusion.9), channel_id=1, source_target_pairs={{0,18},{1,19},{2,16},{3,17},{4,22},{5,23},{6,20},{7,21},{8,26},{9,... | collective-permute-start | bytes 1572872 | tf_op jit(solution)/shard_map/ppermute | solution.py:746
  84.2 1.0 copy-start.22
  84.2 0.9 copy-start.18
  85.2 11.1 %copy-start.23 = (bf16[256,1024]{1,0:T(8,128)(2,1)S(1)}, bf16[256,1024]{1,0:T(8,128)(2,1)}, u32[]{:S(2)}) copy-start(bf16[256,1024]{1,0:T(8,128)(2,1)} %copy-done.22) | copy-start | bytes 1572868
  97.4 81.5 %all-gather.5.cloned.1.call-start = ((), (), s32[]{:S(2)}) async-start(), calls=%async_computation.3 | async-start | bytes 2621440 | tf_op jit(solution)/shard_map/all_gather | solution.py:752
  98.2 0.7 collective-permute-start.9
  100.6 44.3 %collective-permute-start.11 = (bf16[256,1024]{1,0:T(8,128)(2,1)S(1)}, bf16[256,1024]{1,0:T(8,128)(2,1)S(1)}, u32[]{:S(2)}, u32[]{:S(2)}) collective-permute-start(bf16[256,1024]{1,0:T(8,128)(2,1)S(1)} %get-tuple-element.292), channel_id=1, source_target_pairs={{16,2},{17,3},{18,0},{19,1},{20,6},{21,7},{22,4},{23,5},{24,10},{2... | collective-permute-start | bytes 1572872 | tf_op jit(solution)/shard_map/ppermute | solution.py:746
  101.9 52.2 %collective-permute-start.10 = (bf16[256,1024]{1,0:T(8,128)(2,1)S(1)}, bf16[256,1024]{1,0:T(8,128)(2,1)S(1)}, u32[]{:S(2)}, u32[]{:S(2)}) collective-permute-start(bf16[256,1024]{1,0:T(8,128)(2,1)S(1)} %get-tuple-element.293), channel_id=1, source_target_pairs={{16,0},{17,1},{18,2},{19,3},{20,4},{21,5},{22,6},{23,7},{24,8},{25... | collective-permute-start | bytes 1572872 | tf_op jit(solution)/shard_map/ppermute | solution.py:746
  155.2 133.4 %reduce-scatter.3.cloned.1.call-start = ((), (), s32[]{:S(2)}) async-start(), calls=%async_computation.4 | async-start | bytes 3276800 | tf_op jit(solution)/shard_map/reduce_scatter | solution.py:770
  156.3 0.7 collective-permute-start.12
  158.7 39.7 %collective-permute-start.14 = (bf16[256,1024]{1,0:T(8,128)(2,1)S(1)}, bf16[256,1024]{1,0:T(8,128)(2,1)S(1)}, u32[]{:S(2)}, u32[]{:S(2)}) collective-permute-start(bf16[256,1024]{1,0:T(8,128)(2,1)S(1)} %get-tuple-element.290), channel_id=1, source_target_pairs={{16,2},{17,3},{18,0},{19,1},{20,6},{21,7},{22,4},{23,5},{24,10},{2... | collective-permute-start | bytes 1572872 | tf_op jit(solution)/shard_map/ppermute | solution.py:746
  160.0 44.5 %collective-permute-start.13 = (bf16[256,1024]{1,0:T(8,128)(2,1)S(1)}, bf16[256,1024]{1,0:T(8,128)(2,1)S(1)}, u32[]{:S(2)}, u32[]{:S(2)}) collective-permute-start(bf16[256,1024]{1,0:T(8,128)(2,1)S(1)} %get-tuple-element.291), channel_id=1, source_target_pairs={{16,0},{17,1},{18,2},{19,3},{20,4},{21,5},{22,6},{23,7},{24,8},{25... | collective-permute-start | bytes 1572872 | tf_op jit(solution)/shard_map/ppermute | solution.py:746
  204.7 12.8 %copy-start.10 = (bf16[256,1024]{1,0:T(8,128)(2,1)}, bf16[256,1024]{1,0:T(8,128)(2,1)S(1)}, u32[]{:S(2)}) copy-start(bf16[256,1024]{1,0:T(8,128)(2,1)S(1)} %add_convert_fusion.4.refs_0_) | copy-start | bytes 1572868
  204.8 13.0 %collective-permute-start.16 = (bf16[256,1024]{1,0:T(8,128)(2,1)S(1)}, bf16[256,1024]{1,0:T(8,128)(2,1)S(1)}, u32[]{:S(2)}, u32[]{:S(2)}) collective-permute-start(bf16[256,1024]{1,0:T(8,128)(2,1)S(1)} %add_convert_fusion.4.refs_0_), channel_id=1, source_target_pairs={{0,1},{1,0},{2,3},{3,2},{4,5},{5,4},{6,7},{7,6},{8,9},{9,8},{10,11... | collective-permute-start | bytes 1572872 | tf_op jit(solution)/shard_map/ppermute | solution.py:722
  206.7 16.6 %collective-permute-start.15 = (bf16[256,1024]{1,0:T(8,128)(2,1)S(1)}, bf16[256,1024]{1,0:T(8,128)(2,1)S(1)}, u32[]{:S(2)}, u32[]{:S(2)}) collective-permute-start(bf16[256,1024]{1,0:T(8,128)(2,1)S(1)} %add_convert_fusion.4.refs_0_), channel_id=1, source_target_pairs={{0,2},{1,3},{2,0},{3,1},{4,6},{5,7},{6,4},{7,5},{8,10},{9,11},{10,... | collective-permute-start | bytes 1572872 | tf_op jit(solution)/shard_map/ppermute | solution.py:722
  217.8 9.3 %copy-start.19 = (bf16[256,1024]{1,0:T(8,128)(2,1)}, bf16[256,1024]{1,0:T(8,128)(2,1)S(1)}, u32[]{:S(2)}) copy-start(bf16[256,1024]{1,0:T(8,128)(2,1)S(1)} %collective-permute-done.16.refs_1_) | copy-start | bytes 1572868
  223.3 3.8 %copy-start.20 = (bf16[256,1024]{1,0:T(8,128)(2,1)}, bf16[256,1024]{1,0:T(8,128)(2,1)S(1)}, u32[]{:S(2)}) copy-start(bf16[256,1024]{1,0:T(8,128)(2,1)S(1)} %collective-permute-done.15.refs_2_) | copy-start | bytes 1572868
  223.3 3.8 %collective-permute-start.17 = (bf16[256,1024]{1,0:T(8,128)(2,1)S(1)}, bf16[256,1024]{1,0:T(8,128)(2,1)S(1)}, u32[]{:S(2)}, u32[]{:S(2)}) collective-permute-start(bf16[256,1024]{1,0:T(8,128)(2,1)S(1)} %collective-permute-done.15.refs_2_), channel_id=1, source_target_pairs={{0,1},{1,0},{2,3},{3,2},{4,5},{5,4},{6,7},{7,6},{8,9},{9,8},{10,11... | collective-permute-start | bytes 1572872 | tf_op jit(solution)/shard_map/ppermute | solution.py:722
  227.1 0.8 copy-start.21
  235.7 123.2 %reduce-scatter.5.cloned.1.call-start = ((), (), s32[]{:S(2)}) async-start(), calls=%async_computation.5 | async-start | bytes 4587520 | tf_op jit(solution)/shard_map/reduce_scatter | solution.py:770
  235.8 19.6 %copy-start.6 = (bf16[1024,1024]{1,0:T(8,128)(2,1)S(1)}, bf16[1024,1024]{1,0:T(8,128)(2,1)}, u32[]{:S(2)}) copy-start(bf16[1024,1024]{1,0:T(8,128)(2,1)} %get-tuple-element.254) | copy-start | bytes 6291460
  255.4 3.5 copy-start.1
  255.4 3.5 copy-start.7
  258.9 2.5 copy-start.8
  258.9 2.5 copy-start.11
  261.4 2.0 copy-start.2
  261.4 2.2 copy-start.9
  268.3 20.4 %copy-start.24 = (f32[8,1024]{1,0:T(8,128)S(1)}, f32[8,1024]{1,0:T(8,128)}, u32[]{:S(2)}) copy-start(f32[8,1024]{1,0:T(8,128)} %get-tuple-element.266) | copy-start | bytes 98308
  268.3 20.4 %copy-start.25 = (f32[8,1024]{1,0:T(8,128)S(1)}, f32[8,1024]{1,0:T(8,128)}, u32[]{:S(2)}) copy-start(f32[8,1024]{1,0:T(8,128)} %get-tuple-element.267) | copy-start | bytes 98308
  268.3 29.6 %copy-start.14 = (bf16[2,256,1024]{2,1,0:T(8,128)(2,1)S(1)}, bf16[2,256,1024]{2,1,0:T(8,128)(2,1)}, u32[]{:S(2)}) copy-start(bf16[2,256,1024]{2,1,0:T(8,128)(2,1)} %get-tuple-element.265) | copy-start | bytes 3145732
  268.3 36.3 %copy-start.4 = (bf16[2,256,1024]{2,1,0:T(8,128)(2,1)S(1)}, bf16[2,256,1024]{2,1,0:T(8,128)(2,1)}, u32[]{:S(2)}) copy-start(bf16[2,256,1024]{2,1,0:T(8,128)(2,1)} %get-tuple-element.258) | copy-start | bytes 3145732
  268.3 39.8 %copy-start.3 = (bf16[2,256,1024]{2,1,0:T(8,128)(2,1)S(1)}, bf16[2,256,1024]{2,1,0:T(8,128)(2,1)}, u32[]{:S(2)}) copy-start(bf16[2,256,1024]{2,1,0:T(8,128)(2,1)} %get-tuple-element.264) | copy-start | bytes 3145732
  288.6 15.9 %collective-permute-start.18 = (bf16[2,256,1024]{2,1,0:T(8,128)(2,1)}, bf16[2,256,1024]{2,1,0:T(8,128)(2,1)}, u32[]{:S(2)}, u32[]{:S(2)}) collective-permute-start(bf16[2,256,1024]{2,1,0:T(8,128)(2,1)} %get-tuple-element.259), channel_id=1, source_target_pairs={{0,1},{1,0},{2,3},{3,2},{16,17},{17,16},{18,19},{19,18},{4,5},{5,4... | collective-permute-start | bytes 3145736 | tf_op jit(solution)/shard_map/ppermute | solution.py:722
  288.8 4.0 %collective-permute-start.22 = (f32[8,1024]{1,0:T(8,128)S(1)}, f32[8,1024]{1,0:T(8,128)S(1)}, u32[]{:S(2)}, u32[]{:S(2)}) collective-permute-start(f32[8,1024]{1,0:T(8,128)S(1)} %add.201), channel_id=1, source_target_pairs={{0,4},{4,0},{8,12},{12,8},{1,5},{5,1},{9,13},{13,9},{2,6},{6,2},{1... | collective-permute-start | bytes 98312 | tf_op jit(solution)/shard_map/ppermute | solution.py:762
  292.7 5.2 %collective-permute-start.23 = (f32[8,1024]{1,0:T(8,128)S(1)}, f32[8,1024]{1,0:T(8,128)S(1)}, u32[]{:S(2)}, u32[]{:S(2)}) collective-permute-start(f32[8,1024]{1,0:T(8,128)S(1)} %add.202), channel_id=1, source_target_pairs={{0,8},{4,12},{8,0},{12,4},{1,9},{5,13},{9,1},{13,5},{2,10},{6,14},... | collective-permute-start | bytes 98312 | tf_op jit(solution)/shard_map/ppermute | solution.py:762
  297.9 10.2 %collective-permute-start.20 = (bf16[2,256,1024]{2,1,0:T(8,128)(2,1)S(1)}, bf16[2,256,1024]{2,1,0:T(8,128)(2,1)}, u32[]{:S(2)}, u32[]{:S(2)}) collective-permute-start(bf16[2,256,1024]{2,1,0:T(8,128)(2,1)S(1)} %copy-done.14), channel_id=1, source_target_pairs={{0,1},{1,0},{2,3},{3,2},{16,17},{17,16},{18,19},{19,18},{4,5},{5,4... | collective-permute-start | bytes 3145736 | tf_op jit(solution)/shard_map/ppermute | solution.py:722
  298.0 2.3 collective-permute-start.24
  298.6 12.1 %copy-start.15 = (bf16[256,1280]{1,0:T(8,128)(2,1)S(1)}, bf16[256,1280]{1,0:T(8,128)(2,1)}, u32[]{:S(2)}) copy-start(bf16[256,1280]{1,0:T(8,128)(2,1)} %reduce-scatter.3.cloned.1.call-done) | copy-start | bytes 1966084
  300.3 3.7 collective-permute-start.25
  306.6 15.2 %collective-permute-start.19 = (bf16[256,1024]{1,0:T(8,128)(2,1)}, bf16[256,1024]{1,0:T(8,128)(2,1)}, u32[]{:S(2)}, u32[]{:S(2)}) collective-permute-start(bf16[256,1024]{1,0:T(8,128)(2,1)} %fusion.14), channel_id=1, source_target_pairs={{0,2},{1,3},{2,0},{3,1},{16,18},{17,19},{18,16},{19,17},{4,6},{5,7... | collective-permute-start | bytes 1572872 | tf_op jit(solution)/shard_map/ppermute | solution.py:722
  310.1 21.5 %collective-permute-start.21 = (bf16[256,1024]{1,0:T(8,128)(2,1)}, bf16[256,1024]{1,0:T(8,128)(2,1)}, u32[]{:S(2)}, u32[]{:S(2)}) collective-permute-start(bf16[256,1024]{1,0:T(8,128)(2,1)} %fusion.15), channel_id=1, source_target_pairs={{0,2},{1,3},{2,0},{3,1},{16,18},{17,19},{18,16},{19,17},{4,6},{5,7... | collective-permute-start | bytes 1572872 | tf_op jit(solution)/shard_map/ppermute | solution.py:722
Sparse Core Ops, SparseCore 0:
  97.5 30.1 all-gather.2
  155.3 23.5 all-gather.4
  235.8 52.7 reduce-scatter.2
  290.8 68.0 reduce-scatter.4

commit v5 on v4

--- a/solution.py
+++ b/solution.py
@@ -233,11 +233,11 @@
             slot = lax.broadcasted_iota(jnp.int32, (BLOCK, e), 0) + (b * BLOCK + base)
             k_feat = jnp.where(slot < v_len[cfg["m"]:cfg["m"] + 1, :], feats[BLOCK:], 0.0)
             value = qkv[:, 2 * e:].astype(BF)
-            o_qf[rb] = q_feat
-            o_kf[rb] = k_feat
-            o_v[rb] = value
             q_b = q_feat.astype(BF)
             k_b = k_feat.astype(BF)
+            o_qf[rb] = q_b
+            o_kf[rb] = k_b
+            o_v[rb] = value
             row = lax.broadcasted_iota(jnp.int32, (CHUNK, hc * CHUNK), 0)
             col = lax.broadcasted_iota(jnp.int32, (CHUNK, hc * CHUNK), 1) & (CHUNK - 1)
             causal = row >= col
@@ -253,7 +253,7 @@
                 inverse = 1.0 / (both[:, e:] + dot(weighted, v_same[...].astype(BF)))
                 mixed = (both[:, :e] + dot(q_c, state[...].astype(BF))) * inverse
                 rg = rows_at(at, CHUNK)
-                o_inv[rg] = inverse
+                o_inv[rg] = inverse.astype(BF)
                 o_mf[rg] = mixed
                 o_am[rg, f:] = mixed.astype(BF)
                 state[...] += dot_tn(k_c, v_c) * v_same[...]
@@ -343,8 +343,8 @@
         some = pl.ds(base, rows)
         some_chunks = pl.ds(base // CHUNK, chunks)
         in_g = [(place(g_in[0]), v_g)] if len(g_in) == 1 else [(g, v_g.at[pl.ds(i * g.shape[0], g.shape[0])]) for i, g in enumerate(g_in)]
-        in_a = io.start(*in_g, *([(in_gup.at[some], o_gup), (in_mix.at[some], mixes)] if opened else
-                                [(wdown.at[0], v_wdown), (wo.at[0], v_wo), (s_gp.at[some], i_gp)]))
+        in_a = io.start(*([(in_mix.at[some], mixes)] if opened else
+                          in_g + [(wdown.at[0], v_wdown), (wo.at[0], v_wo), (s_gp.at[some], i_gp)]))
         in_b = io.start((s_mf.at[some], i_mf), (s_inv.at[some], i_inv), (s_qf.at[some], i_qf), (s_kf.at[some], i_kf), (s_v.at[some], i_v),
                         (s_st.at[some_chunks], i_st), (s_kt.at[some_chunks], i_kt), (heads, v_heads), (same, v_same),
                         (turn.at[:, some], v_turn), (dct, v_dct))
@@ -353,12 +353,13 @@
         else:
             state[...] = jnp.zeros_like(state)
             total[...] = jnp.zeros_like(total)
-        in_c = io.start(*[(w.at[0], v_wqkv.at[:, pl.ds(i * e, e)]) for i, w in enumerate((wq, wk, wv))], (wup.at[0], v_wup), (place(h_in), v_h),
+        in_c = io.start(*(in_g + [(in_gup.at[some], o_gup)] if opened else []))
+        in_c += io.start(*[(w.at[0], v_wqkv.at[:, pl.ds(i * e, e)]) for i, w in enumerate((wq, wk, wv))], (wup.at[0], v_wup), (place(h_in), v_h),
                         *[(norm, v_norms.at[i]) for i, norm in enumerate(norms)], (scales.at[0], v_scales))
         acc[...] = jnp.zeros_like(acc)
         acc_s[...] = jnp.zeros_like(acc_s)
         wait(in_a)
-        out_s = io.start((v_g.at[rows_at(me, rows // 4)], own))
+        out_s = [] if opened else io.start((v_g.at[rows_at(me, rows // 4)], own))
 
         def fold(x):
             return jnp.sum(x.reshape(x.shape[0] // 8, 8, x.shape[1]), axis=0)
@@ -378,16 +379,14 @@
         def _(step):
             b = blocks - 1 - step
             rb = rows_at(b, BLOCK)
-            g_num = (mixes[rb].astype(F32) * i_inv[rb]).astype(BF)
+            g_num = (mixes[rb].astype(F32) * i_inv[rb].astype(F32)).astype(BF)
             high, low = split(g_num.astype(F32) * i_mf[rb])
             same_b = v_same[...].astype(BF)
             g_den = -(dot(high, same_b) + dot(low, same_b))
             gd_high, gd_low = split(g_den)
-            q_feat = i_qf[rb]
-            k_feat = i_kf[rb]
+            q_b = i_qf[rb]
+            k_b = i_kf[rb]
             value = i_v[rb]
-            q_b = q_feat.astype(BF)
-            k_b = k_feat.astype(BF)
             row = lax.broadcasted_iota(jnp.int32, (CHUNK, hc * CHUNK), 0)
             col = lax.broadcasted_iota(jnp.int32, (CHUNK, hc * CHUNK), 1) & (CHUNK - 1)
             causal = row >= col
@@ -413,8 +412,8 @@
                 gv_parts[c] = dot(lanes_of_heads(scores_t, hc), stack_heads(n_c, hm, hc)) + dot(k_c, after[:, :e])
                 state[...] += dot_tn(q_c, n_c) * v_same[...]
                 total[...] += jnp.sum(q_c.astype(F32) * g_den[rc], axis=0, keepdims=True)
-            gc_q = jnp.concatenate(gq_parts, axis=0) * q_feat
-            gc_k = jnp.concatenate(gk_parts, axis=0) * k_feat
+            gc_q = jnp.concatenate(gq_parts, axis=0) * q_b.astype(F32)
+            gc_k = jnp.concatenate(gk_parts, axis=0) * k_b.astype(F32)
             g_value = jnp.concatenate(gv_parts, axis=0)
             acc_s[...] += fold(gc_q + gc_k)
             cos_b = jnp.concatenate([jnp.concatenate([v_turn[0, rb]] * (hc // 2), axis=1)] * 2, axis=0)
@@ -427,6 +426,8 @@
 
         out_s += io.start((state, c_st), (total, c_kt))
         wait(in_c)
+        if opened:
+            out_s += io.start((v_g.at[rows_at(me, rows // 4)], own))
 
         @pl.loop(0, blocks)
         def _(b):
@@ -475,8 +476,8 @@
     own = some // CHUNK
     shapes = [
         like((rows, d), BF), like((rows, d), BF), like((rows, f + e), BF), like((rows, f), BF),
-        like((rows, e), F32), like((rows, e), F32), like((rows, e), BF), like((rows, e), F32),
-        like((rows, e), F32), like((chunks, e, e), F32), like((chunks, 8, e), F32), like((rows, d), BF),
+        like((rows, e), BF), like((rows, e), BF), like((rows, e), BF), like((rows, e), F32),
+        like((rows, e), BF), like((chunks, e, e), F32), like((chunks, 8, e), F32), like((rows, d), BF),
         like((some // 4, d), BF), like((e, e), F32), like((8, e), F32),
     ] + ([like((2, share, d), BF)] * 2 if section == 0 else [like((rows, e), BF)])
     through = list(store) + list(parts)
@@ -485,8 +486,8 @@
         ((some, d), BF), ((d, 3 * e), BF), ((e, d), BF), ((d, f), BF), ((f, d), BF),
         ((4, 1, d), F32), ((hc, e // hc), F32), ((2, some, 2 * (e // hc)), F32), ((2, e, e), BF), ((hc * CHUNK, e), BF), ((e, e), F32),
         ((some, d), BF), ((some, d), BF), ((some, f + e), BF), ((some, f), BF),
-        ((some, e), F32), ((some, e), F32), ((some, e), BF), ((some, e), F32),
-        ((some, e), F32), ((own, e, e), F32), ((own, 8, e), F32), ((some, d), BF),
+        ((some, e), BF), ((some, e), BF), ((some, e), BF), ((some, e), F32),
+        ((some, e), BF), ((own, e, e), F32), ((own, 8, e), F32), ((some, d), BF),
         ((e, e), F32), ((8, e), F32))]
     scratch += [pltpu.VMEM(tabs[-1].shape, jnp.int32), pltpu.VMEM((some, d), BF), pltpu.VMEM((some, e), BF), pltpu.SemaphoreType.DMA((32,)), pltpu.SemaphoreType.DMA((16, some // BLOCK))]
     cfg = {"m": m, "section": section, "pieces": len(pieces), "base": base, "share": share, "origin": base // share if ends else 0,
@@ -517,8 +518,8 @@
     scratch = [pltpu.VMEM(shape, dtype) for shape, dtype in (
         ((some, d), BF), ((some, d), BF), ((d, 3 * e), BF), ((e, d), BF), ((d, f), BF), ((f, d), BF),
         ((4, 1, d), F32), ((hc, e // hc), F32), ((2, some, 2 * (e // hc)), F32), ((2, e, e), BF), ((hc * CHUNK, e), BF), ((e, e), F32),
-        ((some, f), BF), ((some, e), F32), ((some, e), F32), ((some, e), BF),
-        ((some, e), F32), ((some, e), F32), ((own, e, e), F32), ((own, 8, e), F32),
+        ((some, f), BF), ((some, e), BF), ((some, e), BF), ((some, e), BF),
+        ((some, e), F32), ((some, e), BF), ((own, e, e), F32), ((own, 8, e), F32),
         ((some, f), BF), ((some, 3 * e), BF), ((some, d), BF), ((8, d), F32),
         ((some, e), BF), ((5, 8, d), F32), ((8, e), F32), ((e, e), F32), ((8, e), F32))]
     scratch += [pltpu.SemaphoreType.DMA((40,)), pltpu.SemaphoreType.DMA((4, some // BLOCK))]

time: 375 us -> 371 us (0.989)
  waiting for transfers between devices: 162 us -> 158 us
  transfers between devices with their start and end apart: 30 -> 30, of which waited for: 18 -> 18; matrix products, arithmetic and copies ran while one was open for 10% -> 11% of each run, Pallas kernels for 18% -> 19%
where the time goes in v5:
time: 371 us; the launch traced here: 364 us
  waiting for transfers between devices  158 us (43%)
  Pallas kernels  95.8 us (26%)
  starting transfers between devices  50.3 us (14%)
  other arithmetic  21.2 us (6%)
  between operations  15 us (4%)
  local copies, waits for them, and re-layouts  13.6 us (4%)
  matrix products  10.5 us (3%)
    reduce_scatter x2, waiting for transfers between devices, scatter(): return lax.psum_scatter(total, 'dp', scatter_dimension=0, tiled=True)  43.2 us
    all_gather x2, waiting for transfers between devices, whole_rows(): return lax.all_gather(own, 'tensor', axis=0, tiled=True)  41.9 us
    pallas_call x4, Pallas kernels, backward_call(): pl.pallas_call(functools.partial(backward_kernel, cfg), out_shape=shapes,...  40.7 us
    pallas_call x4, Pallas kernels, forward_call(): pl.pallas_call(functools.partial(forward_kernel, cfg), out_shape=shapes,...  37.7 us
    ppermute x4, waiting for transfers between devices, relay(): lax.ppermute(sent, both, pairs[1])  26.8 us
    ppermute x14, waiting for transfers between devices, swap(): lax.ppermute(x, both, [(k * teams + i, k * teams + (i ^ bit)) for k in se...  22.7 us
    ppermute x14, starting transfers between devices, swap(): lax.ppermute(x, both, [(k * teams + i, k * teams + (i ^ bit)) for k in se...  17.9 us
    ppermute x4, starting transfers between devices, relay(): lax.ppermute(sent, both, pairs[1])  15.4 us
  transfers between devices with their start and end apart: 30, of which 18 were waited for; matrix products, arithmetic and copies ran while one was open for 11% of the time, Pallas kernels for 19%

profile of v5, /device:TPU:0, one launch (start us, length us, event | category | flops | bytes accessed | tf_op | source)
XLA Modules:
  0.0 364.4 jit_solution(14812365997739972450)
XLA Ops:
  7.2 1.3 copy.69.refs_16_.refs_19_.refs_17_
  8.5 17.9 %forward.4 = (bf16[1024,1024]{1,0:T(8,128)(2,1)}, bf16[1024,1024]{1,0:T(8,128)(2,1)}, bf16[1024,1280]{1,0:T(8,128)(2,1)}, bf16[1024,1024]{1,0:T(8,128)(2,1)}, bf...) custom-call(f32[1,1024]{1,0:T(1,128)} %refs_8_.15, ...), custom_call_target="tpu_custom_call" | custom-call | flops 6442450944 | bytes 26214400 | tf_op jit(solution)/shard_map/forward/pallas_call | solution.py:496
  26.4 2.3 collective-permute-start
  28.8 2.8 fusion.17
  31.7 1.0 fusion.7
  32.7 2.1 collective-permute-start.1
  34.7 1.0 fusion.8
  35.8 1.3 collective-permute-start.2
  37.1 18.2 %forward.5 = (bf16[1024,1024]{1,0:T(8,128)(2,1)}, bf16[1024,1024]{1,0:T(8,128)(2,1)}, bf16[1024,1280]{1,0:T(8,128)(2,1)}, bf16[1024,1024]{1,0:T(8,128)(2,1)}, bf...) custom-call(f32[1,1024]{1,0:T(1,128)} %refs_8_.15, ...), custom_call_target="tpu_custom_call" | custom-call | flops 6442450944 | bytes 26214400 | tf_op jit(solution)/shard_map/forward/pallas_call | solution.py:496
  55.3 1.9 collective-permute-done.2
  57.2 1.9 collective-permute-start.3
  59.1 1.3 add_convert_fusion.11.refs_0_
  61.9 1.0 fusion.9
  63.9 7.5 %collective-permute-start.4 = (bf16[256,1024]{1,0:T(8,128)(2,1)S(1)}, bf16[256,1024]{1,0:T(8,128)(2,1)S(1)}, u32[]{:S(2)}, u32[]{:S(2)}) collective-permute-start(bf16[256,1024]{1,0:T(8,128)(2,1)S(1)} %fusion.6), channel_id=1, source_target_pairs={{0,16},{1,17},{2,18},{3,19},{4,20},{5,21},{6,22},{7,23},{8,24},{9,... | collective-permute-start | bytes 1572872 | tf_op jit(solution)/shard_map/ppermute | solution.py:747
  72.7 11.5 %collective-permute-start.5 = (bf16[256,1024]{1,0:T(8,128)(2,1)}, bf16[256,1024]{1,0:T(8,128)(2,1)S(1)}, u32[]{:S(2)}, u32[]{:S(2)}) collective-permute-start(bf16[256,1024]{1,0:T(8,128)(2,1)} %fusion.9), channel_id=1, source_target_pairs={{0,18},{1,19},{2,16},{3,17},{4,22},{5,23},{6,20},{7,21},{8,26},{9,... | collective-permute-start | bytes 1572872 | tf_op jit(solution)/shard_map/ppermute | solution.py:747
  85.9 10.3 %collective-permute-done.5 = bf16[256,1024]{1,0:T(8,128)(2,1)S(1)} collective-permute-done((bf16[256,1024]{1,0:T(8,128)(2,1)}, bf16[256,1024]{1,0:T(8,128)(2,1)S(1)}, u32[]{:S(2)}, u32[]{:S(2)}) %collective-permute-start.5) | collective-permute-done | bytes 524320 | tf_op jit(solution)/shard_map/ppermute | solution.py:747
  96.3 1.1 add_convert_fusion.10
  99.0 1.6 fusion.11
  100.6 1.3 collective-permute-start.11
  101.9 1.3 collective-permute-start.10
  103.2 24.5 %all-gather.3.cloned.1.call-done.refs_0_ = bf16[1024,1024]{1,0:T(8,128)(2,1)} async-done(((bf16[256,1024]{1,0:T(8,128)(2,1)}), bf16[1024,1024]{1,0:T(8,128)(2,1)}) %all-gather.3.cloned.1.call-update) | async-done | bytes 2097168 | tf_op jit(solution)/shard_map/all_gather | solution.py:753
  127.7 0.8 forward.7
  128.5 14.5 %collective-permute-done.11 = bf16[256,1024]{1,0:T(8,128)(2,1)S(1)} collective-permute-done((bf16[256,1024]{1,0:T(8,128)(2,1)S(1)}, bf16[256,1024]{1,0:T(8,128)(2,1)S(1)}, u32[]{:S(2)}, u32[]{:S(2)}) %collective-permute-start.11) | collective-permute-done | bytes 524320 | tf_op jit(solution)/shard_map/ppermute | solution.py:747
  143.0 9.3 %collective-permute-done.10 = bf16[256,1024]{1,0:T(8,128)(2,1)S(1)} collective-permute-done((bf16[256,1024]{1,0:T(8,128)(2,1)S(1)}, bf16[256,1024]{1,0:T(8,128)(2,1)S(1)}, u32[]{:S(2)}, u32[]{:S(2)}) %collective-permute-start.10) | collective-permute-done | bytes 524320 | tf_op jit(solution)/shard_map/ppermute | solution.py:747
  152.3 1.1 add_convert_fusion.7
  153.5 1.0 backward.5
  155.3 1.6 fusion.13
  156.9 1.3 collective-permute-start.14
  158.2 1.3 collective-permute-start.13
  159.5 17.4 %all-gather.5.cloned.1.call-done.refs_0_ = bf16[1024,1024]{1,0:T(8,128)(2,1)} async-done(((bf16[256,1024]{1,0:T(8,128)(2,1)}), bf16[1024,1024]{1,0:T(8,128)(2,1)}) %all-gather.5.cloned.1.call-update) | async-done | bytes 2097168 | tf_op jit(solution)/shard_map/all_gather | solution.py:753
  177.0 19.4 %backward.6 = (bf16[1024,1024]{1,0:T(8,128)(2,1)}, bf16[1024,768]{1,0:T(8,128)(2,1)}, bf16[2,256,1024]{2,1,0:T(8,128)(2,1)}, bf16[2,256,1024]{2,1,0:T(8,128)(2,1...) custom-call(f32[1,1024]{1,0:T(1,128)} %refs_8_.15, ...), custom_call_target="tpu_custom_call", output_to_operand_aliasing={{0}: (26, {}), {1}: (27, {}), {2}: (28, {}), {3}: (29, {}),... | custom-call | flops 6442450944 | bytes 31457280 | tf_op jit(solution)/shard_map/backward/pallas_call | solution.py:528
  196.4 4.5 %collective-permute-done.13 = bf16[256,1024]{1,0:T(8,128)(2,1)S(1)} collective-permute-done((bf16[256,1024]{1,0:T(8,128)(2,1)S(1)}, bf16[256,1024]{1,0:T(8,128)(2,1)S(1)}, u32[]{:S(2)}, u32[]{:S(2)}) %collective-permute-start.13) | collective-permute-done | bytes 524320 | tf_op jit(solution)/shard_map/ppermute | solution.py:747
  201.1 1.9 collective-permute-start.16
  203.1 3.9 %collective-permute-start.15 = (bf16[256,1024]{1,0:T(8,128)(2,1)S(1)}, bf16[256,1024]{1,0:T(8,128)(2,1)S(1)}, u32[]{:S(2)}, u32[]{:S(2)}) collective-permute-start(bf16[256,1024]{1,0:T(8,128)(2,1)S(1)} %add_convert_fusion.4.refs_0_), channel_id=1, source_target_pairs={{0,2},{1,3},{2,0},{3,1},{4,6},{5,7},{6,4},{7,5},{8,10},{9,11},{10,... | collective-permute-start | bytes 1572872 | tf_op jit(solution)/shard_map/ppermute | solution.py:723
  207.0 6.8 %down.4.refs_5_ = bf16[1024,1280]{1,0:T(8,128)(2,1)} custom-call(f32[1,1024]{1,0:T(1,128)} %refs_8_.15, bf16[1024,1024]{1,0:T(8,128)(2,1)} %all-gather.5.cloned.1.call-done.refs_0_, bf16[1024,1280]{1,0:T(8,128)(2,1)} %get-tuple-element.222.am.refs_1_), custom_call_target="tpu_custom_call" | custom-call | tf_op jit(solution)/shard_map/down/pallas_call | solution.py:691
  214.1 5.5 %collective-permute-done.15.refs_2_ = bf16[256,1024]{1,0:T(8,128)(2,1)S(1)} collective-permute-done((bf16[256,1024]{1,0:T(8,128)(2,1)S(1)}, bf16[256,1024]{1,0:T(8,128)(2,1)S(1)}, u32[]{:S(2)}, u32[]{:S(2)}) %collective-permute-start.15) | collective-permute-done | bytes 524320 | tf_op jit(solution)/shard_map/ppermute | solution.py:723
  219.6 1.9 collective-permute-start.17
  221.5 1.9 collective-permute-done.17.refs_3_
  224.2 7.8 %down.7 = (bf16[1024,1280]{1,0:T(8,128)(2,1)}, bf16[1024,1024]{1,0:T(8,128)(2,1)}) custom-call(f32[1,1024]{1,0:T(1,128)} %refs_8_.15, bf16[256,1024]{1,0:T(8,128)(2,1)} %copy-done.10, bf16[256,1024]{1,0:T(8,128)(2,1)} %copy-done.19, bf16[256,1024]{1,0:T(8,128)(2,1)} %copy-done.20, bf16[256,1024]{1,0:T(8,128)(2,1)} %copy-done.21, ...), custom_call_target="tpu_custom_call", output_to_operand_aliasing={{0}: (7, {})} | custom-call | flops 2684354560 | bytes 12582912 | tf_op jit(solution)/shard_map/down/pallas_call | solution.py:691
  232.1 19.6 %backward.7 = (bf16[1024,1024]{1,0:T(8,128)(2,1)}, bf16[1024,768]{1,0:T(8,128)(2,1)}, bf16[2,256,1024]{2,1,0:T(8,128)(2,1)}, bf16[2,256,1024]{2,1,0:T(8,128)(2,1...) custom-call(f32[1,1024]{1,0:T(1,128)} %refs_8_.15, ...), custom_call_target="tpu_custom_call", output_to_operand_aliasing={{0}: (26, {}), {1}: (27, {}), {2}: (28, {}), {3}: (29, {}),... | custom-call | flops 6442450944 | bytes 31457280 | tf_op jit(solution)/shard_map/backward/pallas_call | solution.py:528
  251.7 3.5 fusion.19
  255.3 2.4 fusion.18
  257.7 2.0 add_convert_fusion.1
  260.0 2.6 add_convert_fusion
  262.5 2.1 pad_maximum_fusion
  264.6 20.1 %reduce-scatter.3.cloned.1.call-done = bf16[256,1280]{1,0:T(8,128)(2,1)} async-done(((bf16[1024,1280]{1,0:T(8,128)(2,1)}), bf16[256,1280]{1,0:T(8,128)(2,1)}) %reduce-scatter.3.cloned.1.call-update) | async-done | bytes 655376 | tf_op jit(solution)/shard_map/reduce_scatter | solution.py:771
  285.6 3.3 collective-permute-done.22
  288.8 2.1 collective-permute-start.23
  290.9 3.1 collective-permute-done.23
  294.7 1.7 collective-permute-done.24
  296.4 1.5 collective-permute-start.25
  298.5 1.5 collective-permute-done.25
  300.6 2.0 fusion.14
  302.7 1.5 collective-permute-start.19
  304.2 2.0 fusion.15
  306.9 1.1 slice_bitcast_fusion
  308.0 2.5 copy.83
  311.2 1.8 copy.82
  313.0 4.8 %collective-permute-done.19 = bf16[256,1024]{1,0:T(8,128)(2,1)} collective-permute-done((bf16[256,1024]{1,0:T(8,128)(2,1)}, bf16[256,1024]{1,0:T(8,128)(2,1)}, u32[]{:S(2)}, u32[]{:S(2)}) %collective-permute-start.19) | collective-permute-done | bytes 524320 | tf_op jit(solution)/shard_map/ppermute | solution.py:723
  317.9 9.8 %collective-permute-done.21 = bf16[256,1024]{1,0:T(8,128)(2,1)} collective-permute-done((bf16[256,1024]{1,0:T(8,128)(2,1)}, bf16[256,1024]{1,0:T(8,128)(2,1)}, u32[]{:S(2)}, u32[]{:S(2)}) %collective-permute-start.21) | collective-permute-done | bytes 524320 | tf_op jit(solution)/shard_map/ppermute | solution.py:723
  327.7 2.7 fusion.5
  330.4 1.5 maximum_bitcast_fusion
  331.9 23.1 %reduce-scatter.5.cloned.1.call-done.packed = bf16[256,1792]{1,0:T(8,128)(2,1)} async-done(((bf16[1024,1792]{1,0:T(8,128)(2,1)}), bf16[256,1792]{1,0:T(8,128)(2,1)}) %reduce-scatter.5.cloned.1.call-update) | async-done | bytes 917520 | tf_op jit(solution)/shard_map/reduce_scatter | solution.py:771
  355.0 2.4 unpack.1
  (110 shorter events, 13.6 us)
Async XLA Ops:
  7.2 120.5 %all-gather.3.cloned.1.call-start = ((), (), s32[]{:S(2)}) async-start(), calls=%async_computation.2 | async-start | bytes 2621440 | tf_op jit(solution)/shard_map/all_gather | solution.py:753
  26.4 5.2 %collective-permute-start = (bf16[2,256,1024]{2,1,0:T(8,128)(2,1)}, bf16[2,256,1024]{2,1,0:T(8,128)(2,1)S(1)}, u32[]{:S(2)}, u32[]{:S(2)}) collective-permute-start(bf16[2,256,1024]{2,1,0:T(8,128)(2,1)} %get-tuple-element.144), channel_id=1, source_target_pairs={{0,1},{1,0},{2,3},{3,2},{4,5},{5,4},{6,7},{7,6},{8,9},{9,8},{10,11... | collective-permute-start | bytes 3145736 | tf_op jit(solution)/shard_map/ppermute | solution.py:723
  28.8 2.8 copy-start.12
  28.8 2.8 copy-start.26
  32.7 22.6 %collective-permute-start.1 = (bf16[256,1024]{1,0:T(8,128)(2,1)}, bf16[256,1024]{1,0:T(8,128)(2,1)}, u32[]{:S(2)}, u32[]{:S(2)}) collective-permute-start(bf16[256,1024]{1,0:T(8,128)(2,1)} %fusion.7), channel_id=1, source_target_pairs={{0,16},{1,17},{2,18},{3,19},{4,20},{5,21},{6,22},{7,23},{8,24},{9,... | collective-permute-start | bytes 1572872 | tf_op jit(solution)/shard_map/ppermute | solution.py:747
  35.8 21.4 %collective-permute-start.2 = (bf16[256,1024]{1,0:T(8,128)(2,1)}, bf16[256,1024]{1,0:T(8,128)(2,1)S(1)}, u32[]{:S(2)}, u32[]{:S(2)}) collective-permute-start(bf16[256,1024]{1,0:T(8,128)(2,1)} %fusion.8), channel_id=1, source_target_pairs={{0,18},{1,19},{2,16},{3,17},{4,22},{5,23},{6,20},{7,21},{8,26},{9,... | collective-permute-start | bytes 1572872 | tf_op jit(solution)/shard_map/ppermute | solution.py:747
  55.3 6.7 %copy-start.13 = (bf16[2,256,1024]{2,1,0:T(8,128)(2,1)S(1)}, bf16[2,256,1024]{2,1,0:T(8,128)(2,1)}, u32[]{:S(2)}) copy-start(bf16[2,256,1024]{2,1,0:T(8,128)(2,1)} %get-tuple-element.148) | copy-start | bytes 3145732
  57.2 4.8 %collective-permute-start.3 = (bf16[2,256,1024]{2,1,0:T(8,128)(2,1)}, bf16[2,256,1024]{2,1,0:T(8,128)(2,1)S(1)}, u32[]{:S(2)}, u32[]{:S(2)}) collective-permute-start(bf16[2,256,1024]{2,1,0:T(8,128)(2,1)} %get-tuple-element.149), channel_id=1, source_target_pairs={{0,1},{1,0},{2,3},{3,2},{4,5},{5,4},{6,7},{7,6},{8,9},{9,8},{10,11... | collective-permute-start | bytes 3145736 | tf_op jit(solution)/shard_map/ppermute | solution.py:723
  60.4 11.7 %copy-start.5 = (bf16[256,1024]{1,0:T(8,128)(2,1)}, bf16[256,1024]{1,0:T(8,128)(2,1)S(1)}, u32[]{:S(2)}) copy-start(bf16[256,1024]{1,0:T(8,128)(2,1)S(1)} %add_convert_fusion.11.refs_0_) | copy-start | bytes 1572868
  60.4 11.7 %copy-start = (bf16[2,1,1024,1024]{3,2,1,0:T(8,128)(2,1)S(1)}, bf16[2,1,1024,1024]{3,2,1,0:T(8,128)(2,1)}, u32[]{:S(2)}) copy-start(bf16[2,1,1024,1024]{3,2,1,0:T(8,128)(2,1)} %refs_0_.11) | copy-start | bytes 12582916
  60.4 10.9 %collective-permute-start.6 = (bf16[256,1024]{1,0:T(8,128)(2,1)S(1)}, bf16[256,1024]{1,0:T(8,128)(2,1)S(1)}, u32[]{:S(2)}, u32[]{:S(2)}) collective-permute-start(bf16[256,1024]{1,0:T(8,128)(2,1)S(1)} %add_convert_fusion.11.refs_0_), channel_id=1, source_target_pairs={{16,18},{17,19},{18,16},{19,17},{20,22},{21,23},{22,20},{23,21},{2... | collective-permute-start | bytes 1572872 | tf_op jit(solution)/shard_map/ppermute | solution.py:723
  63.2 8.2 %collective-permute-start.7 = (bf16[256,1024]{1,0:T(8,128)(2,1)S(1)}, bf16[256,1024]{1,0:T(8,128)(2,1)S(1)}, u32[]{:S(2)}, u32[]{:S(2)}) collective-permute-start(bf16[256,1024]{1,0:T(8,128)(2,1)S(1)} %add_convert_fusion.11.refs_0_), channel_id=1, source_target_pairs={{16,17},{17,16},{18,19},{19,18},{20,21},{21,20},{22,23},{23,22},{2... | collective-permute-start | bytes 1572872 | tf_op jit(solution)/shard_map/ppermute | solution.py:723
  63.9 20.3 %collective-permute-start.4 = (bf16[256,1024]{1,0:T(8,128)(2,1)S(1)}, bf16[256,1024]{1,0:T(8,128)(2,1)S(1)}, u32[]{:S(2)}, u32[]{:S(2)}) collective-permute-start(bf16[256,1024]{1,0:T(8,128)(2,1)S(1)} %fusion.6), channel_id=1, source_target_pairs={{0,16},{1,17},{2,18},{3,19},{4,20},{5,21},{6,22},{7,23},{8,24},{9,... | collective-permute-start | bytes 1572872 | tf_op jit(solution)/shard_map/ppermute | solution.py:747
  71.4 1.3 copy-start.16
  71.4 1.3 copy-start.17
  71.4 12.8 %collective-permute-start.8 = (bf16[256,1024]{1,0:T(8,128)(2,1)S(1)}, bf16[256,1024]{1,0:T(8,128)(2,1)S(1)}, u32[]{:S(2)}, u32[]{:S(2)}) collective-permute-start(bf16[256,1024]{1,0:T(8,128)(2,1)S(1)} %collective-permute-done.6.refs_2_), channel_id=1, source_target_pairs={{16,17},{17,16},{18,19},{19,18},{20,21},{21,20},{22,23},{23,22},{2... | collective-permute-start | bytes 1572872 | tf_op jit(solution)/shard_map/ppermute | solution.py:723
  72.7 23.6 %collective-permute-start.5 = (bf16[256,1024]{1,0:T(8,128)(2,1)}, bf16[256,1024]{1,0:T(8,128)(2,1)S(1)}, u32[]{:S(2)}, u32[]{:S(2)}) collective-permute-start(bf16[256,1024]{1,0:T(8,128)(2,1)} %fusion.9), channel_id=1, source_target_pairs={{0,18},{1,19},{2,16},{3,17},{4,22},{5,23},{6,20},{7,21},{8,26},{9,... | collective-permute-start | bytes 1572872 | tf_op jit(solution)/shard_map/ppermute | solution.py:747
  84.2 1.0 copy-start.22
  84.2 0.8 copy-start.18
  85.2 11.1 %copy-start.23 = (bf16[256,1024]{1,0:T(8,128)(2,1)S(1)}, bf16[256,1024]{1,0:T(8,128)(2,1)}, u32[]{:S(2)}) copy-start(bf16[256,1024]{1,0:T(8,128)(2,1)} %copy-done.22) | copy-start | bytes 1572868
  97.4 79.6 %all-gather.5.cloned.1.call-start = ((), (), s32[]{:S(2)}) async-start(), calls=%async_computation.3 | async-start | bytes 2621440 | tf_op jit(solution)/shard_map/all_gather | solution.py:753
  98.2 0.7 collective-permute-start.9
  100.6 42.5 %collective-permute-start.11 = (bf16[256,1024]{1,0:T(8,128)(2,1)S(1)}, bf16[256,1024]{1,0:T(8,128)(2,1)S(1)}, u32[]{:S(2)}, u32[]{:S(2)}) collective-permute-start(bf16[256,1024]{1,0:T(8,128)(2,1)S(1)} %get-tuple-element.292), channel_id=1, source_target_pairs={{16,2},{17,3},{18,0},{19,1},{20,6},{21,7},{22,4},{23,5},{24,10},{2... | collective-permute-start | bytes 1572872 | tf_op jit(solution)/shard_map/ppermute | solution.py:747
  101.9 50.5 %collective-permute-start.10 = (bf16[256,1024]{1,0:T(8,128)(2,1)S(1)}, bf16[256,1024]{1,0:T(8,128)(2,1)S(1)}, u32[]{:S(2)}, u32[]{:S(2)}) collective-permute-start(bf16[256,1024]{1,0:T(8,128)(2,1)S(1)} %get-tuple-element.293), channel_id=1, source_target_pairs={{16,0},{17,1},{18,2},{19,3},{20,4},{21,5},{22,6},{23,7},{24,8},{25... | collective-permute-start | bytes 1572872 | tf_op jit(solution)/shard_map/ppermute | solution.py:747
  153.4 131.3 %reduce-scatter.3.cloned.1.call-start = ((), (), s32[]{:S(2)}) async-start(), calls=%async_computation.4 | async-start | bytes 3276800 | tf_op jit(solution)/shard_map/reduce_scatter | solution.py:771
  154.5 0.7 collective-permute-start.12
  156.9 39.5 %collective-permute-start.14 = (bf16[256,1024]{1,0:T(8,128)(2,1)S(1)}, bf16[256,1024]{1,0:T(8,128)(2,1)S(1)}, u32[]{:S(2)}, u32[]{:S(2)}) collective-permute-start(bf16[256,1024]{1,0:T(8,128)(2,1)S(1)} %get-tuple-element.290), channel_id=1, source_target_pairs={{16,2},{17,3},{18,0},{19,1},{20,6},{21,7},{22,4},{23,5},{24,10},{2... | collective-permute-start | bytes 1572872 | tf_op jit(solution)/shard_map/ppermute | solution.py:747
  158.2 42.7 %collective-permute-start.13 = (bf16[256,1024]{1,0:T(8,128)(2,1)S(1)}, bf16[256,1024]{1,0:T(8,128)(2,1)S(1)}, u32[]{:S(2)}, u32[]{:S(2)}) collective-permute-start(bf16[256,1024]{1,0:T(8,128)(2,1)S(1)} %get-tuple-element.291), channel_id=1, source_target_pairs={{16,0},{17,1},{18,2},{19,3},{20,4},{21,5},{22,6},{23,7},{24,8},{25... | collective-permute-start | bytes 1572872 | tf_op jit(solution)/shard_map/ppermute | solution.py:747
  201.1 12.7 %copy-start.10 = (bf16[256,1024]{1,0:T(8,128)(2,1)}, bf16[256,1024]{1,0:T(8,128)(2,1)S(1)}, u32[]{:S(2)}) copy-start(bf16[256,1024]{1,0:T(8,128)(2,1)S(1)} %add_convert_fusion.4.refs_0_) | copy-start | bytes 1572868
  201.1 12.9 %collective-permute-start.16 = (bf16[256,1024]{1,0:T(8,128)(2,1)S(1)}, bf16[256,1024]{1,0:T(8,128)(2,1)S(1)}, u32[]{:S(2)}, u32[]{:S(2)}) collective-permute-start(bf16[256,1024]{1,0:T(8,128)(2,1)S(1)} %add_convert_fusion.4.refs_0_), channel_id=1, source_target_pairs={{0,1},{1,0},{2,3},{3,2},{4,5},{5,4},{6,7},{7,6},{8,9},{9,8},{10,11... | collective-permute-start | bytes 1572872 | tf_op jit(solution)/shard_map/ppermute | solution.py:723
  203.1 16.5 %collective-permute-start.15 = (bf16[256,1024]{1,0:T(8,128)(2,1)S(1)}, bf16[256,1024]{1,0:T(8,128)(2,1)S(1)}, u32[]{:S(2)}, u32[]{:S(2)}) collective-permute-start(bf16[256,1024]{1,0:T(8,128)(2,1)S(1)} %add_convert_fusion.4.refs_0_), channel_id=1, source_target_pairs={{0,2},{1,3},{2,0},{3,1},{4,6},{5,7},{6,4},{7,5},{8,10},{9,11},{10,... | collective-permute-start | bytes 1572872 | tf_op jit(solution)/shard_map/ppermute | solution.py:723
  214.1 9.3 %copy-start.19 = (bf16[256,1024]{1,0:T(8,128)(2,1)}, bf16[256,1024]{1,0:T(8,128)(2,1)S(1)}, u32[]{:S(2)}) copy-start(bf16[256,1024]{1,0:T(8,128)(2,1)S(1)} %collective-permute-done.16.refs_1_) | copy-start | bytes 1572868
  219.6 3.8 %copy-start.20 = (bf16[256,1024]{1,0:T(8,128)(2,1)}, bf16[256,1024]{1,0:T(8,128)(2,1)S(1)}, u32[]{:S(2)}) copy-start(bf16[256,1024]{1,0:T(8,128)(2,1)S(1)} %collective-permute-done.15.refs_2_) | copy-start | bytes 1572868
  219.6 3.8 %collective-permute-start.17 = (bf16[256,1024]{1,0:T(8,128)(2,1)S(1)}, bf16[256,1024]{1,0:T(8,128)(2,1)S(1)}, u32[]{:S(2)}, u32[]{:S(2)}) collective-permute-start(bf16[256,1024]{1,0:T(8,128)(2,1)S(1)} %collective-permute-done.15.refs_2_), channel_id=1, source_target_pairs={{0,1},{1,0},{2,3},{3,2},{4,5},{5,4},{6,7},{7,6},{8,9},{9,8},{10,11... | collective-permute-start | bytes 1572872 | tf_op jit(solution)/shard_map/ppermute | solution.py:723
  223.4 0.8 copy-start.21
  232.0 123.0 %reduce-scatter.5.cloned.1.call-start = ((), (), s32[]{:S(2)}) async-start(), calls=%async_computation.5 | async-start | bytes 4587520 | tf_op jit(solution)/shard_map/reduce_scatter | solution.py:771
  232.1 19.6 %copy-start.6 = (bf16[1024,1024]{1,0:T(8,128)(2,1)S(1)}, bf16[1024,1024]{1,0:T(8,128)(2,1)}, u32[]{:S(2)}) copy-start(bf16[1024,1024]{1,0:T(8,128)(2,1)} %get-tuple-element.254) | copy-start | bytes 6291460
  251.7 3.5 copy-start.1
  251.7 3.5 copy-start.7
  255.2 2.5 copy-start.8
  255.2 2.5 copy-start.11
  257.7 2.0 copy-start.2
  257.7 2.2 copy-start.9
  264.6 20.2 %copy-start.24 = (f32[8,1024]{1,0:T(8,128)S(1)}, f32[8,1024]{1,0:T(8,128)}, u32[]{:S(2)}) copy-start(f32[8,1024]{1,0:T(8,128)} %get-tuple-element.266) | copy-start | bytes 98308
  264.6 20.2 %copy-start.25 = (f32[8,1024]{1,0:T(8,128)S(1)}, f32[8,1024]{1,0:T(8,128)}, u32[]{:S(2)}) copy-start(f32[8,1024]{1,0:T(8,128)} %get-tuple-element.267) | copy-start | bytes 98308
  264.6 29.4 %copy-start.14 = (bf16[2,256,1024]{2,1,0:T(8,128)(2,1)S(1)}, bf16[2,256,1024]{2,1,0:T(8,128)(2,1)}, u32[]{:S(2)}) copy-start(bf16[2,256,1024]{2,1,0:T(8,128)(2,1)} %get-tuple-element.265) | copy-start | bytes 3145732
  264.6 36.0 %copy-start.4 = (bf16[2,256,1024]{2,1,0:T(8,128)(2,1)S(1)}, bf16[2,256,1024]{2,1,0:T(8,128)(2,1)}, u32[]{:S(2)}) copy-start(bf16[2,256,1024]{2,1,0:T(8,128)(2,1)} %get-tuple-element.258) | copy-start | bytes 3145732
  264.6 39.6 %copy-start.3 = (bf16[2,256,1024]{2,1,0:T(8,128)(2,1)S(1)}, bf16[2,256,1024]{2,1,0:T(8,128)(2,1)}, u32[]{:S(2)}) copy-start(bf16[2,256,1024]{2,1,0:T(8,128)(2,1)} %get-tuple-element.264) | copy-start | bytes 3145732
  284.7 15.9 %collective-permute-start.18 = (bf16[2,256,1024]{2,1,0:T(8,128)(2,1)}, bf16[2,256,1024]{2,1,0:T(8,128)(2,1)}, u32[]{:S(2)}, u32[]{:S(2)}) collective-permute-start(bf16[2,256,1024]{2,1,0:T(8,128)(2,1)} %get-tuple-element.259), channel_id=1, source_target_pairs={{0,1},{1,0},{2,3},{3,2},{16,17},{17,16},{18,19},{19,18},{4,5},{5,4... | collective-permute-start | bytes 3145736 | tf_op jit(solution)/shard_map/ppermute | solution.py:723
  284.8 4.0 %collective-permute-start.22 = (f32[8,1024]{1,0:T(8,128)S(1)}, f32[8,1024]{1,0:T(8,128)S(1)}, u32[]{:S(2)}, u32[]{:S(2)}) collective-permute-start(f32[8,1024]{1,0:T(8,128)S(1)} %add.201), channel_id=1, source_target_pairs={{0,4},{4,0},{8,12},{12,8},{1,5},{5,1},{9,13},{13,9},{2,6},{6,2},{1... | collective-permute-start | bytes 98312 | tf_op jit(solution)/shard_map/ppermute | solution.py:763
  288.8 5.2 %collective-permute-start.23 = (f32[8,1024]{1,0:T(8,128)S(1)}, f32[8,1024]{1,0:T(8,128)S(1)}, u32[]{:S(2)}, u32[]{:S(2)}) collective-permute-start(f32[8,1024]{1,0:T(8,128)S(1)} %add.202), channel_id=1, source_target_pairs={{0,8},{4,12},{8,0},{12,4},{1,9},{5,13},{9,1},{13,5},{2,10},{6,14},... | collective-permute-start | bytes 98312 | tf_op jit(solution)/shard_map/ppermute | solution.py:763
  294.0 10.2 %collective-permute-start.20 = (bf16[2,256,1024]{2,1,0:T(8,128)(2,1)S(1)}, bf16[2,256,1024]{2,1,0:T(8,128)(2,1)}, u32[]{:S(2)}, u32[]{:S(2)}) collective-permute-start(bf16[2,256,1024]{2,1,0:T(8,128)(2,1)S(1)} %copy-done.14), channel_id=1, source_target_pairs={{0,1},{1,0},{2,3},{3,2},{16,17},{17,16},{18,19},{19,18},{4,5},{5,4... | collective-permute-start | bytes 3145736 | tf_op jit(solution)/shard_map/ppermute | solution.py:723
  294.1 2.3 collective-permute-start.24
  294.7 12.1 %copy-start.15 = (bf16[256,1280]{1,0:T(8,128)(2,1)S(1)}, bf16[256,1280]{1,0:T(8,128)(2,1)}, u32[]{:S(2)}) copy-start(bf16[256,1280]{1,0:T(8,128)(2,1)} %reduce-scatter.3.cloned.1.call-done) | copy-start | bytes 1966084
  296.4 3.7 %collective-permute-start.25 = (f32[5,256]{1,0:T(8,128)S(1)}, f32[5,256]{1,0:T(8,128)S(1)}, u32[]{:S(2)}, u32[]{:S(2)}) collective-permute-start(f32[5,256]{1,0:T(8,128)S(1)} %fusion.28), channel_id=1, source_target_pairs={{0,2},{1,3},{2,0},{3,1},{4,6},{5,7},{6,4},{7,5},{8,10},{9,11},{10,... | collective-permute-start | bytes 15368 | tf_op jit(solution)/shard_map/ppermute | solution.py:763
  302.7 15.2 %collective-permute-start.19 = (bf16[256,1024]{1,0:T(8,128)(2,1)}, bf16[256,1024]{1,0:T(8,128)(2,1)}, u32[]{:S(2)}, u32[]{:S(2)}) collective-permute-start(bf16[256,1024]{1,0:T(8,128)(2,1)} %fusion.14), channel_id=1, source_target_pairs={{0,2},{1,3},{2,0},{3,1},{16,18},{17,19},{18,16},{19,17},{4,6},{5,7... | collective-permute-start | bytes 1572872 | tf_op jit(solution)/shard_map/ppermute | solution.py:723
  306.2 21.5 %collective-permute-start.21 = (bf16[256,1024]{1,0:T(8,128)(2,1)}, bf16[256,1024]{1,0:T(8,128)(2,1)}, u32[]{:S(2)}, u32[]{:S(2)}) collective-permute-start(bf16[256,1024]{1,0:T(8,128)(2,1)} %fusion.15), channel_id=1, source_target_pairs={{0,2},{1,3},{2,0},{3,1},{16,18},{17,19},{18,16},{19,17},{4,6},{5,7... | collective-permute-start | bytes 1572872 | tf_op jit(solution)/shard_map/ppermute | solution.py:723
Sparse Core Ops, SparseCore 0:
  97.5 30.1 all-gather.2
  153.6 23.3 all-gather.4
  232.1 52.5 reduce-scatter.2
  286.9 68.0 reduce-scatter.4

commit v6 on v5

--- a/solution.py
+++ b/solution.py
@@ -204,9 +204,9 @@
         else:
             state[...] = jnp.zeros_like(state)
             total[...] = jnp.zeros_like(total)
+        wait(in_h)
         in_c = io.start((wup.at[0], v_wup), (wo.at[0], v_wo), (wdown.at[0], v_wdown),
                         *([] if cfg["branch"] else [(cotangent.at[cfg["m"], 0], v_g)]))
-        wait(in_h)
         out_h = io.start(*([(v_h, s_h.at[pl.ds(base, rows)])] if cfg["section"] else []), (v_h.at[rows_at(me, rows // 4)], own))
 
         @pl.loop(0, blocks)
@@ -806,8 +806,8 @@
     *took_1, ends_0[0] = tie_all(*took_1, ends_0[0])
     grad_1 = summed(own_c[1], took_1).astype(BF)
     far_rows = swap(grad_1, 0, 2)
-    (acc,) = down_call(0, 0, tie(order, grad_1), [gb_0], store_0[2])
     near_rows = swap(grad_1, 0, 1)
+    (acc,) = down_call(0, 0, tie(order, near_rows), [gb_0], store_0[2])
     (acc_b,) = down_call(0, 1, tie(order, acc), [cotangent], store_0[2])
     (down_sum,) = down_call(1, 1, order, [cotangent], store_1[2], acc_b)
     far_rows, near_rows, down_sum = tie_all(far_rows, near_rows, down_sum)

time: 371 us -> 371 us (level)
  no operation moved by 1% of the time
where the time goes in v6:
time: 371 us; the launch traced here: 364 us
  waiting for transfers between devices  158 us (43%)
  Pallas kernels  96 us (26%)
  starting transfers between devices  50.2 us (14%)
  other arithmetic  21.2 us (6%)
  between operations  15 us (4%)
  local copies, waits for them, and re-layouts  13.6 us (4%)
  matrix products  10.5 us (3%)
    reduce_scatter x2, waiting for transfers between devices, scatter(): return lax.psum_scatter(total, 'dp', scatter_dimension=0, tiled=True)  43.2 us
    all_gather x2, waiting for transfers between devices, whole_rows(): return lax.all_gather(own, 'tensor', axis=0, tiled=True)  41.9 us
    pallas_call x4, Pallas kernels, backward_call(): pl.pallas_call(functools.partial(backward_kernel, cfg), out_shape=shapes,...  40.7 us
    pallas_call x4, Pallas kernels, forward_call(): pl.pallas_call(functools.partial(forward_kernel, cfg), out_shape=shapes,...  37.7 us
    ppermute x4, waiting for transfers between devices, relay(): lax.ppermute(sent, both, pairs[1])  26.7 us
    ppermute x14, waiting for transfers between devices, swap(): lax.ppermute(x, both, [(k * teams + i, k * teams + (i ^ bit)) for k in se...  22.5 us
    ppermute x14, starting transfers between devices, swap(): lax.ppermute(x, both, [(k * teams + i, k * teams + (i ^ bit)) for k in se...  17.9 us
    ppermute x4, starting transfers between devices, relay(): lax.ppermute(sent, both, pairs[1])  15.4 us
  transfers between devices with their start and end apart: 30, of which 18 were waited for; matrix products, arithmetic and copies ran while one was open for 11% of the time, Pallas kernels for 19%

profile of v6, /device:TPU:0, one launch (start us, length us, event | category | flops | bytes accessed | tf_op | source)
XLA Modules:
  0.0 364.4 jit_solution(2791853406181605418)
XLA Ops:
  7.2 1.3 copy.69.refs_16_.refs_19_.refs_17_
  8.5 17.9 %forward.4 = (bf16[1024,1024]{1,0:T(8,128)(2,1)}, bf16[1024,1024]{1,0:T(8,128)(2,1)}, bf16[1024,1280]{1,0:T(8,128)(2,1)}, bf16[1024,1024]{1,0:T(8,128)(2,1)}, bf...) custom-call(f32[1,1024]{1,0:T(1,128)} %refs_8_.15, ...), custom_call_target="tpu_custom_call" | custom-call | flops 6442450944 | bytes 26214400 | tf_op jit(solution)/shard_map/forward/pallas_call | solution.py:496
  26.4 2.4 collective-permute-start
  28.8 2.8 fusion.17
  31.7 1.0 fusion.7
  32.7 2.1 collective-permute-start.1
  34.8 1.0 fusion.8
  35.8 1.3 collective-permute-start.2
  37.1 18.2 %forward.5 = (bf16[1024,1024]{1,0:T(8,128)(2,1)}, bf16[1024,1024]{1,0:T(8,128)(2,1)}, bf16[1024,1280]{1,0:T(8,128)(2,1)}, bf16[1024,1024]{1,0:T(8,128)(2,1)}, bf...) custom-call(f32[1,1024]{1,0:T(1,128)} %refs_8_.15, ...), custom_call_target="tpu_custom_call" | custom-call | flops 6442450944 | bytes 26214400 | tf_op jit(solution)/shard_map/forward/pallas_call | solution.py:496
  55.3 1.8 collective-permute-done.2
  57.2 1.9 collective-permute-start.3
  59.1 1.3 add_convert_fusion.11.refs_0_
  61.9 1.0 fusion.9
  63.8 7.5 %collective-permute-start.4 = (bf16[256,1024]{1,0:T(8,128)(2,1)S(1)}, bf16[256,1024]{1,0:T(8,128)(2,1)S(1)}, u32[]{:S(2)}, u32[]{:S(2)}) collective-permute-start(bf16[256,1024]{1,0:T(8,128)(2,1)S(1)} %fusion.6), channel_id=1, source_target_pairs={{0,16},{1,17},{2,18},{3,19},{4,20},{5,21},{6,22},{7,23},{8,24},{9,... | collective-permute-start | bytes 1572872 | tf_op jit(solution)/shard_map/ppermute | solution.py:747
  72.7 11.5 %collective-permute-start.5 = (bf16[256,1024]{1,0:T(8,128)(2,1)}, bf16[256,1024]{1,0:T(8,128)(2,1)S(1)}, u32[]{:S(2)}, u32[]{:S(2)}) collective-permute-start(bf16[256,1024]{1,0:T(8,128)(2,1)} %fusion.9), channel_id=1, source_target_pairs={{0,18},{1,19},{2,16},{3,17},{4,22},{5,23},{6,20},{7,21},{8,26},{9,... | collective-permute-start | bytes 1572872 | tf_op jit(solution)/shard_map/ppermute | solution.py:747
  85.9 10.3 %collective-permute-done.5 = bf16[256,1024]{1,0:T(8,128)(2,1)S(1)} collective-permute-done((bf16[256,1024]{1,0:T(8,128)(2,1)}, bf16[256,1024]{1,0:T(8,128)(2,1)S(1)}, u32[]{:S(2)}, u32[]{:S(2)}) %collective-permute-start.5) | collective-permute-done | bytes 524320 | tf_op jit(solution)/shard_map/ppermute | solution.py:747
  96.3 1.1 add_convert_fusion.10
  99.0 1.6 fusion.11
  100.6 1.3 collective-permute-start.11
  101.9 1.3 collective-permute-start.10
  103.2 24.5 %all-gather.3.cloned.1.call-done.refs_0_ = bf16[1024,1024]{1,0:T(8,128)(2,1)} async-done(((bf16[256,1024]{1,0:T(8,128)(2,1)}), bf16[1024,1024]{1,0:T(8,128)(2,1)}) %all-gather.3.cloned.1.call-update) | async-done | bytes 2097168 | tf_op jit(solution)/shard_map/all_gather | solution.py:753
  127.7 0.8 forward.7
  128.5 14.5 %collective-permute-done.11 = bf16[256,1024]{1,0:T(8,128)(2,1)S(1)} collective-permute-done((bf16[256,1024]{1,0:T(8,128)(2,1)S(1)}, bf16[256,1024]{1,0:T(8,128)(2,1)S(1)}, u32[]{:S(2)}, u32[]{:S(2)}) %collective-permute-start.11) | collective-permute-done | bytes 524320 | tf_op jit(solution)/shard_map/ppermute | solution.py:747
  143.0 9.3 %collective-permute-done.10 = bf16[256,1024]{1,0:T(8,128)(2,1)S(1)} collective-permute-done((bf16[256,1024]{1,0:T(8,128)(2,1)S(1)}, bf16[256,1024]{1,0:T(8,128)(2,1)S(1)}, u32[]{:S(2)}, u32[]{:S(2)}) %collective-permute-start.10) | collective-permute-done | bytes 524320 | tf_op jit(solution)/shard_map/ppermute | solution.py:747
  152.4 1.1 add_convert_fusion.7
  153.5 1.0 backward.5
  155.3 1.6 fusion.13
  156.9 1.3 collective-permute-start.14
  158.2 1.3 collective-permute-start.13
  159.5 17.4 %all-gather.5.cloned.1.call-done.refs_0_ = bf16[1024,1024]{1,0:T(8,128)(2,1)} async-done(((bf16[256,1024]{1,0:T(8,128)(2,1)}), bf16[1024,1024]{1,0:T(8,128)(2,1)}) %all-gather.5.cloned.1.call-update) | async-done | bytes 2097168 | tf_op jit(solution)/shard_map/all_gather | solution.py:753
  177.0 19.4 %backward.6 = (bf16[1024,1024]{1,0:T(8,128)(2,1)}, bf16[1024,768]{1,0:T(8,128)(2,1)}, bf16[2,256,1024]{2,1,0:T(8,128)(2,1)}, bf16[2,256,1024]{2,1,0:T(8,128)(2,1...) custom-call(f32[1,1024]{1,0:T(1,128)} %refs_8_.15, ...), custom_call_target="tpu_custom_call", output_to_operand_aliasing={{0}: (26, {}), {1}: (27, {}), {2}: (28, {}), {3}: (29, {}),... | custom-call | flops 6442450944 | bytes 31457280 | tf_op jit(solution)/shard_map/backward/pallas_call | solution.py:528
  196.4 4.5 %collective-permute-done.13 = bf16[256,1024]{1,0:T(8,128)(2,1)S(1)} collective-permute-done((bf16[256,1024]{1,0:T(8,128)(2,1)S(1)}, bf16[256,1024]{1,0:T(8,128)(2,1)S(1)}, u32[]{:S(2)}, u32[]{:S(2)}) %collective-permute-start.13) | collective-permute-done | bytes 524320 | tf_op jit(solution)/shard_map/ppermute | solution.py:747
  201.2 1.9 collective-permute-start.16
  203.1 3.9 %collective-permute-start.15 = (bf16[256,1024]{1,0:T(8,128)(2,1)S(1)}, bf16[256,1024]{1,0:T(8,128)(2,1)S(1)}, u32[]{:S(2)}, u32[]{:S(2)}) collective-permute-start(bf16[256,1024]{1,0:T(8,128)(2,1)S(1)} %add_convert_fusion.4.refs_0_), channel_id=1, source_target_pairs={{0,2},{1,3},{2,0},{3,1},{4,6},{5,7},{6,4},{7,5},{8,10},{9,11},{10,... | collective-permute-start | bytes 1572872 | tf_op jit(solution)/shard_map/ppermute | solution.py:723
  207.0 7.0 %down.4.refs_5_ = bf16[1024,1280]{1,0:T(8,128)(2,1)} custom-call(f32[1,1024]{1,0:T(1,128)} %refs_8_.15, bf16[1024,1024]{1,0:T(8,128)(2,1)} %all-gather.5.cloned.1.call-done.refs_0_, bf16[1024,1280]{1,0:T(8,128)(2,1)} %get-tuple-element.222.am.refs_1_), custom_call_target="tpu_custom_call" | custom-call | tf_op jit(solution)/shard_map/down/pallas_call | solution.py:691
  214.3 5.3 %collective-permute-done.15.refs_2_ = bf16[256,1024]{1,0:T(8,128)(2,1)S(1)} collective-permute-done((bf16[256,1024]{1,0:T(8,128)(2,1)S(1)}, bf16[256,1024]{1,0:T(8,128)(2,1)S(1)}, u32[]{:S(2)}, u32[]{:S(2)}) %collective-permute-start.15) | collective-permute-done | bytes 524320 | tf_op jit(solution)/shard_map/ppermute | solution.py:723
  219.6 1.9 collective-permute-start.17
  221.5 1.9 collective-permute-done.17.refs_3_
  224.2 7.8 %down.7 = (bf16[1024,1280]{1,0:T(8,128)(2,1)}, bf16[1024,1024]{1,0:T(8,128)(2,1)}) custom-call(f32[1,1024]{1,0:T(1,128)} %refs_8_.15, bf16[256,1024]{1,0:T(8,128)(2,1)} %copy-done.10, bf16[256,1024]{1,0:T(8,128)(2,1)} %copy-done.19, bf16[256,1024]{1,0:T(8,128)(2,1)} %copy-done.20, bf16[256,1024]{1,0:T(8,128)(2,1)} %copy-done.21, ...), custom_call_target="tpu_custom_call", output_to_operand_aliasing={{0}: (7, {})} | custom-call | flops 2684354560 | bytes 12582912 | tf_op jit(solution)/shard_map/down/pallas_call | solution.py:691
  232.1 19.5 %backward.7 = (bf16[1024,1024]{1,0:T(8,128)(2,1)}, bf16[1024,768]{1,0:T(8,128)(2,1)}, bf16[2,256,1024]{2,1,0:T(8,128)(2,1)}, bf16[2,256,1024]{2,1,0:T(8,128)(2,1...) custom-call(f32[1,1024]{1,0:T(1,128)} %refs_8_.15, ...), custom_call_target="tpu_custom_call", output_to_operand_aliasing={{0}: (26, {}), {1}: (27, {}), {2}: (28, {}), {3}: (29, {}),... | custom-call | flops 6442450944 | bytes 31457280 | tf_op jit(solution)/shard_map/backward/pallas_call | solution.py:528
  251.7 3.5 fusion.19
  255.2 2.4 fusion.18
  257.7 2.0 add_convert_fusion.1
  259.9 2.6 add_convert_fusion
  262.5 2.1 pad_maximum_fusion
  264.6 20.1 %reduce-scatter.3.cloned.1.call-done = bf16[256,1280]{1,0:T(8,128)(2,1)} async-done(((bf16[1024,1280]{1,0:T(8,128)(2,1)}), bf16[256,1280]{1,0:T(8,128)(2,1)}) %reduce-scatter.3.cloned.1.call-update) | async-done | bytes 655376 | tf_op jit(solution)/shard_map/reduce_scatter | solution.py:771
  285.5 3.3 collective-permute-done.22
  288.8 2.1 collective-permute-start.23
  290.9 3.1 collective-permute-done.23
  294.7 1.7 collective-permute-done.24
  296.4 1.5 collective-permute-start.25
  298.5 1.5 collective-permute-done.25
  300.7 2.0 fusion.14
  302.7 1.5 collective-permute-start.19
  304.2 2.0 fusion.15
  306.9 1.1 slice_bitcast_fusion
  308.0 2.5 copy.83
  311.2 1.8 copy.82
  313.0 4.8 %collective-permute-done.19 = bf16[256,1024]{1,0:T(8,128)(2,1)} collective-permute-done((bf16[256,1024]{1,0:T(8,128)(2,1)}, bf16[256,1024]{1,0:T(8,128)(2,1)}, u32[]{:S(2)}, u32[]{:S(2)}) %collective-permute-start.19) | collective-permute-done | bytes 524320 | tf_op jit(solution)/shard_map/ppermute | solution.py:723
  317.9 9.8 %collective-permute-done.21 = bf16[256,1024]{1,0:T(8,128)(2,1)} collective-permute-done((bf16[256,1024]{1,0:T(8,128)(2,1)}, bf16[256,1024]{1,0:T(8,128)(2,1)}, u32[]{:S(2)}, u32[]{:S(2)}) %collective-permute-start.21) | collective-permute-done | bytes 524320 | tf_op jit(solution)/shard_map/ppermute | solution.py:723
  327.7 2.7 fusion.5
  330.4 1.5 maximum_bitcast_fusion
  331.9 23.1 %reduce-scatter.5.cloned.1.call-done.packed = bf16[256,1792]{1,0:T(8,128)(2,1)} async-done(((bf16[1024,1792]{1,0:T(8,128)(2,1)}), bf16[256,1792]{1,0:T(8,128)(2,1)}) %reduce-scatter.5.cloned.1.call-update) | async-done | bytes 917520 | tf_op jit(solution)/shard_map/reduce_scatter | solution.py:771
  355.0 2.4 unpack.1
  (110 shorter events, 13.6 us)
Async XLA Ops:
  7.2 120.5 %all-gather.3.cloned.1.call-start = ((), (), s32[]{:S(2)}) async-start(), calls=%async_computation.2 | async-start | bytes 2621440 | tf_op jit(solution)/shard_map/all_gather | solution.py:753
  26.4 5.2 %collective-permute-start = (bf16[2,256,1024]{2,1,0:T(8,128)(2,1)}, bf16[2,256,1024]{2,1,0:T(8,128)(2,1)S(1)}, u32[]{:S(2)}, u32[]{:S(2)}) collective-permute-start(bf16[2,256,1024]{2,1,0:T(8,128)(2,1)} %get-tuple-element.144), channel_id=1, source_target_pairs={{0,1},{1,0},{2,3},{3,2},{4,5},{5,4},{6,7},{7,6},{8,9},{9,8},{10,11... | collective-permute-start | bytes 3145736 | tf_op jit(solution)/shard_map/ppermute | solution.py:723
  28.8 2.8 copy-start.12
  28.8 2.8 copy-start.26
  32.7 22.6 %collective-permute-start.1 = (bf16[256,1024]{1,0:T(8,128)(2,1)}, bf16[256,1024]{1,0:T(8,128)(2,1)}, u32[]{:S(2)}, u32[]{:S(2)}) collective-permute-start(bf16[256,1024]{1,0:T(8,128)(2,1)} %fusion.7), channel_id=1, source_target_pairs={{0,16},{1,17},{2,18},{3,19},{4,20},{5,21},{6,22},{7,23},{8,24},{9,... | collective-permute-start | bytes 1572872 | tf_op jit(solution)/shard_map/ppermute | solution.py:747
  35.8 21.4 %collective-permute-start.2 = (bf16[256,1024]{1,0:T(8,128)(2,1)}, bf16[256,1024]{1,0:T(8,128)(2,1)S(1)}, u32[]{:S(2)}, u32[]{:S(2)}) collective-permute-start(bf16[256,1024]{1,0:T(8,128)(2,1)} %fusion.8), channel_id=1, source_target_pairs={{0,18},{1,19},{2,16},{3,17},{4,22},{5,23},{6,20},{7,21},{8,26},{9,... | collective-permute-start | bytes 1572872 | tf_op jit(solution)/shard_map/ppermute | solution.py:747
  55.3 6.6 %copy-start.13 = (bf16[2,256,1024]{2,1,0:T(8,128)(2,1)S(1)}, bf16[2,256,1024]{2,1,0:T(8,128)(2,1)}, u32[]{:S(2)}) copy-start(bf16[2,256,1024]{2,1,0:T(8,128)(2,1)} %get-tuple-element.148) | copy-start | bytes 3145732
  57.2 4.8 %collective-permute-start.3 = (bf16[2,256,1024]{2,1,0:T(8,128)(2,1)}, bf16[2,256,1024]{2,1,0:T(8,128)(2,1)S(1)}, u32[]{:S(2)}, u32[]{:S(2)}) collective-permute-start(bf16[2,256,1024]{2,1,0:T(8,128)(2,1)} %get-tuple-element.149), channel_id=1, source_target_pairs={{0,1},{1,0},{2,3},{3,2},{4,5},{5,4},{6,7},{7,6},{8,9},{9,8},{10,11... | collective-permute-start | bytes 3145736 | tf_op jit(solution)/shard_map/ppermute | solution.py:723
  60.4 11.7 %copy-start.5 = (bf16[256,1024]{1,0:T(8,128)(2,1)}, bf16[256,1024]{1,0:T(8,128)(2,1)S(1)}, u32[]{:S(2)}) copy-start(bf16[256,1024]{1,0:T(8,128)(2,1)S(1)} %add_convert_fusion.11.refs_0_) | copy-start | bytes 1572868
  60.4 11.7 %copy-start = (bf16[2,1,1024,1024]{3,2,1,0:T(8,128)(2,1)S(1)}, bf16[2,1,1024,1024]{3,2,1,0:T(8,128)(2,1)}, u32[]{:S(2)}) copy-start(bf16[2,1,1024,1024]{3,2,1,0:T(8,128)(2,1)} %refs_0_.11) | copy-start | bytes 12582916
  60.4 10.9 %collective-permute-start.6 = (bf16[256,1024]{1,0:T(8,128)(2,1)S(1)}, bf16[256,1024]{1,0:T(8,128)(2,1)S(1)}, u32[]{:S(2)}, u32[]{:S(2)}) collective-permute-start(bf16[256,1024]{1,0:T(8,128)(2,1)S(1)} %add_convert_fusion.11.refs_0_), channel_id=1, source_target_pairs={{16,18},{17,19},{18,16},{19,17},{20,22},{21,23},{22,20},{23,21},{2... | collective-permute-start | bytes 1572872 | tf_op jit(solution)/shard_map/ppermute | solution.py:723
  63.1 8.2 %collective-permute-start.7 = (bf16[256,1024]{1,0:T(8,128)(2,1)S(1)}, bf16[256,1024]{1,0:T(8,128)(2,1)S(1)}, u32[]{:S(2)}, u32[]{:S(2)}) collective-permute-start(bf16[256,1024]{1,0:T(8,128)(2,1)S(1)} %add_convert_fusion.11.refs_0_), channel_id=1, source_target_pairs={{16,17},{17,16},{18,19},{19,18},{20,21},{21,20},{22,23},{23,22},{2... | collective-permute-start | bytes 1572872 | tf_op jit(solution)/shard_map/ppermute | solution.py:723
  63.8 20.3 %collective-permute-start.4 = (bf16[256,1024]{1,0:T(8,128)(2,1)S(1)}, bf16[256,1024]{1,0:T(8,128)(2,1)S(1)}, u32[]{:S(2)}, u32[]{:S(2)}) collective-permute-start(bf16[256,1024]{1,0:T(8,128)(2,1)S(1)} %fusion.6), channel_id=1, source_target_pairs={{0,16},{1,17},{2,18},{3,19},{4,20},{5,21},{6,22},{7,23},{8,24},{9,... | collective-permute-start | bytes 1572872 | tf_op jit(solution)/shard_map/ppermute | solution.py:747
  71.3 1.3 copy-start.16
  71.4 1.3 copy-start.17
  71.4 12.8 %collective-permute-start.8 = (bf16[256,1024]{1,0:T(8,128)(2,1)S(1)}, bf16[256,1024]{1,0:T(8,128)(2,1)S(1)}, u32[]{:S(2)}, u32[]{:S(2)}) collective-permute-start(bf16[256,1024]{1,0:T(8,128)(2,1)S(1)} %collective-permute-done.6.refs_2_), channel_id=1, source_target_pairs={{16,17},{17,16},{18,19},{19,18},{20,21},{21,20},{22,23},{23,22},{2... | collective-permute-start | bytes 1572872 | tf_op jit(solution)/shard_map/ppermute | solution.py:723
  72.7 23.6 %collective-permute-start.5 = (bf16[256,1024]{1,0:T(8,128)(2,1)}, bf16[256,1024]{1,0:T(8,128)(2,1)S(1)}, u32[]{:S(2)}, u32[]{:S(2)}) collective-permute-start(bf16[256,1024]{1,0:T(8,128)(2,1)} %fusion.9), channel_id=1, source_target_pairs={{0,18},{1,19},{2,16},{3,17},{4,22},{5,23},{6,20},{7,21},{8,26},{9,... | collective-permute-start | bytes 1572872 | tf_op jit(solution)/shard_map/ppermute | solution.py:747
  84.2 1.0 copy-start.22
  84.2 0.8 copy-start.18
  85.2 11.1 %copy-start.23 = (bf16[256,1024]{1,0:T(8,128)(2,1)S(1)}, bf16[256,1024]{1,0:T(8,128)(2,1)}, u32[]{:S(2)}) copy-start(bf16[256,1024]{1,0:T(8,128)(2,1)} %copy-done.22) | copy-start | bytes 1572868
  97.4 79.6 %all-gather.5.cloned.1.call-start = ((), (), s32[]{:S(2)}) async-start(), calls=%async_computation.3 | async-start | bytes 2621440 | tf_op jit(solution)/shard_map/all_gather | solution.py:753
  98.2 0.7 collective-permute-start.9
  100.6 42.5 %collective-permute-start.11 = (bf16[256,1024]{1,0:T(8,128)(2,1)S(1)}, bf16[256,1024]{1,0:T(8,128)(2,1)S(1)}, u32[]{:S(2)}, u32[]{:S(2)}) collective-permute-start(bf16[256,1024]{1,0:T(8,128)(2,1)S(1)} %get-tuple-element.292), channel_id=1, source_target_pairs={{16,2},{17,3},{18,0},{19,1},{20,6},{21,7},{22,4},{23,5},{24,10},{2... | collective-permute-start | bytes 1572872 | tf_op jit(solution)/shard_map/ppermute | solution.py:747
  101.9 50.5 %collective-permute-start.10 = (bf16[256,1024]{1,0:T(8,128)(2,1)S(1)}, bf16[256,1024]{1,0:T(8,128)(2,1)S(1)}, u32[]{:S(2)}, u32[]{:S(2)}) collective-permute-start(bf16[256,1024]{1,0:T(8,128)(2,1)S(1)} %get-tuple-element.293), channel_id=1, source_target_pairs={{16,0},{17,1},{18,2},{19,3},{20,4},{21,5},{22,6},{23,7},{24,8},{25... | collective-permute-start | bytes 1572872 | tf_op jit(solution)/shard_map/ppermute | solution.py:747
  153.5 131.3 %reduce-scatter.3.cloned.1.call-start = ((), (), s32[]{:S(2)}) async-start(), calls=%async_computation.4 | async-start | bytes 3276800 | tf_op jit(solution)/shard_map/reduce_scatter | solution.py:771
  154.6 0.7 collective-permute-start.12
  156.9 39.5 %collective-permute-start.14 = (bf16[256,1024]{1,0:T(8,128)(2,1)S(1)}, bf16[256,1024]{1,0:T(8,128)(2,1)S(1)}, u32[]{:S(2)}, u32[]{:S(2)}) collective-permute-start(bf16[256,1024]{1,0:T(8,128)(2,1)S(1)} %get-tuple-element.290), channel_id=1, source_target_pairs={{16,2},{17,3},{18,0},{19,1},{20,6},{21,7},{22,4},{23,5},{24,10},{2... | collective-permute-start | bytes 1572872 | tf_op jit(solution)/shard_map/ppermute | solution.py:747
  158.2 42.7 %collective-permute-start.13 = (bf16[256,1024]{1,0:T(8,128)(2,1)S(1)}, bf16[256,1024]{1,0:T(8,128)(2,1)S(1)}, u32[]{:S(2)}, u32[]{:S(2)}) collective-permute-start(bf16[256,1024]{1,0:T(8,128)(2,1)S(1)} %get-tuple-element.291), channel_id=1, source_target_pairs={{16,0},{17,1},{18,2},{19,3},{20,4},{21,5},{22,6},{23,7},{24,8},{25... | collective-permute-start | bytes 1572872 | tf_op jit(solution)/shard_map/ppermute | solution.py:747
  201.1 12.9 %copy-start.10 = (bf16[256,1024]{1,0:T(8,128)(2,1)}, bf16[256,1024]{1,0:T(8,128)(2,1)S(1)}, u32[]{:S(2)}) copy-start(bf16[256,1024]{1,0:T(8,128)(2,1)S(1)} %add_convert_fusion.4.refs_0_) | copy-start | bytes 1572868
  201.2 5.9 %collective-permute-start.16 = (bf16[256,1024]{1,0:T(8,128)(2,1)S(1)}, bf16[256,1024]{1,0:T(8,128)(2,1)S(1)}, u32[]{:S(2)}, u32[]{:S(2)}) collective-permute-start(bf16[256,1024]{1,0:T(8,128)(2,1)S(1)} %add_convert_fusion.4.refs_0_), channel_id=1, source_target_pairs={{0,1},{1,0},{2,3},{3,2},{4,5},{5,4},{6,7},{7,6},{8,9},{9,8},{10,11... | collective-permute-start | bytes 1572872 | tf_op jit(solution)/shard_map/ppermute | solution.py:723
  203.1 16.5 %collective-permute-start.15 = (bf16[256,1024]{1,0:T(8,128)(2,1)S(1)}, bf16[256,1024]{1,0:T(8,128)(2,1)S(1)}, u32[]{:S(2)}, u32[]{:S(2)}) collective-permute-start(bf16[256,1024]{1,0:T(8,128)(2,1)S(1)} %add_convert_fusion.4.refs_0_), channel_id=1, source_target_pairs={{0,2},{1,3},{2,0},{3,1},{4,6},{5,7},{6,4},{7,5},{8,10},{9,11},{10,... | collective-permute-start | bytes 1572872 | tf_op jit(solution)/shard_map/ppermute | solution.py:723
  207.0 7.1 %copy-start.19 = (bf16[256,1024]{1,0:T(8,128)(2,1)}, bf16[256,1024]{1,0:T(8,128)(2,1)S(1)}, u32[]{:S(2)}) copy-start(bf16[256,1024]{1,0:T(8,128)(2,1)S(1)} %collective-permute-done.16.refs_1_) | copy-start | bytes 1572868
  219.6 3.8 %copy-start.20 = (bf16[256,1024]{1,0:T(8,128)(2,1)}, bf16[256,1024]{1,0:T(8,128)(2,1)S(1)}, u32[]{:S(2)}) copy-start(bf16[256,1024]{1,0:T(8,128)(2,1)S(1)} %collective-permute-done.15.refs_2_) | copy-start | bytes 1572868
  219.6 3.8 %collective-permute-start.17 = (bf16[256,1024]{1,0:T(8,128)(2,1)S(1)}, bf16[256,1024]{1,0:T(8,128)(2,1)S(1)}, u32[]{:S(2)}, u32[]{:S(2)}) collective-permute-start(bf16[256,1024]{1,0:T(8,128)(2,1)S(1)} %collective-permute-done.15.refs_2_), channel_id=1, source_target_pairs={{0,1},{1,0},{2,3},{3,2},{4,5},{5,4},{6,7},{7,6},{8,9},{9,8},{10,11... | collective-permute-start | bytes 1572872 | tf_op jit(solution)/shard_map/ppermute | solution.py:723
  223.4 0.8 copy-start.21
  232.0 123.0 %reduce-scatter.5.cloned.1.call-start = ((), (), s32[]{:S(2)}) async-start(), calls=%async_computation.5 | async-start | bytes 4587520 | tf_op jit(solution)/shard_map/reduce_scatter | solution.py:771
  232.1 19.6 %copy-start.6 = (bf16[1024,1024]{1,0:T(8,128)(2,1)S(1)}, bf16[1024,1024]{1,0:T(8,128)(2,1)}, u32[]{:S(2)}) copy-start(bf16[1024,1024]{1,0:T(8,128)(2,1)} %get-tuple-element.254) | copy-start | bytes 6291460
  251.7 3.5 copy-start.1
  251.7 3.5 copy-start.7
  255.2 2.5 copy-start.8
  255.2 2.5 copy-start.11
  257.7 2.0 copy-start.2
  257.7 2.2 copy-start.9
  264.6 20.3 %copy-start.24 = (f32[8,1024]{1,0:T(8,128)S(1)}, f32[8,1024]{1,0:T(8,128)}, u32[]{:S(2)}) copy-start(f32[8,1024]{1,0:T(8,128)} %get-tuple-element.266) | copy-start | bytes 98308
  264.6 20.3 %copy-start.25 = (f32[8,1024]{1,0:T(8,128)S(1)}, f32[8,1024]{1,0:T(8,128)}, u32[]{:S(2)}) copy-start(f32[8,1024]{1,0:T(8,128)} %get-tuple-element.267) | copy-start | bytes 98308
  264.6 29.4 %copy-start.14 = (bf16[2,256,1024]{2,1,0:T(8,128)(2,1)S(1)}, bf16[2,256,1024]{2,1,0:T(8,128)(2,1)}, u32[]{:S(2)}) copy-start(bf16[2,256,1024]{2,1,0:T(8,128)(2,1)} %get-tuple-element.265) | copy-start | bytes 3145732
  264.6 36.1 %copy-start.4 = (bf16[2,256,1024]{2,1,0:T(8,128)(2,1)S(1)}, bf16[2,256,1024]{2,1,0:T(8,128)(2,1)}, u32[]{:S(2)}) copy-start(bf16[2,256,1024]{2,1,0:T(8,128)(2,1)} %get-tuple-element.258) | copy-start | bytes 3145732
  264.6 39.6 %copy-start.3 = (bf16[2,256,1024]{2,1,0:T(8,128)(2,1)S(1)}, bf16[2,256,1024]{2,1,0:T(8,128)(2,1)}, u32[]{:S(2)}) copy-start(bf16[2,256,1024]{2,1,0:T(8,128)(2,1)} %get-tuple-element.264) | copy-start | bytes 3145732
  284.7 15.9 %collective-permute-start.18 = (bf16[2,256,1024]{2,1,0:T(8,128)(2,1)}, bf16[2,256,1024]{2,1,0:T(8,128)(2,1)}, u32[]{:S(2)}, u32[]{:S(2)}) collective-permute-start(bf16[2,256,1024]{2,1,0:T(8,128)(2,1)} %get-tuple-element.259), channel_id=1, source_target_pairs={{0,1},{1,0},{2,3},{3,2},{16,17},{17,16},{18,19},{19,18},{4,5},{5,4... | collective-permute-start | bytes 3145736 | tf_op jit(solution)/shard_map/ppermute | solution.py:723
  284.9 4.0 %collective-permute-start.22 = (f32[8,1024]{1,0:T(8,128)S(1)}, f32[8,1024]{1,0:T(8,128)S(1)}, u32[]{:S(2)}, u32[]{:S(2)}) collective-permute-start(f32[8,1024]{1,0:T(8,128)S(1)} %add.201), channel_id=1, source_target_pairs={{0,4},{4,0},{8,12},{12,8},{1,5},{5,1},{9,13},{13,9},{2,6},{6,2},{1... | collective-permute-start | bytes 98312 | tf_op jit(solution)/shard_map/ppermute | solution.py:763
  288.8 5.2 %collective-permute-start.23 = (f32[8,1024]{1,0:T(8,128)S(1)}, f32[8,1024]{1,0:T(8,128)S(1)}, u32[]{:S(2)}, u32[]{:S(2)}) collective-permute-start(f32[8,1024]{1,0:T(8,128)S(1)} %add.202), channel_id=1, source_target_pairs={{0,8},{4,12},{8,0},{12,4},{1,9},{5,13},{9,1},{13,5},{2,10},{6,14},... | collective-permute-start | bytes 98312 | tf_op jit(solution)/shard_map/ppermute | solution.py:763
  294.0 10.1 %collective-permute-start.20 = (bf16[2,256,1024]{2,1,0:T(8,128)(2,1)S(1)}, bf16[2,256,1024]{2,1,0:T(8,128)(2,1)}, u32[]{:S(2)}, u32[]{:S(2)}) collective-permute-start(bf16[2,256,1024]{2,1,0:T(8,128)(2,1)S(1)} %copy-done.14), channel_id=1, source_target_pairs={{0,1},{1,0},{2,3},{3,2},{16,17},{17,16},{18,19},{19,18},{4,5},{5,4... | collective-permute-start | bytes 3145736 | tf_op jit(solution)/shard_map/ppermute | solution.py:723
  294.1 2.3 collective-permute-start.24
  294.7 12.1 %copy-start.15 = (bf16[256,1280]{1,0:T(8,128)(2,1)S(1)}, bf16[256,1280]{1,0:T(8,128)(2,1)}, u32[]{:S(2)}) copy-start(bf16[256,1280]{1,0:T(8,128)(2,1)} %reduce-scatter.3.cloned.1.call-done) | copy-start | bytes 1966084
  296.4 3.7 %collective-permute-start.25 = (f32[5,256]{1,0:T(8,128)S(1)}, f32[5,256]{1,0:T(8,128)S(1)}, u32[]{:S(2)}, u32[]{:S(2)}) collective-permute-start(f32[5,256]{1,0:T(8,128)S(1)} %fusion.28), channel_id=1, source_target_pairs={{0,2},{1,3},{2,0},{3,1},{4,6},{5,7},{6,4},{7,5},{8,10},{9,11},{10,... | collective-permute-start | bytes 15368 | tf_op jit(solution)/shard_map/ppermute | solution.py:763
  302.7 15.2 %collective-permute-start.19 = (bf16[256,1024]{1,0:T(8,128)(2,1)}, bf16[256,1024]{1,0:T(8,128)(2,1)}, u32[]{:S(2)}, u32[]{:S(2)}) collective-permute-start(bf16[256,1024]{1,0:T(8,128)(2,1)} %fusion.14), channel_id=1, source_target_pairs={{0,2},{1,3},{2,0},{3,1},{16,18},{17,19},{18,16},{19,17},{4,6},{5,7... | collective-permute-start | bytes 1572872 | tf_op jit(solution)/shard_map/ppermute | solution.py:723
  306.2 21.5 %collective-permute-start.21 = (bf16[256,1024]{1,0:T(8,128)(2,1)}, bf16[256,1024]{1,0:T(8,128)(2,1)}, u32[]{:S(2)}, u32[]{:S(2)}) collective-permute-start(bf16[256,1024]{1,0:T(8,128)(2,1)} %fusion.15), channel_id=1, source_target_pairs={{0,2},{1,3},{2,0},{3,1},{16,18},{17,19},{18,16},{19,17},{4,6},{5,7... | collective-permute-start | bytes 1572872 | tf_op jit(solution)/shard_map/ppermute | solution.py:723
Sparse Core Ops, SparseCore 0:
  97.5 30.1 all-gather.2
  153.6 23.3 all-gather.4
  232.1 52.5 reduce-scatter.2
  286.9 68.0 reduce-scatter.4
